TPU v7x, 32 devices: a whole 2x2x4 slice. The times are simulated.
32 devices in a mesh: dp: 8 (over y, x, core), mp: 4 (over z).
Axes of the slice: x: 2, y: 2, z: 4, core: 2. Of those that a mesh axis runs over, the one named last changes fastest.
Arguments:
- hidden: bfloat16 [16384, 1024], P('dp'), may hold values from -6 to 6
- lengths: int32 [8, 8], P('dp'), may hold values from 0 to 2048, as said below
- query_weight: bfloat16 [1024, 1024], P(None, 'mp'), may hold values from -0.1875 to 0.1875
- query_bias: float32 [1024], P('mp'), may hold values from -3 to 3
- key_weight: bfloat16 [1024, 1024], P(None, 'mp'), may hold values from -0.1875 to 0.1875
- key_bias: float32 [1024], P('mp'), may hold values from -3 to 3
- value_weight: bfloat16 [1024, 1024], P(None, 'mp'), may hold values from -0.1875 to 0.1875
- value_bias: float32 [1024], P('mp'), may hold values from -3 to 3
- out_weight: bfloat16 [1024, 1024], P('mp'), may hold values from -0.75 to 0.75
- out_bias: float32 [1024], replicated, may hold values from -3 to 3
- first_gain: float32 [1024], replicated, may hold values from 0.5 to 1.5
- first_shift: float32 [1024], replicated, may hold values from -3 to 3
- up_weight: bfloat16 [1024, 4096], P(None, 'mp'), may hold values from -0.1875 to 0.1875
- up_bias: float32 [4096], P('mp'), may hold values from -3 to 3
- down_weight: bfloat16 [4096, 1024], P('mp'), may hold values from -0.09375 to 0.09375
- down_bias: float32 [1024], replicated, may hold values from -3 to 3
- second_gain: float32 [1024], replicated, may hold values from 0.5 to 1.5
- second_shift: float32 [1024], replicated, may hold values from -3 to 3
- out_grad: bfloat16 [16384, 1024], P('dp'), may hold values from -6 to 6
Outputs:
- result: bfloat16 [16384, 1024], P('dp')
- hidden_grad: bfloat16 [16384, 1024], P('dp')
- query_weight_grad: float32 [1024, 1024], P(None, 'mp')
- query_bias_grad: float32 [1024], P('mp')
- key_weight_grad: float32 [1024, 1024], P(None, 'mp')
- key_bias_grad: float32 [1024], P('mp')
- value_weight_grad: float32 [1024, 1024], P(None, 'mp')
- value_bias_grad: float32 [1024], P('mp')
- out_weight_grad: float32 [1024, 1024], P('mp')
- out_bias_grad: float32 [1024], replicated
- first_gain_grad: float32 [1024], replicated
- first_shift_grad: float32 [1024], replicated
- up_weight_grad: float32 [1024, 4096], P(None, 'mp')
- up_bias_grad: float32 [4096], P('mp')
- down_weight_grad: float32 [4096, 1024], P('mp')
- down_bias_grad: float32 [1024], replicated
- second_gain_grad: float32 [1024], replicated
- second_shift_grad: float32 [1024], replicated
Inputs may be any that keep to these rules, and one draw needn't show every extreme that they name: Row r lists the lengths of the sequences packed in order from the start of the r-th block of 2048 slots; every length is 0 (an unused slot) or a multiple of 64; a row sums to at most 2048, and the slots after its sum are padding.
All inputs are finite; a program needn't handle non-finite values.
Results may differ from a plain program's by a relative error of at most 0.03.
Values may be sent and summed in bfloat16 or wider, within the bound.
No kernel may reach another device: no remote copies, remote signals or barrier semaphores. Data moves between devices by JAX's collectives and lax.ppermute only.
A program may use at most 192 MiB of HBM per device.

v0:
```python
import math

import jax
import jax.numpy as jnp
from jax import lax
from jax.sharding import PartitionSpec as P

HEAD = 64


epsilon = 1e-06


def layout(lengths_row, row_count):
    seq_ends = jnp.cumsum(lengths_row)
    token_index = jnp.arange(row_count, dtype=jnp.int32)
    segment = jnp.sum((token_index[:, None] >= seq_ends[None, :]).astype(jnp.int32), axis=1)
    is_valid = token_index < seq_ends[-1]
    starts = jnp.max(
        jnp.where(seq_ends[None, :] <= token_index[:, None], seq_ends[None, :], 0), axis=1
    )
    position = (token_index - starts).astype(jnp.float32)
    return (segment, is_valid, position)


def rotate(matrix, position, head_size, direction):
    row_count = matrix.shape[0]
    half_size = head_size // 2
    frequency = 10000.0 ** (-2.0 * jnp.arange(half_size, dtype=jnp.float32) / head_size)
    angles = position[:, None] * frequency[None, :]
    cosine = jnp.cos(angles)[:, None, :]
    sine_term = direction * jnp.sin(angles)[:, None, :]
    pair_view = matrix.reshape(row_count, -1, half_size, 2)
    former = pair_view[..., 0]
    latter = pair_view[..., 1]
    turned = jnp.stack(
        [former * cosine - latter * sine_term, latter * cosine + former * sine_term], axis=-1
    )
    return turned.reshape(row_count, -1)


def layer_norm(summed, gain_row, shift_row):
    row_mean = jnp.mean(summed, axis=-1, keepdims=True)
    centered = summed - row_mean
    variance = jnp.mean(centered * centered, axis=-1, keepdims=True)
    inv_std = lax.rsqrt(variance + epsilon)
    normed = centered * inv_std
    return (normed * gain_row + shift_row, normed, inv_std)


def norm_back(grad_normed, normed, inv_std):
    first_mean = jnp.mean(grad_normed, axis=-1, keepdims=True)
    second_mean = jnp.mean(grad_normed * normed, axis=-1, keepdims=True)
    return inv_std * (grad_normed - first_mean - normed * second_mean)


def gelu_slope(values):
    cumulative = 0.5 * (1.0 + jax.scipy.special.erf(values * 0.7071067811865476))
    return cumulative + values * jnp.exp(-0.5 * values * values) * 0.3989422804014327


def masked_scores(query_part, key_low, segment_part, valid_part, segment, is_valid, score_scale):
    raw_scores = (
        jnp.einsum("qhd,khd->hqk", query_part, key_low, preferred_element_type=jnp.float32)
        * score_scale
    )
    allowed = (segment_part[:, None] == segment[None, :]) & valid_part[:, None] & is_valid[None, :]
    return jnp.where(allowed[None], raw_scores, -1e30)


def column_sum(matrix):
    return jnp.sum(matrix.astype(jnp.float32), axis=0)


def local(
    hidden,
    lengths,
    query_weight,
    query_bias,
    key_weight,
    key_bias,
    value_weight,
    value_bias,
    out_weight,
    out_bias,
    first_gain,
    first_shift,
    up_weight,
    up_bias,
    down_weight,
    down_bias,
    second_gain,
    second_shift,
    out_grad,
):
    row_count = hidden.shape[0]
    local_width = query_weight.shape[1]
    head_count = local_width // HEAD
    score_scale = 1.0 / math.sqrt(HEAD)
    block_rows = min(512, row_count)
    starts = jnp.arange(row_count // block_rows, dtype=jnp.int32) * block_rows
    segment, is_valid, position = layout(lengths[0], row_count)
    inputs = hidden.astype(jnp.float32)
    queries = jnp.dot(hidden, query_weight, preferred_element_type=jnp.float32) + query_bias
    keyset = jnp.dot(hidden, key_weight, preferred_element_type=jnp.float32) + key_bias
    valueset = jnp.dot(hidden, value_weight, preferred_element_type=jnp.float32) + value_bias
    query_low = (
        rotate(queries, position, HEAD, 1.0)
        .astype(jnp.bfloat16)
        .reshape(row_count, head_count, HEAD)
    )
    key_low = (
        rotate(keyset, position, HEAD, 1.0)
        .astype(jnp.bfloat16)
        .reshape(row_count, head_count, HEAD)
    )
    value_low = valueset.astype(jnp.bfloat16).reshape(row_count, head_count, HEAD)

    def forward_block(start_row):
        query_part = lax.dynamic_slice_in_dim(query_low, start_row, block_rows, 0)
        segment_part = lax.dynamic_slice_in_dim(segment, start_row, block_rows, 0)
        valid_part = lax.dynamic_slice_in_dim(is_valid, start_row, block_rows, 0)
        masked = masked_scores(
            query_part, key_low, segment_part, valid_part, segment, is_valid, score_scale
        )
        row_top = jnp.where(valid_part[None, :], jnp.max(masked, axis=-1), 0.0)
        weights_exp = jnp.exp(masked - row_top[..., None])
        row_total = jnp.sum(weights_exp, axis=-1) + (1.0 - valid_part.astype(jnp.float32))[None, :]
        attention = weights_exp / row_total[..., None]
        context_part = jnp.einsum(
            "hqk,khd->qhd",
            attention.astype(jnp.bfloat16),
            value_low,
            preferred_element_type=jnp.float32,
        )
        return (context_part, row_top, row_total)

    context_blocks, tops, totals = lax.map(forward_block, starts)
    context = context_blocks.reshape(row_count, local_width).astype(jnp.bfloat16)
    attended = (
        lax.psum(
            jnp.dot(context, out_weight, preferred_element_type=jnp.float32).astype(jnp.bfloat16),
            "mp",
        ).astype(jnp.float32)
        + out_bias
    )
    first, first_normed, first_inv_std = layer_norm(inputs + attended, first_gain, first_shift)
    first_low = first.astype(jnp.bfloat16)
    upper = jnp.dot(first_low, up_weight, preferred_element_type=jnp.float32) + up_bias
    activated = jax.nn.gelu(upper, approximate=False).astype(jnp.bfloat16)
    lowered = (
        lax.psum(
            jnp.dot(activated, down_weight, preferred_element_type=jnp.float32).astype(
                jnp.bfloat16
            ),
            "mp",
        ).astype(jnp.float32)
        + down_bias
    )
    output, second_normed, second_inv_std = layer_norm(first + lowered, second_gain, second_shift)
    result = output.astype(jnp.bfloat16)
    cotangent = out_grad.astype(jnp.float32)
    second_shift_grad = jnp.sum(cotangent, axis=0)
    second_gain_grad = jnp.sum(cotangent * second_normed, axis=0)
    second_back = norm_back(cotangent * second_gain, second_normed, second_inv_std)
    lowered_grad = second_back.astype(jnp.bfloat16)
    down_bias_grad = column_sum(lowered_grad)
    down_weight_grad = jnp.einsum(
        "tf,td->fd", activated, lowered_grad, preferred_element_type=jnp.float32
    )
    upper_grad = (
        jnp.einsum("td,fd->tf", lowered_grad, down_weight, preferred_element_type=jnp.float32)
        * gelu_slope(upper)
    ).astype(jnp.bfloat16)
    up_bias_grad = column_sum(upper_grad)
    up_weight_grad = jnp.einsum(
        "td,tf->df", first_low, upper_grad, preferred_element_type=jnp.float32
    )
    first_grad = second_back + lax.psum(
        jnp.einsum("tf,df->td", upper_grad, up_weight, preferred_element_type=jnp.float32).astype(
            jnp.bfloat16
        ),
        "mp",
    ).astype(jnp.float32)
    first_shift_grad = jnp.sum(first_grad, axis=0)
    first_gain_grad = jnp.sum(first_grad * first_normed, axis=0)
    first_back = norm_back(first_grad * first_gain, first_normed, first_inv_std)
    attended_grad = first_back.astype(jnp.bfloat16)
    out_bias_grad = column_sum(attended_grad)
    out_weight_grad = jnp.einsum(
        "tc,td->cd", context, attended_grad, preferred_element_type=jnp.float32
    )
    context_grad = jnp.einsum(
        "td,cd->tc", attended_grad, out_weight, preferred_element_type=jnp.float32
    )
    context_grad = context_grad.astype(jnp.bfloat16).reshape(row_count, head_count, HEAD)

    def backward_block(carried, pieces):
        key_total, value_total = carried
        start_row, row_top, row_total = pieces
        query_part = lax.dynamic_slice_in_dim(query_low, start_row, block_rows, 0)
        segment_part = lax.dynamic_slice_in_dim(segment, start_row, block_rows, 0)
        valid_part = lax.dynamic_slice_in_dim(is_valid, start_row, block_rows, 0)
        grad_part = lax.dynamic_slice_in_dim(context_grad, start_row, block_rows, 0)
        masked = masked_scores(
            query_part, key_low, segment_part, valid_part, segment, is_valid, score_scale
        )
        attention = jnp.exp(masked - row_top[..., None]) / row_total[..., None]
        prob_grad = jnp.einsum(
            "qhd,khd->hqk", grad_part, value_low, preferred_element_type=jnp.float32
        )
        row_delta = jnp.sum(attention * prob_grad, axis=-1, keepdims=True)
        score_grad = (attention * (prob_grad - row_delta)).astype(jnp.bfloat16)
        query_part_grad = (
            jnp.einsum("hqk,khd->qhd", score_grad, key_low, preferred_element_type=jnp.float32)
            * score_scale
        )
        key_total = (
            key_total
            + jnp.einsum("hqk,qhd->khd", score_grad, query_part, preferred_element_type=jnp.float32)
            * score_scale
        )
        value_total = value_total + jnp.einsum(
            "hqk,qhd->khd",
            attention.astype(jnp.bfloat16),
            grad_part,
            preferred_element_type=jnp.float32,
        )
        return ((key_total, value_total), query_part_grad)

    empty = jnp.zeros((row_count, head_count, HEAD), jnp.float32)
    (key_rot_grad, value_grad), query_blocks = lax.scan(
        backward_block, (empty, empty), (starts, tops, totals)
    )
    query_low_grad = rotate(
        query_blocks.reshape(row_count, local_width), position, HEAD, -1.0
    ).astype(jnp.bfloat16)
    key_low_grad = rotate(
        key_rot_grad.reshape(row_count, local_width), position, HEAD, -1.0
    ).astype(jnp.bfloat16)
    value_low_grad = value_grad.reshape(row_count, local_width).astype(jnp.bfloat16)
    query_bias_grad = column_sum(query_low_grad)
    key_bias_grad = column_sum(key_low_grad)
    value_bias_grad = column_sum(value_low_grad)
    query_weight_grad = jnp.einsum(
        "td,tc->dc", hidden, query_low_grad, preferred_element_type=jnp.float32
    )
    key_weight_grad = jnp.einsum(
        "td,tc->dc", hidden, key_low_grad, preferred_element_type=jnp.float32
    )
    value_weight_grad = jnp.einsum(
        "td,tc->dc", hidden, value_low_grad, preferred_element_type=jnp.float32
    )
    partial_input = jnp.einsum(
        "tc,dc->td", query_low_grad, query_weight, preferred_element_type=jnp.float32
    )
    partial_input = partial_input + jnp.einsum(
        "tc,dc->td", key_low_grad, key_weight, preferred_element_type=jnp.float32
    )
    partial_input = partial_input + jnp.einsum(
        "tc,dc->td", value_low_grad, value_weight, preferred_element_type=jnp.float32
    )
    hidden_grad = (
        first_back + lax.psum(partial_input.astype(jnp.bfloat16), "mp").astype(jnp.float32)
    ).astype(jnp.bfloat16)
    summed = tuple(
        (
            lax.psum(query_weight_grad.astype(jnp.bfloat16), "dp").astype(jnp.float32),
            lax.psum(query_bias_grad.astype(jnp.bfloat16), "dp").astype(jnp.float32),
            lax.psum(key_weight_grad.astype(jnp.bfloat16), "dp").astype(jnp.float32),
            lax.psum(key_bias_grad.astype(jnp.bfloat16), "dp").astype(jnp.float32),
            lax.psum(value_weight_grad.astype(jnp.bfloat16), "dp").astype(jnp.float32),
            lax.psum(value_bias_grad.astype(jnp.bfloat16), "dp").astype(jnp.float32),
            lax.psum(out_weight_grad.astype(jnp.bfloat16), "dp").astype(jnp.float32),
            lax.psum(out_bias_grad.astype(jnp.bfloat16), "dp").astype(jnp.float32),
            lax.psum(first_gain_grad.astype(jnp.bfloat16), "dp").astype(jnp.float32),
            lax.psum(first_shift_grad.astype(jnp.bfloat16), "dp").astype(jnp.float32),
            lax.psum(up_weight_grad.astype(jnp.bfloat16), "dp").astype(jnp.float32),
            lax.psum(up_bias_grad.astype(jnp.bfloat16), "dp").astype(jnp.float32),
            lax.psum(down_weight_grad.astype(jnp.bfloat16), "dp").astype(jnp.float32),
            lax.psum(down_bias_grad.astype(jnp.bfloat16), "dp").astype(jnp.float32),
            lax.psum(second_gain_grad.astype(jnp.bfloat16), "dp").astype(jnp.float32),
            lax.psum(second_shift_grad.astype(jnp.bfloat16), "dp").astype(jnp.float32),
        )
    )
    return (result, hidden_grad) + summed


def solution(mesh):
    in_specs = (
        P("dp", None),
        P("dp", None),
        P(None, "mp"),
        P("mp"),
        P(None, "mp"),
        P("mp"),
        P(None, "mp"),
        P("mp"),
        P("mp", None),
        P(),
        P(),
        P(),
        P(None, "mp"),
        P("mp"),
        P("mp", None),
        P(),
        P(),
        P(),
        P("dp", None),
    )
    out_specs = (
        P("dp", None),
        P("dp", None),
        P(None, "mp"),
        P("mp"),
        P(None, "mp"),
        P("mp"),
        P(None, "mp"),
        P("mp"),
        P("mp", None),
        P(),
        P(),
        P(),
        P(None, "mp"),
        P("mp"),
        P("mp", None),
        P(),
        P(),
        P(),
    )
    return jax.shard_map(local, mesh=mesh, in_specs=in_specs, out_specs=out_specs, check_vma=False)
```

profile of v0, /device:TPU:0, one launch (start us, length us, event | category | flops | bytes accessed | tf_op | source)
XLA Modules:
  0.0 1290.4 jit_solution(1822977652131072372)
XLA Ops:
  9.7 5.0 convolution_add_fusion.2
  18.1 4.8 convolution_add_fusion.1
  28.1 8.3 subtract_convert_fusion
  52.1 74.0 %while.29 = (s32[]{:T(128)}, bf16[4,512,4,64]{1,3,2,0:T(8,128)(2,1)}, f32[4,4,512]{2,1,0:T(4,128)}, f32[4,4,512]{2,1,0:T(4,128)}, s32[4]{0:T(128)S(1)}, /*index=...) while((s32[]{:T(128)}, ...), condition=%wide.region_6.7_spmd, body=%wide.region_3.6_spmd.sunk | while | flops 1127224320 | bytes 70124320 | solution.py:138
  65.0 4.8 fusion.137
  83.5 4.8 fusion.137
  101.9 4.8 fusion.137
  134.3 157.7 %all-reduce.8.cloned.1.call-done = bf16[2048,1024]{1,0:T(8,128)(2,1)} async-done(((bf16[2048,1024]{1,0:T(8,128)(2,1)}), bf16[2048,1024]{1,0:T(8,128)(2,1)}) %all-reduce.8.cloned.1.call-update) | async-done | bytes 4194320 | tf_op jit(solution)/shard_map/psum | solution.py:141
  292.0 5.0 fusion.56
  300.5 25.4 %fusion.41 = (bf16[2048,1024]{1,0:T(8,128)(2,1)S(1)}, f32[2048,1024]{1,0:T(8,128)}) fusion(f32[1024]{0:T(1024)S(1)} %copy-done.50, bf16[1024,1024]{1,0:T(8,128)(2,1)S(1)} %copy-done, f32[1024]{0:T(1024)S(1)} %copy-done.45, f32[1024]{0:T(1024)S(1)} %copy-done.36, f32[2048]{0:T(1024)S(1)} %add_rsqrt_fusion.1, f32[2048]{0:T(1024)S(1)} %broadcast_multiply_fusion.6, ...), kind=kOutput, calls=%fused_computation.58 | convolution fusion | flops 4452253696 | bytes 23101440 | tf_op jit(solution)/shard_map/dot_general | solution.py:149
  328.0 6.0 convolution_convert_fusion.2
  334.1 154.1 %all-reduce.10.cloned.1.call-done = bf16[2048,1024]{1,0:T(8,128)(2,1)} async-done(((bf16[2048,1024]{1,0:T(8,128)(2,1)}), bf16[2048,1024]{1,0:T(8,128)(2,1)}) %all-reduce.10.cloned.1.call-update) | async-done | bytes 4194320 | tf_op jit(solution)/shard_map/psum | solution.py:152
  488.2 6.8 fusion.73
  497.2 6.4 fusion.38
  507.8 11.6 fusion.74
  521.4 6.2 convolution_convert_fusion.1
  528.2 11.4 convolution_convert_fusion.4
  539.6 7.5 convolution_convert_fusion.5
  547.1 134.7 %all-reduce.12.cloned.1.call-done = bf16[2048,1024]{1,0:T(8,128)(2,1)} async-done(((bf16[2048,1024]{1,0:T(8,128)(2,1)}), bf16[2048,1024]{1,0:T(8,128)(2,1)}) %all-reduce.12.cloned.1.call-update) | async-done | bytes 4194320 | tf_op jit(solution)/shard_map/psum | solution.py:179
  681.8 12.0 multiply_reduce_fusion.1
  693.8 7.2 convert_reduce_fusion.1
  706.1 267.2 %while.30 = (s32[]{:T(128)}, f32[2048,4,64]{0,2,1:T(8,128)}, f32[2048,4,64]{0,2,1:T(8,128)}, f32[4,512,4,64]{1,0,3,2:T(4,128)}, s32[4]{0:T(128)S(1)}, /*index=5*...) while((s32[]{:T(128)}, f32[2048,4,64]{0,2,1:T(8,128)}, ...), condition=%wide.region_20.21_spmd.clone, body=%wide.region_18.20_spmd.clone.sunk | while | flops 2732193792 | bytes 164185936 | solution.py:232
  710.7 9.3 fusion.148
  719.9 15.0 %multiply_reduce_fusion.7 = (f32[4,512]{1,0:T(4,128)S(1)}, f32[4,512,2048]{2,1,0:T(8,128)}) fusion(f32[4,512,2048]{2,1,0:T(8,128)} %fusion.148, f32[4,512]{1,0:T(4,128)S(1)} %get-tuple-element.515, f32[4,512]{1,0:T(4,128)S(1)} %get-tuple-element.516, bf16[2048,4,64]{0,2,1:T(8,128)(2,1)S(1)} %get-tuple-element.598, ...), kind=kOutput, calls=%fused_computation.22.clone.1 | convolution fusion | flops 562034688 | bytes 35938308 | tf_op jit(solution)/shard_map/while/body/eval_jaxpr/qhd,khd->hqk/dot_general | solution.py:64
  734.9 11.3 multiply_convert_fusion.2
  746.3 8.8 fusion.150
  761.6 11.1 dynamic_update_slice.23
  777.0 9.3 fusion.148
  786.2 15.0 %multiply_reduce_fusion.7 = (f32[4,512]{1,0:T(4,128)S(1)}, f32[4,512,2048]{2,1,0:T(8,128)}) fusion(f32[4,512,2048]{2,1,0:T(8,128)} %fusion.148, f32[4,512]{1,0:T(4,128)S(1)} %get-tuple-element.515, f32[4,512]{1,0:T(4,128)S(1)} %get-tuple-element.516, bf16[2048,4,64]{0,2,1:T(8,128)(2,1)S(1)} %get-tuple-element.598, ...), kind=kOutput, calls=%fused_computation.22.clone.1 | convolution fusion | flops 562034688 | bytes 35938308 | tf_op jit(solution)/shard_map/while/body/eval_jaxpr/qhd,khd->hqk/dot_general | solution.py:64
  801.2 11.3 multiply_convert_fusion.2
  812.6 9.4 fusion.150
  828.5 11.1 dynamic_update_slice.23
  843.9 9.3 fusion.148
  853.2 15.0 %multiply_reduce_fusion.7 = (f32[4,512]{1,0:T(4,128)S(1)}, f32[4,512,2048]{2,1,0:T(8,128)}) fusion(f32[4,512,2048]{2,1,0:T(8,128)} %fusion.148, f32[4,512]{1,0:T(4,128)S(1)} %get-tuple-element.515, f32[4,512]{1,0:T(4,128)S(1)} %get-tuple-element.516, bf16[2048,4,64]{0,2,1:T(8,128)(2,1)S(1)} %get-tuple-element.598, ...), kind=kOutput, calls=%fused_computation.22.clone.1 | convolution fusion | flops 562034688 | bytes 35938308 | tf_op jit(solution)/shard_map/while/body/eval_jaxpr/qhd,khd->hqk/dot_general | solution.py:64
  868.2 11.3 multiply_convert_fusion.2
  879.5 9.4 fusion.150
  895.4 11.1 dynamic_update_slice.23
  910.8 9.2 fusion.148
  920.0 15.0 %multiply_reduce_fusion.7 = (f32[4,512]{1,0:T(4,128)S(1)}, f32[4,512,2048]{2,1,0:T(8,128)}) fusion(f32[4,512,2048]{2,1,0:T(8,128)} %fusion.148, f32[4,512]{1,0:T(4,128)S(1)} %get-tuple-element.515, f32[4,512]{1,0:T(4,128)S(1)} %get-tuple-element.516, bf16[2048,4,64]{0,2,1:T(8,128)(2,1)S(1)} %get-tuple-element.598, ...), kind=kOutput, calls=%fused_computation.22.clone.1 | convolution fusion | flops 562034688 | bytes 35938308 | tf_op jit(solution)/shard_map/while/body/eval_jaxpr/qhd,khd->hqk/dot_general | solution.py:64
  935.0 11.3 multiply_convert_fusion.2
  946.4 9.4 fusion.150
  962.2 11.1 dynamic_update_slice.23
  986.3 7.3 multiply_subtract_fusion
  993.5 7.4 fusion.71
  1020.5 25.7 %all-reduce = (bf16[256]{0:T(256)(128)(2,1)S(1)}, bf16[256]{0:T(256)(128)(2,1)S(1)}, bf16[256]{0:T(256)(128)(2,1)S(1)}, bf16[1024]{0:T(1024)(128)(2,1)S(1)}, bf1...) all-reduce(bf16[256]{0:T(256)(128)(2,1)S(1)} %reduce_sum.228, ...), channel_id=1, replica_groups=mesh['dp'=8,'mp'=4] {'dp'}, use_global_device_ids=true, to_apply=%region_24.25 | all-reduce | flops 7936 | bytes 31744 | tf_op jit(solution)/shard_map/psum | solution.py:269
  1052.1 65.2 %all-reduce.16.cloned.1.call-done = (bf16[1024,256]{0,1:T(8,128)(2,1)}, bf16[1024,256]{0,1:T(8,128)(2,1)}, bf16[1024,256]{0,1:T(8,128)(2,1)}, bf16[256,1024]{1,0...) async-done(((bf16[1024,256]{0,1:T(8,128)(2,1)}, bf16[1024,256]{0,1:T(8,128)(2,1)}, bf16[1024,256]{0,1:T(8,128)(2,1)}, bf16[256,1024]{1,0:T(8,128)(2,1)}, ...) | async-done | bytes 6291472 | tf_op jit(solution)/shard_map/psum | solution.py:268
  1132.8 142.4 %all-reduce.14.cloned.1.call-done = bf16[2048,1024]{1,0:T(8,128)(2,1)} async-done(((bf16[2048,1024]{1,0:T(8,128)(2,1)}), bf16[2048,1024]{1,0:T(8,128)(2,1)}) %all-reduce.14.cloned.1.call-update) | async-done | bytes 4194320 | tf_op jit(solution)/shard_map/psum | solution.py:264
  1275.2 8.2 add_convert_fusion
  (298 shorter events, 194.6 us)
Async XLA Ops:
  7.2 293.3 %copy-start = (bf16[1024,1024]{1,0:T(8,128)(2,1)S(1)}, bf16[1024,1024]{1,0:T(8,128)(2,1)}, u32[]{:S(2)}) copy-start(bf16[1024,1024]{1,0:T(8,128)(2,1)} %param.35) | copy-start | bytes 6291460
  7.2 284.8 %all-reduce.8.cloned.1.call-start = ((), (), s32[]{:S(2)}) async-start(), calls=%async_computation | async-start | bytes 8388608 | tf_op jit(solution)/shard_map/psum | solution.py:141
  9.6 8.5 copy-start.30
  9.7 8.5 copy-start.51
  28.1 8.3 copy-start.22
  28.1 19.4 %copy-start.52 = (f32[256]{0:T(256)S(1)}, f32[256]{0:T(256)}, u32[]{:S(2)}) copy-start(f32[256]{0:T(256)} %param.30) | copy-start | bytes 3076
  60.6 4.4 copy-start.15
  60.6 4.4 copy-start.28
  79.1 4.4 copy-start.15
  79.1 4.4 copy-start.28
  97.5 4.4 copy-start.15
  97.5 4.4 copy-start.28
  116.0 4.4 copy-start.15
  116.0 4.4 copy-start.28
  126.1 8.1 copy-start.53
  126.1 8.1 copy-start.2
  126.1 8.1 copy-start.26
  126.1 8.1 copy-start.33
  126.1 165.9 %copy-start.35 = (f32[1024]{0:T(1024)S(1)}, f32[1024]{0:T(1024)}, u32[]{:S(2)}) copy-start(f32[1024]{0:T(1024)} %param.32) | copy-start | bytes 12292
  134.2 166.2 %copy-start.36 = (f32[1024]{0:T(1024)S(1)}, f32[1024]{0:T(1024)}, u32[]{:S(2)}) copy-start(f32[1024]{0:T(1024)} %param.33) | copy-start | bytes 12292
  134.3 166.2 %copy-start.45 = (f32[1024]{0:T(1024)S(1)}, f32[1024]{0:T(1024)}, u32[]{:S(2)}) copy-start(f32[1024]{0:T(1024)} %param.34) | copy-start | bytes 12292
  134.3 166.2 %copy-start.50 = (f32[1024]{0:T(1024)S(1)}, f32[1024]{0:T(1024)}, u32[]{:S(2)}) copy-start(f32[1024]{0:T(1024)} %param.36) | copy-start | bytes 12292
  134.3 353.9 %all-reduce.10.cloned.1.call-start = ((), (), s32[]{:S(2)}) async-start(), calls=%async_computation.1 | async-start | bytes 8388608 | tf_op jit(solution)/shard_map/psum | solution.py:152
  292.0 5.1 copy-start.5
  292.0 5.9 copy-start.8
  300.5 27.5 %copy-start.48 = (bf16[1024,1024]{1,0:T(8,128)(2,1)S(1)}, bf16[1024,1024]{1,0:T(8,128)(2,1)}, u32[]{:S(2)}) copy-start(bf16[1024,1024]{1,0:T(8,128)(2,1)} %param.37) | copy-start | bytes 6291460
  328.0 160.2 %copy-start.44 = (f32[1024]{0:T(1024)S(1)}, f32[1024]{0:T(1024)}, u32[]{:S(2)}) copy-start(f32[1024]{0:T(1024)} %param.38) | copy-start | bytes 12292
  334.0 347.8 %all-reduce.12.cloned.1.call-start = ((), (), s32[]{:S(2)}) async-start(), calls=%async_computation.2 | async-start | bytes 8388608 | tf_op jit(solution)/shard_map/psum | solution.py:179
  503.5 4.3 copy-start.49
  507.8 11.6 copy-start.14
  527.7 589.6 %all-reduce.16.cloned.1.call-start = ((), (), s32[]{:S(2)}) async-start(), calls=%async_computation.4 | async-start | bytes 12582912 | tf_op jit(solution)/shard_map/psum | solution.py:268
  528.1 11.4 copy-start.6
  528.1 11.4 copy-start.9
  528.2 11.4 copy-start.57
  681.8 12.0 copy-start.7
  681.8 12.0 copy-start.10
  681.8 12.0 copy-start.18
  693.8 7.3 copy-start.20
  701.1 5.0 copy-start.4
  710.7 9.3 copy-start.21
  777.0 9.3 copy-start.21
  843.9 9.3 copy-start.21
  910.8 9.3 copy-start.21
  973.3 10.8 copy-start.13
  978.0 8.3 copy-start.23
  1012.4 262.8 %all-reduce.14.cloned.1.call-start = ((), (), s32[]{:S(2)}) async-start(), calls=%async_computation.3 | async-start | bytes 8388608 | tf_op jit(solution)/shard_map/psum | solution.py:264
  1123.9 6.4 copy-start.24
  1130.3 153.1 %copy-start.1 = (bf16[1024,1024]{1,0:T(8,128)(2,1)S(1)}, bf16[1024,1024]{1,0:T(8,128)(2,1)}, u32[]{:S(2)}) copy-start(bf16[1024,1024]{1,0:T(8,128)(2,1)} %param.35) | copy-start | bytes 6291460
  (33 other events, 77.3 us)
Sparse Core Ops, SparseCore 0:
  134.3 157.6 all-reduce.7
  334.1 153.9 all-reduce.9
  527.8 153.9 all-reduce.11
  1012.5 104.7 all-reduce.15
  1120.1 155.1 all-reduce.13
where the time goes:
time: 1300 us; the launch traced here: 1290 us
  waiting for transfers between devices  654 us (50%)
  matrix products  302 us (23%)
  other arithmetic  177 us (14%)
  local copies, waits for them, and re-layouts  99.3 us (8%)
  blocking collectives  25.7 us (2%)
  loops' own time  16.5 us (1%)
  between operations  14.9 us (1%)
    psum x1, waiting for transfers between devices, local(): lax.psum(jnp.dot(context, out_weight, preferred_element_type=jnp.float32)...  158 us
    psum x1, waiting for transfers between devices, local(): lax.psum(jnp.dot(activated, down_weight, preferred_element_type=jnp.float...  154 us
    psum x1, waiting for transfers between devices, local(): lax.psum(partial_input.astype(jnp.bfloat16), 'mp').astype(jnp.float32)  142 us
    psum x1, waiting for transfers between devices, local(): lax.psum(jnp.einsum('tf,df->td', upper_grad, up_weight, preferred_element...  135 us
    dot_general x8, matrix products, masked_scores(): jnp.einsum('qhd,khd->hqk', query_part, key_low, preferred_element_type=jn...  78.5 us
    psum x1, waiting for transfers between devices, local(): lax.psum(query_weight_grad.astype(jnp.bfloat16), 'dp').astype(jnp.float32)  65.2 us
    dynamic_update_slice x8, local copies, waits for them, and re-layouts, local(): context_blocks, tops, totals = lax.map(forward_block, starts)  46.4 us
    convert_element_type x4, other arithmetic, backward_block(): score_grad = (attention * (prob_grad - row_delta)).astype(jnp.bfloat16)  45.3 us
  transfers between devices with their start and end apart: 5, of which 5 were waited for; matrix products, arithmetic and copies ran while one was open for 4% of the time, Pallas kernels for 0%

commit v1 on v0

v1 whole, which is shorter than its diff:
```python
import functools
import math

import jax
import jax.numpy as jnp
from jax import lax
from jax.experimental import pallas as pl
from jax.experimental.pallas import tpu as pltpu
from jax.sharding import PartitionSpec as P

HEAD = 64
HALF = HEAD // 2
LANES = 128
FEAT = 16
FAR = -1e30
FLOOR = -1e29
LOG2E = 1.4426950408889634
LN2 = 0.6931471805599453
VMEM_LIMIT = 60 * 1024 * 1024
epsilon = 1e-06
f32 = jnp.float32
bf16 = jnp.bfloat16


def params(*semantics):
    return pltpu.CompilerParams(
        dimension_semantics=semantics, vmem_limit_bytes=VMEM_LIMIT
    )


def nn(a, b):
    return lax.dot_general(a, b, (((1,), (0,)), ((), ())), preferred_element_type=f32)


def nt(a, b):
    return lax.dot_general(a, b, (((1,), (1,)), ((), ())), preferred_element_type=f32)


def tn(a, b):
    return lax.dot_general(a, b, (((0,), (0,)), ((), ())), preferred_element_type=f32)


def interleave_matrix(transposed):
    row = lax.broadcasted_iota(jnp.int32, (HEAD, HEAD), 0)
    col = lax.broadcasted_iota(jnp.int32, (HEAD, HEAD), 1)
    if transposed:
        row, col = col, row
    source = jnp.where(row < HALF, 2 * row, 2 * (row - HALF) + 1)
    return jnp.where(col == source, 1.0, 0.0).astype(bf16)


def project_kernel(
    heads, lengths_ref, hidden_ref, qw_ref, kw_ref, vw_ref, qb_ref, kb_ref, vb_ref,
    qt_ref, kt_ref, kn_ref, vt_ref, vn_ref, cos_ref, sin_ref, turned_ref, wt_ref, bias_ref,
):
    width = heads * HEAD
    rows = hidden_ref.shape[0]

    @pl.when(pl.program_id(0) == 0)
    def _():
        split = interleave_matrix(False)
        for index, weight in enumerate((qw_ref, kw_ref)):
            for h in range(heads):
                turned = weight[:, h * HEAD:(h + 1) * HEAD]
                wt_ref[index * width + h * HEAD:index * width + (h + 1) * HEAD, :] = nt(
                    split, turned
                ).astype(bf16)
        for index, weight in enumerate((qw_ref, kw_ref, vw_ref)):
            turned = weight[...].astype(f32).T.astype(bf16)
            for h in range(heads):
                at = (3 * h + index) * HEAD
                turned_ref[at:at + HEAD] = turned[h * HEAD:(h + 1) * HEAD]
        wt_ref[2 * width:, :] = turned
        same = jnp.where(
            lax.broadcasted_iota(jnp.int32, (HEAD, HEAD), 0)
            == lax.broadcasted_iota(jnp.int32, (HEAD, HEAD), 1),
            1.0,
            0.0,
        )
        chosen = (split.astype(f32), split.astype(f32), same)
        for index, source in enumerate((qb_ref, kb_ref, vb_ref)):
            for h in range(heads):
                part = source[:, h * HEAD:(h + 1) * HEAD]
                bias_ref[index * width + h * HEAD:index * width + (h + 1) * HEAD, :] = jnp.sum(
                    chosen[index] * part, axis=1, keepdims=True
                )

    token = lax.broadcasted_iota(jnp.int32, (8, rows), 1) + pl.program_id(0) * rows
    end = jnp.int32(0)
    segment = jnp.zeros((8, rows), jnp.int32)
    start = jnp.zeros((8, rows), jnp.int32)
    for j in range(lengths_ref.shape[1]):
        end = end + lengths_ref[0, j]
        past = token >= end
        segment = segment + past.astype(jnp.int32)
        start = jnp.where(past, jnp.maximum(start, end), start)
    valid = (token < end)[:1]
    segment = segment[:1]
    same = lax.broadcasted_iota(jnp.int32, (FEAT, rows), 0) == segment
    query_side = jnp.where(same, 1.0, 0.0).astype(bf16)
    key_side = jnp.where(same & valid, 0.0, FAR)
    position = (token - start)[:1].astype(f32)
    pair = lax.broadcasted_iota(jnp.int32, (HALF, rows), 0).astype(f32)
    angle = jnp.exp(pair * (-2.0 * math.log(10000.0) / HEAD)) * position
    cosine, sine = jnp.cos(angle), jnp.sin(angle)
    cos_ref[...] = cosine
    sin_ref[...] = sine
    lane_row = lax.broadcasted_iota(jnp.int32, (LANES - HEAD - FEAT, rows), 0)
    tail = jnp.where(lane_row < 3, 1.0, 0.0)
    ones_row = lax.broadcasted_iota(jnp.int32, (LANES - HEAD, rows), 0)
    projected = nt(wt_ref[...], hidden_ref[...]) + bias_ref[...]
    for h in range(heads):
        for index in range(2):
            base = index * width + h * HEAD
            former = projected[base:base + HALF]
            latter = projected[base + HALF:base + HEAD]
            turned_a = former * cosine - latter * sine
            turned_b = latter * cosine + former * sine
            if index == 0:
                scale = LOG2E / math.sqrt(HEAD)
                qt_ref[h] = jnp.concatenate(
                    [
                        (turned_a * scale).astype(bf16),
                        (turned_b * scale).astype(bf16),
                        query_side,
                        jnp.zeros((LANES - HEAD - FEAT, rows), bf16),
                    ],
                    axis=0,
                )
            else:
                kt_ref[h] = jnp.concatenate([turned_a, turned_b], axis=0).astype(bf16)
                kn_ref[h] = (
                    jnp.concatenate([turned_a, turned_b, key_side, tail], axis=0)
                    .T.astype(bf16)
                )
        base = 2 * width + h * HEAD
        flat = projected[base:base + HEAD]
        ones = jnp.where((ones_row >= 3 * h) & (ones_row < 3 * h + 3), 1.0, 0.0)
        vt_ref[h] = jnp.concatenate([flat, jnp.ones((FEAT, rows), f32)], axis=0).astype(bf16)
        vn_ref[h] = jnp.concatenate([flat, ones], axis=0).T.astype(bf16)


def project(lengths, hidden, qw, kw, vw, qb, kb, vb):
    rows, depth = hidden.shape
    width = qw.shape[1]
    heads = width // HEAD
    block = min(512, rows)
    whole = lambda *shape: pl.BlockSpec(shape, lambda i: (0,) * len(shape))
    table = pl.BlockSpec((HALF, block), lambda i: (0, i))
    return pl.pallas_call(
        functools.partial(project_kernel, heads),
        grid=(rows // block,),
        in_specs=[pl.BlockSpec(memory_space=pltpu.SMEM)]
        + [pl.BlockSpec((block, depth), lambda i: (i, 0))]
        + [whole(depth, width)] * 3
        + [whole(1, width)] * 3,
        out_specs=[
            pl.BlockSpec((heads, LANES, block), lambda i: (0, 0, i)),
            pl.BlockSpec((heads, HEAD, block), lambda i: (0, 0, i)),
            pl.BlockSpec((heads, block, LANES), lambda i: (0, i, 0)),
            pl.BlockSpec((heads, HEAD + FEAT, block), lambda i: (0, 0, i)),
            pl.BlockSpec((heads, block, LANES), lambda i: (0, i, 0)),
            table,
            table,
            whole(3 * width, depth),
        ],
        out_shape=[
            jax.ShapeDtypeStruct((heads, LANES, rows), bf16),
            jax.ShapeDtypeStruct((heads, HEAD, rows), bf16),
            jax.ShapeDtypeStruct((heads, rows, LANES), bf16),
            jax.ShapeDtypeStruct((heads, HEAD + FEAT, rows), bf16),
            jax.ShapeDtypeStruct((heads, rows, LANES), bf16),
            jax.ShapeDtypeStruct((HALF, rows), f32),
            jax.ShapeDtypeStruct((HALF, rows), f32),
            jax.ShapeDtypeStruct((3 * width, depth), bf16),
        ],
        scratch_shapes=[
            pltpu.VMEM((3 * width, depth), bf16), pltpu.VMEM((3 * width, 1), f32)
        ],
        compiler_params=params("arbitrary"),
        cost_estimate=pl.CostEstimate(
            flops=6 * rows * depth * width, bytes_accessed=16 * rows * depth, transcendentals=0
        ),
        name="project",
    )(lengths, hidden, qw, kw, vw, qb[None], kb[None], vb[None])


def pack_kernel(chips, me_ref, up_ref, down_ref, out_ref, bias_ref, pack_ref, sems):
    depth, local = up_ref.shape
    half, width = local // 2, out_ref.shape[0]
    core, chip = me_ref[1] & 1, me_ref[1] >> 1
    ups, downs, outs = depth // chips, half // chips, width // (2 * chips)
    row = pl.multiple_of(chip * ups, ups)
    pieces = [(up_ref, row, ups, pl.multiple_of(core * half, half))]
    row = pl.multiple_of(core * half + chip * downs, downs)
    pieces += [(down_ref, row, downs, c * half) for c in range(2)]
    row = pl.multiple_of(core * (width // 2) + chip * outs, outs)
    pieces += [(out_ref, row, outs, c * half) for c in range(2)]
    at, copies = 0, []
    for i, (source, row, extent, column) in enumerate(pieces):
        copies.append(
            pltpu.make_async_copy(
                source.at[pl.ds(row, extent), pl.ds(column, half)],
                pack_ref.at[at:at + extent],
                sems.at[i],
            )
        )
        at += extent
    for copy in copies:
        copy.start()
    row = lax.broadcasted_iota(jnp.int32, (FEAT, half), 0)
    total = jnp.zeros((FEAT, half), f32)
    for c in range(2):
        total = total + split_rows(bias_ref[:, c * half:(c + 1) * half], FEAT, half, 3 * c)
    pack_ref[at:] = total.astype(bf16)
    for copy in copies:
        copy.wait()


def make_pack(me, chips, up, down, out, bias):
    depth, local = up.shape
    half, width = local // 2, out.shape[0]
    rows = depth // chips + 2 * (half // chips + width // (2 * chips)) + FEAT
    hbm = pl.BlockSpec(memory_space=pl.ANY)
    vmem = pl.BlockSpec(memory_space=pltpu.VMEM)
    return pl.pallas_call(
        functools.partial(pack_kernel, chips),
        in_specs=[pl.BlockSpec(memory_space=pltpu.SMEM), hbm, hbm, hbm, vmem],
        out_specs=vmem,
        out_shape=jax.ShapeDtypeStruct((rows, half), bf16),
        scratch_shapes=[pltpu.SemaphoreType.DMA((5,))],
        name="pack",
    )(me, up, down, out, bias[None])


def attend_kernel(heads, me_ref, qt_ref, kn_ref, vt_ref, *refs):
    ctx_ref, lse_ref = refs[-2:]
    for h in range(heads):
        scores = nn(kn_ref[h], qt_ref[h])
        top = jnp.maximum(jnp.max(scores, axis=0, keepdims=True), FLOOR)
        weights = jnp.exp2(scores - top).astype(bf16)
        mixed = nn(vt_ref[h], weights)
        total = mixed[HEAD:HEAD + 1] + jnp.where(top <= FLOOR, 1.0, 0.0)
        ctx_ref[0, h * HEAD:(h + 1) * HEAD] = (mixed[:HEAD] / total).astype(bf16)
        lse_ref[0, h] = top + jnp.log2(total)


def attend(me, first, count, n_mp, qt, kn, vt, after):
    heads, _, rows = qt.shape
    own = rows // n_mp
    block = min(256, own)
    blocks = own // block
    whole = lambda *shape: pl.BlockSpec(shape, lambda i, me: (0,) * len(shape))
    return pl.pallas_call(
        functools.partial(attend_kernel, heads),
        grid_spec=pltpu.PrefetchScalarGridSpec(
            num_scalar_prefetch=1,
            grid=(count * blocks,),
            in_specs=[
                pl.BlockSpec(
                    (heads, LANES, block),
                    lambda i, me: (
                        0, 0, (me[0] ^ (first - i // blocks)) * blocks + i % blocks
                    ),
                ),
                whole(heads, rows, LANES),
                whole(heads, HEAD + FEAT, rows),
            ]
            + [pl.BlockSpec(memory_space=pl.ANY)] * len(after),
            out_specs=[
                pl.BlockSpec(
                    (1, heads * HEAD, block), lambda i, me: (i // blocks, 0, i % blocks)
                ),
                pl.BlockSpec(
                    (1, heads, 1, block), lambda i, me: (i // blocks, 0, 0, i % blocks)
                ),
            ],
        ),
        out_shape=[
            jax.ShapeDtypeStruct((count, heads * HEAD, own), bf16),
            jax.ShapeDtypeStruct((count, heads, 1, own), f32),
        ],
        compiler_params=params("arbitrary"),
        cost_estimate=pl.CostEstimate(
            flops=20 * heads * own * rows * HEAD * count,
            bytes_accessed=8 * rows * LANES * heads,
            transcendentals=heads * own * rows * count,
        ),
        name="attend",
    )(me, qt, kn, vt, *after)


def split_rows(value, count, rows, first):
    high = value.astype(bf16).astype(f32)
    rest = value - high
    middle = rest.astype(bf16).astype(f32)
    low = rest - middle
    row = lax.broadcasted_iota(jnp.int32, (count, rows), 0) - first
    return jnp.where(
        row == 0, high, jnp.where(row == 1, middle, jnp.where(row == 2, low, 0.0))
    )


def attend_back_kernel(
    chunk, me_ref, qt_ref, kt_ref, kn_ref, vn_ref, dot_ref, delta_ref, lse_ref, cosq_ref, sinq_ref,
    cos_ref, sin_ref, *refs,
):
    dq_ref, dk_ref, dv_ref, send_ref, dk_acc, dv_acc = refs[-6:]
    outer, inner = pl.program_id(0), pl.program_id(1)
    rows = kn_ref.shape[1]
    block = qt_ref.shape[2]
    query = qt_ref[0, :HEAD]
    grad = dot_ref[0]
    query_full = jnp.concatenate(
        [
            qt_ref[0, :HEAD + FEAT],
            split_rows(-lse_ref[0, 0], FEAT, block, 0).astype(bf16),
            jnp.zeros((LANES - HEAD - 2 * FEAT, block), bf16),
        ],
        axis=0,
    )
    grad_full = jnp.concatenate(
        [grad, delta_ref[0], jnp.zeros((LANES - HEAD - FEAT, block), bf16)], axis=0
    )

    @pl.when((outer == 0) & (inner == 0))
    def _():
        dk_acc[...] = jnp.zeros_like(dk_acc)
        dv_acc[...] = jnp.zeros_like(dv_acc)

    total = None
    for start in range(0, rows, chunk):
        part = slice(start, start + chunk)
        weights = jnp.exp2(nn(kn_ref[0, part], query_full))
        slopes = nn(vn_ref[0, part], grad_full)
        score_grad = (weights * slopes).astype(bf16)
        dv_acc[:, part] += nt(grad, weights.astype(bf16))
        dk_acc[:, part] += nt(query, score_grad)
        piece = nn(kt_ref[0, :, part], score_grad)
        total = piece if total is None else total + piece
    merge = interleave_matrix(True)

    def turn_back(value, cosine, sine, scale):
        former = value[:HALF] * scale
        latter = value[HALF:] * scale
        turned = jnp.concatenate(
            [former * cosine + latter * sine, latter * cosine - former * sine], axis=0
        )
        return nn(merge, turned.astype(bf16)).astype(bf16)

    dq = turn_back(total, cosq_ref[...], sinq_ref[...], 1.0 / math.sqrt(HEAD))
    dq_ref[...] = dq
    send_ref[outer, :HEAD, pl.ds(pl.multiple_of(inner * block, block), block)] = dq

    @pl.when((outer == pl.num_programs(0) - 1) & (inner == pl.num_programs(1) - 1))
    def _():
        dk = turn_back(dk_acc[...], cos_ref[...], sin_ref[...], LN2)
        dv = dv_acc[...].astype(bf16)
        dk_ref[...] = dk
        dv_ref[...] = dv
        count, _, own = send_ref.shape
        for j in range(count):
            send_ref[j, HEAD:2 * HEAD] = dk[:, j * own:(j + 1) * own]
            send_ref[j, 2 * HEAD:] = dv[:, j * own:(j + 1) * own]


def attend_back(me, head, n_mp, qt, kt, kn, vn, grads, lse, cosine, sine, after):
    heads, _, rows = qt.shape
    width = heads * HEAD
    own = rows // n_mp
    block = min(256, own)
    blocks = own // block
    chunk = min(512, rows)
    place = lambda j, i: j * blocks + i
    by_head = lambda *shape: pl.BlockSpec((1,) + shape, lambda j, i, me: (head, 0, 0))
    whole = lambda *shape: pl.BlockSpec(shape, lambda j, i, me: (0,) * len(shape))
    here = lambda count: pl.BlockSpec((count, block), lambda j, i, me: (0, place(j, i)))
    return pl.pallas_call(
        functools.partial(attend_back_kernel, chunk),
        grid_spec=pltpu.PrefetchScalarGridSpec(
            num_scalar_prefetch=1,
            grid=(n_mp, blocks),
            in_specs=[
                pl.BlockSpec((1, LANES, block), lambda j, i, me: (head, 0, place(j, i))),
                by_head(HEAD, rows),
                by_head(rows, LANES),
                by_head(rows, LANES),
                pl.BlockSpec((1, HEAD, block), lambda j, i, me: (j, head, i)),
                pl.BlockSpec((1, FEAT, block), lambda j, i, me: (j, width // FEAT, i)),
                pl.BlockSpec((1, 1, 1, block), lambda j, i, me: (me[0] ^ j, head, 0, i)),
                here(HALF),
                here(HALF),
                whole(HALF, rows),
                whole(HALF, rows),
            ]
            + [pl.BlockSpec(memory_space=pl.ANY)] * len(after),
            out_specs=[
                here(HEAD), whole(HEAD, rows), whole(HEAD, rows), whole(n_mp, 3 * HEAD, own)
            ],
            scratch_shapes=[pltpu.VMEM((HEAD, rows), f32)] * 2,
        ),
        out_shape=[jax.ShapeDtypeStruct((HEAD, rows), bf16)] * 3
        + [jax.ShapeDtypeStruct((n_mp, 3 * HEAD, own), bf16)],
        compiler_params=params("arbitrary", "arbitrary"),
        cost_estimate=pl.CostEstimate(
            flops=80 * rows * rows * HEAD,
            bytes_accessed=8 * rows * LANES,
            transcendentals=rows * rows,
        ),
        name="attend_back",
    )(me, qt, kt, kn, vn, grads, grads, lse, cosine, sine, cosine, sine, *after)


def gelu_parts(value):
    cumulative = 0.5 * (1.0 + lax.erf(value * 0.7071067811865476))
    density = jnp.exp(-0.5 * value * value) * 0.3989422804014327
    return value * cumulative, cumulative + value * density


def row_mean(value):
    return jnp.mean(value, axis=-1, keepdims=True)


def plane_orders(count):
    bits = [1 << b for b in range(count.bit_length() - 1)]
    orders = []
    for sequence in (bits, bits[::-1]):
        held = [0]
        for bit in sequence:
            held = held + [r ^ bit for r in held]
        orders.append(held)
    return orders


def weight_copies(n_mp, packed, splits, me_ref, weights, banks, targets, sems):
    depth, local = weights[1].shape
    width = weights[0].shape[0]
    copies = [[[], [], []] for _ in range(n_mp)]
    for m, source in enumerate(weights):
        copies[0][m].append(
            pltpu.make_async_copy(source, targets[m].at[0], sems.at[0, m, 0])
        )
    for s in range(1, n_mp):
        if not packed:
            for m in range(3):
                copies[s][m].append(
                    pltpu.make_async_copy(
                        banks[m].at[s - 1], targets[m].at[s], sems.at[s, m, 0]
                    )
                )
            continue
        group = max(i for i in range(len(splits) - 1) if splits[i] <= s)
        member = s - splits[group]
        half, chips = local // 2, packed // 2
        ups, downs, outs = depth // chips, half // chips, width // packed
        orders = plane_orders(chips)
        for core in range(2):
            mine = (me_ref[1] & 1) ^ core
            for r in range(chips):
                for kind in range(2):
                    source = banks[4 * group + 2 * core + kind].at[r, member]
                    chip = (me_ref[1] >> 1) ^ orders[kind][r]
                    if kind == 0:
                        pieces = [(1, 0, ups, chip * ups, mine * half)]
                    else:
                        at = pl.multiple_of(mine * half + chip * downs, downs)
                        pieces = [(2, c * downs, downs, at, c * half) for c in range(2)]
                        at = mine * (width // 2) + chip * outs
                        pieces += [
                            (0, 2 * downs + c * outs, outs, at, c * half) for c in range(2)
                        ]
                    for m, start, extent, row, column in pieces:
                        row = pl.multiple_of(row, extent)
                        if m == 1:
                            column = pl.multiple_of(column, half)
                        copies[s][m].append(
                            pltpu.make_async_copy(
                                source.at[start:start + extent],
                                targets[m].at[s, pl.ds(row, extent), pl.ds(column, half)],
                                sems.at[s, m, len(copies[s][m])],
                            )
                        )
    return copies


def column(value):
    return jnp.sum(value, axis=0, keepdims=True)


def run_all(groups, action):
    for group in groups:
        for copy in group:
            getattr(copy, action)()


def feed_kernel(n_mp, packed, splits, me_ref, hidden_ref, cot_ref, *refs):
    refs = list(refs)
    take = lambda count: [refs.pop(0) for _ in range(count)]
    contexts = take(n_mp)
    weights = take(3)
    banks = take(4 * (len(splits) - 1) if packed else 3)
    bias_ref, vectors_ref = take(2)
    (
        result_ref, first_low_ref, act_ref, slope_ref, lg_ref, normed_ref, inv_ref, back_ref,
        vec_ref, out_s, up_s, down_s, first_s, sems,
    ) = refs
    depth, local = weights[1].shape
    own = hidden_ref.shape[0]
    width = weights[0].shape[0]
    step = min(512, local)
    copies = weight_copies(
        n_mp, packed, splits, me_ref, weights, banks, (out_s, up_s, down_s), sems
    )
    for m in range(3):
        run_all([copies[s][m] for s in range(n_mp)], "start")
    run_all([copies[s][0] for s in range(n_mp)], "wait")

    out_bias, first_gain, first_shift, down_bias, second_gain, second_shift = (
        vectors_ref[i:i + 1, :] for i in range(6)
    )
    summed = hidden_ref[...].astype(f32) + out_bias
    for s in range(n_mp):
        summed = summed + tn(contexts[s][:width], out_s[s])
    centered = summed - row_mean(summed)
    first_inv = lax.rsqrt(row_mean(centered * centered) + epsilon)
    inv_ref[...] = jnp.broadcast_to(first_inv, inv_ref.shape)
    normed = centered * first_inv
    normed_ref[...] = normed
    first = normed * first_gain + first_shift
    first_s[...] = first
    first_low_ref[...] = first.astype(bf16)

    lowered = None
    for s in range(n_mp):
        run_all(copies[s][1:], "wait")
        for start in range(0, local, step):
            part = slice(start, start + step)
            upper = nn(first_low_ref[...], up_s[s, :, part]) + bias_ref[s:s + 1, part]
            value, slope = gelu_parts(upper)
            act = value.astype(bf16)
            act_ref[s, :, part] = act
            slope_ref[s, :, part] = slope.astype(bf16)
            piece = nn(act, down_s[s, part, :])
            lowered = piece if lowered is None else lowered + piece

    summed = first_s[...] + (lowered + down_bias)
    centered = summed - row_mean(summed)
    second_inv = lax.rsqrt(row_mean(centered * centered) + epsilon)
    normed = centered * second_inv
    result_ref[...] = (normed * second_gain + second_shift).astype(bf16)
    cotangent = cot_ref[...].astype(f32)
    grad = cotangent * second_gain
    back = second_inv * (grad - row_mean(grad) - normed * row_mean(grad * normed))
    back_ref[...] = back
    low = back.astype(bf16)
    lg_ref[...] = low
    vec_ref[0:1] = column(low.astype(f32))
    vec_ref[1:2] = column(cotangent * normed)
    vec_ref[2:3] = column(cotangent)


def feed_back_kernel(n_mp, packed, splits, me_ref, *refs):
    refs = list(refs)
    take = lambda count: [refs.pop(0) for _ in range(count)]
    contexts = take(n_mp)
    weights = take(3)
    banks = take(4 * (len(splits) - 1) if packed else 3)
    slope_ref, lg_ref, normed_ref, inv_ref, second_ref, some_ref, gain_ref = take(7)
    ug_ref, ag_ref, back_ref, dctx_ref, vec_ref, out_s, up_s, down_s, sems = refs[-9:]
    depth, local = weights[1].shape
    own = lg_ref.shape[0]
    width = weights[0].shape[0]
    heads = width // HEAD
    step = min(512, local)
    copies = weight_copies(
        n_mp, packed, splits, me_ref, weights, banks, (out_s, up_s, down_s), sems
    )
    for s in range(n_mp):
        run_all(copies[s][:0:-1], "start")
    run_all([copies[s][0] for s in range(n_mp)], "start")

    first_grad = second_ref[...]
    up_bias_grads = []
    for s in range(n_mp):
        run_all(copies[s][:0:-1], "wait")
        sums = []
        for start in range(0, local, step):
            part = slice(start, start + step)
            ug = (nt(lg_ref[...], down_s[s, part, :]) * slope_ref[s, :, part]).astype(bf16)
            ug_ref[s, :, part] = ug
            sums.append(column(ug.astype(f32)))
            first_grad = first_grad + nt(ug, up_s[s, :, part])
        up_bias_grads.append(jnp.concatenate(sums, axis=1))

    normed = normed_ref[...]
    grad = first_grad * gain_ref[...]
    back = grad - row_mean(grad) - normed * row_mean(grad * normed)
    back = inv_ref[:, :1] * back
    back_ref[...] = back
    low = back.astype(bf16)
    ag_ref[...] = low
    sums = [
        column(low.astype(f32)), column(first_grad * normed), column(first_grad),
        some_ref[0:1], some_ref[1:2], some_ref[2:3],
    ]
    row = lax.broadcasted_iota(jnp.int32, (FEAT, depth), 0)
    block = jnp.zeros((FEAT, depth), f32)
    for index, value in enumerate(sums):
        block = jnp.where(row == 1 + index, value, block)
    for s in range(n_mp):
        vec_ref[s] = block.astype(bf16)
        vec_ref[s, 0:1, :local] = up_bias_grads[s].astype(bf16)

    run_all([copies[s][0] for s in range(n_mp)], "wait")
    for s in range(n_mp):
        plane = me_ref[0] ^ s
        grads = nt(out_s[s], low).astype(bf16)
        dctx_ref[plane, :width] = grads
        product = grads.astype(f32) * contexts[s][:width].astype(f32)
        rows = None
        for h in range(heads):
            delta = -jnp.sum(product[h * HEAD:(h + 1) * HEAD], axis=0, keepdims=True)
            piece = split_rows(delta, FEAT, own, 3 * h)
            rows = piece if rows is None else rows + piece
        dctx_ref[plane, width:] = rows.astype(bf16)


def weight_scratch(n_mp, packed, width, depth, local):
    return [
        pltpu.VMEM((n_mp, width, depth), bf16),
        pltpu.VMEM((n_mp, depth, local), bf16),
        pltpu.VMEM((n_mp, local, depth), bf16),
    ], pltpu.SemaphoreType.DMA((n_mp, 3, max(2 * packed, 1)))


def feed(me, n_mp, packed, splits, hidden, out_grad, contexts, weights, banks, biases, vectors):
    rows, depth = hidden.shape
    own = rows // n_mp
    width, local = weights[0].shape[0], weights[1].shape[1]
    vmem = pl.BlockSpec(memory_space=pltpu.VMEM)
    hbm = pl.BlockSpec(memory_space=pl.ANY)
    mine = pl.BlockSpec((own, depth), lambda i, me: (me[0], 0))
    shape = jax.ShapeDtypeStruct
    scratch, sems = weight_scratch(n_mp, packed, width, depth, local)
    return pl.pallas_call(
        functools.partial(feed_kernel, n_mp, packed, splits),
        grid_spec=pltpu.PrefetchScalarGridSpec(
            num_scalar_prefetch=1,
            grid=(1,),
            in_specs=[mine, mine]
            + [vmem] * n_mp
            + [hbm] * (3 + len(banks))
            + [vmem, vmem],
            out_specs=[vmem] * 9,
            scratch_shapes=scratch + [pltpu.VMEM((own, depth), f32), sems],
        ),
        out_shape=[
            shape((own, depth), bf16),
            shape((own, depth), bf16),
            shape((n_mp, own, local), bf16),
            shape((n_mp, own, local), bf16),
            shape((own, depth), bf16),
            shape((own, depth), f32),
            shape((own, LANES), f32),
            shape((own, depth), f32),
            shape((8, depth), f32),
        ],
        compiler_params=params("arbitrary"),
        cost_estimate=pl.CostEstimate(
            flops=8 * own * depth * local * n_mp,
            bytes_accessed=4 * depth * local * n_mp,
            transcendentals=2 * own * local * n_mp,
        ),
        name="feed",
    )(me, hidden, out_grad, *contexts, *weights, *banks, biases, vectors)


def feed_back(
    me, n_mp, packed, splits, contexts, weights, banks, slope, lg, normed, inv, second, some, gain
):
    own, depth = lg.shape
    width, local = weights[0].shape[0], weights[1].shape[1]
    vmem = pl.BlockSpec(memory_space=pltpu.VMEM)
    hbm = pl.BlockSpec(memory_space=pl.ANY)
    shape = jax.ShapeDtypeStruct
    scratch, sems = weight_scratch(n_mp, packed, width, depth, local)
    return pl.pallas_call(
        functools.partial(feed_back_kernel, n_mp, packed, splits),
        grid_spec=pltpu.PrefetchScalarGridSpec(
            num_scalar_prefetch=1,
            grid=(1,),
            in_specs=[vmem] * n_mp + [hbm] * (3 + len(banks)) + [vmem] * 7,
            out_specs=[vmem] * 5,
            scratch_shapes=scratch + [sems],
        ),
        out_shape=[
            shape((n_mp, own, local), bf16),
            shape((own, depth), bf16),
            shape((own, depth), f32),
            shape((n_mp, width + FEAT, own), bf16),
            shape((n_mp, FEAT, depth), bf16),
        ],
        compiler_params=params("arbitrary"),
        cost_estimate=pl.CostEstimate(
            flops=8 * own * depth * local * n_mp,
            bytes_accessed=4 * depth * local * n_mp,
            transcendentals=0,
        ),
        name="feed_back",
    )(me, *contexts, *weights, *banks, slope, lg, normed, inv, second, some, gain)


def weigh_kernel(shares, first_ref, act_ref, ug_ref, lg_ref, ctx_ref, ag_ref, vec_ref, *refs):
    out_ref = refs[-1]
    out_rows, up_rows, down_rows = shares
    outs = nn(ctx_ref[0], ag_ref[...]).astype(bf16)
    ups = tn(first_ref[...], ug_ref[0]).astype(bf16)
    downs = tn(act_ref[0], lg_ref[...]).astype(bf16)
    for d in range(out_ref.shape[0]):
        at = 0
        for value, extent in ((outs, out_rows), (ups, up_rows), (downs, down_rows)):
            out_ref[d, 0, at:at + extent] = value[d * extent:(d + 1) * extent]
            at += extent
        out_ref[d, 0, at:] = vec_ref[0]


def weigh(n_dp, width, start, step, first_low, act, ug, lg, ctx, ag, vec, after):
    own, depth = first_low.shape
    n_mp, _, local = act.shape
    shares = (width // n_dp, depth // n_dp, local // n_dp)
    total = sum(shares) + FEAT
    count = min(4, n_dp)
    planes = n_mp // step
    whole = lambda *shape: pl.BlockSpec(shape, lambda s, d: (0, 0))
    return pl.pallas_call(
        functools.partial(weigh_kernel, shares),
        grid=(planes, n_dp // count),
        in_specs=[
            pl.BlockSpec((own, count * shares[1]), lambda s, d: (0, d)),
            pl.BlockSpec((1, own, count * shares[2]), lambda s, d: (start + step * s, 0, d)),
            pl.BlockSpec((1, own, local), lambda s, d: (start + step * s, 0, 0)),
            whole(own, depth),
            pl.BlockSpec((1, count * shares[0], own), lambda s, d: (start + step * s, d, 0)),
            whole(own, depth),
            pl.BlockSpec((1, FEAT, depth), lambda s, d: (start + step * s, 0, 0)),
        ]
        + [pl.BlockSpec(memory_space=pl.ANY)] * len(after),
        out_specs=pl.BlockSpec((count, 1, total, depth), lambda s, d: (d, s, 0, 0)),
        out_shape=jax.ShapeDtypeStruct((n_dp, planes, total, depth), bf16),
        compiler_params=params("arbitrary", "arbitrary"),
        cost_estimate=pl.CostEstimate(
            flops=8 * own * depth * local * planes,
            bytes_accessed=4 * depth * local * planes,
            transcendentals=0,
        ),
        name="weigh",
    )(first_low, act, ug, lg, ctx, ag, vec, *after)


def input_kernel(n_mp, packed, first, me_ref, back_ref, own_ref, bank_ref, *refs):
    grads, (out_ref, weight_s, sems) = refs[:-3], refs[-3:]
    total_rows = own_ref.shape[0]
    copies = [pltpu.make_async_copy(own_ref, weight_s.at[0], sems.at[0, 0])]
    for s in range(1, n_mp):
        if packed:
            rows = total_rows // packed
            for d in range(packed):
                if first * 3 * HEAD <= d * rows < (first + len(grads)) * 3 * HEAD:
                    copies.append(
                        pltpu.make_async_copy(
                            bank_ref.at[d, s - 1],
                            weight_s.at[s, d * rows:(d + 1) * rows],
                            sems.at[s, d],
                        )
                    )
        else:
            copies.append(
                pltpu.make_async_copy(bank_ref.at[s - 1], weight_s.at[s], sems.at[s, 0])
            )
    for copy in copies:
        copy.start()
    for copy in copies:
        copy.wait()
    total = back_ref[...]
    for h, grad_ref in enumerate(grads):
        part = slice(3 * HEAD * (first + h), 3 * HEAD * (first + h + 1))
        for s in range(n_mp):
            total = total + tn(grad_ref[me_ref[0] ^ s], weight_s[s, part])
    out_ref[...] = total.astype(out_ref.dtype)


def input_gradient(me, n_mp, packed, first, back, own_weight, bank, grads, kind):
    vmem = pl.BlockSpec(memory_space=pltpu.VMEM)
    hbm = pl.BlockSpec(memory_space=pl.ANY)
    return pl.pallas_call(
        functools.partial(input_kernel, n_mp, packed, first),
        in_specs=[pl.BlockSpec(memory_space=pltpu.SMEM), vmem, hbm, hbm] + [vmem] * len(grads),
        out_specs=vmem,
        out_shape=jax.ShapeDtypeStruct(back.shape, kind),
        scratch_shapes=[
            pltpu.VMEM((n_mp,) + own_weight.shape, bf16),
            pltpu.SemaphoreType.DMA((n_mp, max(packed, 1))),
        ],
        compiler_params=pltpu.CompilerParams(vmem_limit_bytes=VMEM_LIMIT),
        cost_estimate=pl.CostEstimate(
            flops=2 * back.size * own_weight.shape[0] * n_mp,
            bytes_accessed=2 * own_weight.size * n_mp,
            transcendentals=0,
        ),
        name="input_gradient",
    )(me, back, own_weight, bank, *grads)


def line_kernel(count, me_ref, own_ref, *refs):
    ahead, behind = refs[:count - 1], refs[count - 1:2 * count - 2]
    out_ref, slots, sems = refs[2 * count - 2:]
    me = me_ref[0]
    for k in range(count):
        if k == 0:
            pltpu.make_async_copy(own_ref, slots.at[0], sems.at[0, 0]).start()
            continue

        @pl.when(me >= k)
        def _():
            pltpu.make_async_copy(ahead[k - 1], slots.at[k], sems.at[0, k]).start()

        @pl.when(me < k)
        def _():
            pltpu.make_async_copy(behind[count - k - 1], slots.at[k], sems.at[0, k]).start()

    outs = []
    for k in range(count):
        pltpu.make_async_copy(own_ref, slots.at[k], sems.at[0, k]).wait()
        place = lax.rem(me + count - k, count)
        outs.append(pltpu.make_async_copy(slots.at[k], out_ref.at[place], sems.at[1, k]))
        outs[-1].start()
    for copy in outs:
        copy.wait()


def join_line(me, value, ahead, behind):
    count = len(ahead) + 1
    hbm = pl.BlockSpec(memory_space=pl.ANY)
    return pl.pallas_call(
        functools.partial(line_kernel, count),
        in_specs=[pl.BlockSpec(memory_space=pltpu.SMEM)] + [hbm] * (2 * count - 1),
        out_specs=hbm,
        out_shape=jax.ShapeDtypeStruct((count,) + value.shape, value.dtype),
        scratch_shapes=[
            pltpu.VMEM((count,) + value.shape, value.dtype),
            pltpu.SemaphoreType.DMA((2, count)),
        ],
        compiler_params=pltpu.CompilerParams(vmem_limit_bytes=VMEM_LIMIT),
        name="join_line",
    )(me, value, *ahead, *behind)


def weigh_input_kernel(hidden_ref, *refs):
    out_ref = refs[-1]
    depth, width = hidden_ref.shape[1], out_ref.shape[2]
    heads = width // HEAD
    for i in range(3):
        grads = jnp.concatenate([refs[3 * h + i][...] for h in range(heads)])
        out_ref[i, :depth] = nn(grads, hidden_ref[...]).T.astype(bf16)
        total = jnp.sum(grads.astype(f32), axis=1, keepdims=True)
        total = jnp.broadcast_to(total, (width, LANES)).T[:FEAT]
        out_ref[i, depth:] = total.astype(bf16)


def weigh_input(hidden, parts):
    rows, depth = hidden.shape
    width = len(parts) * HEAD
    vmem = pl.BlockSpec(memory_space=pltpu.VMEM)
    return pl.pallas_call(
        weigh_input_kernel,
        in_specs=[vmem] * (1 + 3 * len(parts)),
        out_specs=vmem,
        out_shape=jax.ShapeDtypeStruct((3, depth + FEAT, width), bf16),
        compiler_params=pltpu.CompilerParams(vmem_limit_bytes=VMEM_LIMIT),
        cost_estimate=pl.CostEstimate(
            flops=6 * rows * depth * width, bytes_accessed=8 * rows * depth, transcendentals=0
        ),
        name="weigh_input",
    )(hidden, *[item for part in parts for item in part])


def unpack_kernel(in_ref, *out_refs):
    at = 0
    for out_ref in out_refs:
        rows = out_ref.shape[0]
        out_ref[...] = in_ref[0, at:at + rows].astype(f32)
        at += rows


def unpack(shares, parts):
    count, total, depth = shares.shape
    return pl.pallas_call(
        unpack_kernel,
        grid=(count,),
        in_specs=[pl.BlockSpec((1, total, depth), lambda i: (i, 0, 0))],
        out_specs=[pl.BlockSpec((rows, depth), lambda i: (i, 0)) for rows in parts],
        out_shape=[jax.ShapeDtypeStruct((count * rows, depth), f32) for rows in parts],
        compiler_params=params("arbitrary"),
        name="unpack",
    )(shares)


def weigh_plain(s, n_dp, first_low, act, ug, lg, context, ag, vec):
    depth = first_low.shape[1]
    parts = [nn(context, ag), tn(first_low, ug[s]), tn(act[s], lg)]
    parts = [item.astype(bf16).reshape(n_dp, -1, depth) for item in parts]
    parts.append(jnp.broadcast_to(vec[s][None], (n_dp, FEAT, depth)))
    return jnp.concatenate(parts, axis=1)


def cross(value, count, bits):
    return lax.ppermute(value, "mp", [(i, i ^ bits) for i in range(count)])


def tie(values, others):
    return lax.optimization_barrier((values, others))[0]


def trade(value):
    return lax.all_to_all(value, "mp", 0, 0, tiled=True)


def swap(value, count, bit):
    return lax.ppermute(value, "dp", [(i, i ^ bit) for i in range(count)])


def hop(came, k, count):
    ahead, behind = came
    return (
        lax.ppermute(ahead, "mp", [(i, i + 1) for i in range(k - 1, count - 1)]),
        lax.ppermute(behind, "mp", [(i, i - 1) for i in range(1, count - k + 1)]),
    )


def finish_line(value, hops, me, count):
    while len(hops) < count - 1:
        hops = hops + [hop(hops[-1] if hops else (value, value), len(hops) + 1, count)]
    total = join_line(me, value, *zip(*hops))
    return total.reshape((-1,) + value.shape[1:])


def local(
    n_dp,
    n_mp,
    hidden,
    lengths,
    query_weight,
    query_bias,
    key_weight,
    key_bias,
    value_weight,
    value_bias,
    out_weight,
    out_bias,
    first_gain,
    first_shift,
    up_weight,
    up_bias,
    down_weight,
    down_bias,
    second_gain,
    second_shift,
    out_grad,
):
    rows, depth = hidden.shape
    width = query_weight.shape[1]
    hidden_local = up_weight.shape[1]
    heads = width // HEAD
    own = rows // n_mp
    me = lax.axis_index("mp")
    peer = lax.axis_index("dp")
    steps = range(n_mp)
    place = jnp.stack([me, peer]).astype(jnp.int32)

    def share_of(weight):
        share = weight.shape[0] // n_dp
        return lax.dynamic_slice_in_dim(weight, peer * share, share, 0)

    def gather_plane(value):
        return lax.all_gather(value, "dp", axis=0)

    def gather_others(weight):
        shares = [gather_plane(cross(share_of(weight), n_mp, s)) for s in steps if s]
        return jnp.stack([item.reshape(weight.shape) for item in shares])

    weights = [out_weight, up_weight, down_weight]
    qt, kt, kn, vt, vn, cosine, sine, turned = project(
        lengths, hidden, query_weight, key_weight, value_weight, query_bias, key_bias, value_bias
    )
    chips = n_dp // 2
    packed = n_dp if width // n_dp % FEAT == 0 and hidden_local == depth else 0
    splits = [1, n_mp - 1, n_mp] if n_mp > 2 else [1, n_mp]
    if packed:
        half = hidden_local // 2
        up_rows, down_rows, out_rows = depth // chips, half // chips, width // n_dp
        pack = make_pack(place, chips, up_weight, down_weight, out_weight, up_bias)
        marks = [up_rows, up_rows + 2 * (down_rows + out_rows)]
        crossed = {0: pack}
        for s in steps:
            if s & (s - 1) == 0 and s:
                crossed[s] = cross(pack, n_mp, s)
        bits = [2 << b for b in range(chips.bit_length() - 1)]

        def begin(group):
            group = jnp.stack([crossed[s] for s in group])[None]
            return [group[:, :, :marks[0]], group[:, :, marks[0]:marks[1]]]

        def double(held, step):
            came = [swap(held[0], n_dp, bits[step]), swap(held[1], n_dp, bits[-1 - step])]
            return came, lambda came: [jnp.concatenate(pair) for pair in zip(held, came)]

    contexts, tops, results = [None] * n_mp, [None] * n_mp, []

    def attend_next(after, count=1):
        first = n_mp - 1 - len(results)
        ctx, top = attend(place, first, count, n_mp, qt, kn, vt, after)
        for i in range(count):
            s = first - i
            tops[s] = top[i]
            results.append(ctx)
            contexts[s] = cross(ctx[i], n_mp, s) if s else ctx[i]

    if packed and n_mp == 4 and len(bits) == 2:
        attend_next([])
        crossed[1], crossed[2] = tie((crossed[1], crossed[2]), results[0])
        crossed[3] = cross(crossed[2], n_mp, 1)
        near = begin([1, 2])
        near_came, near_join = double(near, 0)
        attend_next([])
        near_came, crossed[3], contexts[3] = tie(
            (near_came, crossed[3], contexts[3]), results[1]
        )
        near = near_join(near_came)
        near_came, near_join = double(near, 1)
        far = begin([3])
        far_came, far_join = double(far, 0)
        attend_next([contexts[3]] + near + far, 2)
        near_came, far_came, contexts[2] = tie(
            (near_came, far_came, contexts[2]), results[3]
        )
        near, far = near_join(near_came), far_join(far_came)
        far_came, far_join = double(far, 1)
        near_other = [swap(item, n_dp, 1) for item in near]
        far = tie(far_join(far_came), contexts[1])
        banks = near + near_other + far + [swap(item, n_dp, 1) for item in far]
    else:
        for s in steps:
            attend_next([])
        if packed:
            banks = []
            for s in steps:
                if s & (s - 1):
                    crossed[s] = cross(crossed[s & (s - 1)], n_mp, s & -s)
            for i in range(len(splits) - 1):
                held = begin(range(splits[i], splits[i + 1]))
                for step in range(len(bits)):
                    came, join = double(held, step)
                    held = join(came)
                banks += held + [swap(item, n_dp, 1) for item in held]
    if packed:
        biases = [crossed[s][marks[1]:marks[1] + FEAT] for s in steps]
        biases = jnp.stack(
            [
                jnp.concatenate([jnp.sum(item[3 * c:3 * c + 3].astype(f32), 0) for c in range(2)])
                for item in biases
            ]
        )
    else:
        banks = [gather_others(item) for item in weights]
        biases = jnp.stack([up_bias] + [cross(up_bias, n_mp, s) for s in steps if s])
    tops = jnp.stack(tops)

    vectors = jnp.stack(
        [out_bias, first_gain, first_shift, down_bias, second_gain, second_shift]
    )
    result_own, first_low, act, slope, lg, normed, inv, second_back, some = feed(
        place, n_mp, packed, splits, hidden, out_grad, contexts, weights, banks, biases, vectors,
    )
    if packed:
        share = share_of(turned)
        shares = tie([cross(share, n_mp, s) for s in steps if s], lg)
        input_bank = gather_plane(jnp.stack(shares))
    else:
        input_bank = gather_others(turned)
    ug, ag, first_back, dctx, vec = feed_back(
        place, n_mp, packed, splits, contexts, weights, banks, slope, lg, normed, inv,
        second_back, some, first_gain[None],
    )
    came = tie(hop((result_own, result_own), 1, n_mp), lg if n_mp == 2 else ag)
    hops = [came]
    grads = trade(dctx)

    if packed:
        stacked = jnp.stack([item[:width] for item in contexts])
        operands = (first_low, act, ug, lg, stacked, ag, vec)
        odd = weigh(n_dp, width, 1, 2, *operands, list(came))
        even = weigh(n_dp, width, 0, 2, *operands, [grads])
        ready = [even]
        odd = lax.psum_scatter(tie(odd, (even, input_bank)), "dp", scatter_dimension=0, tiled=False)
        even = lax.psum_scatter(even, "dp", scatter_dimension=0, tiled=False)
    else:
        parts, ready = [], []
        for s in steps:
            part = weigh_plain(s, n_dp, first_low, act, ug, lg, contexts[s], ag, vec)
            parts.append(lax.psum_scatter(part, "dp", scatter_dimension=0, tiled=False))
        odd, even = jnp.stack(parts[1::2]), jnp.stack(parts[::2])

    parts, received = [], []
    for h in range(heads):
        after = ready if h == 0 else [came]
        after = jax.tree.leaves(after + [hops[0]]) if h == 0 else jax.tree.leaves(after)
        if h > 1:
            after.append(received[h - 2])
        *part, send = attend_back(
            place, h, n_mp, qt, kt, kn, vn, grads, tops, cosine, sine, after
        )
        if len(hops) < n_mp - 1:
            came = tie(hop(hops[-1], len(hops) + 1, n_mp), part[0])
            hops.append(came)
        elif h == n_mp - 2:
            came = odd = tie(cross(odd, n_mp, 1), part[0])
        parts.append(part)
        received.append(trade(tie(send, received[-1]) if h else send))
    if came is not odd:
        odd = cross(odd, n_mp, 1)
    result = finish_line(result_own, hops, place, n_mp)
    last = heads - 1
    sums_in = weigh_input(hidden, parts)
    input_grad = input_gradient(
        place, n_mp, packed, 0, tie(first_back, sums_in), turned, input_bank, received[:last], f32
    )
    hidden_own = input_gradient(
        place, n_mp, packed, last, input_grad, turned, input_bank, received[last:], bf16
    )
    first_hop = hop((hidden_own, hidden_own), 1, n_mp)
    even = tie(even, received[-1])
    input_sums = lax.psum(sums_in, "dp")
    tail = [first_hop]
    if n_mp > 2:
        tail.append(tie(hop(first_hop, 2, n_mp), input_sums))
    hidden_grad = finish_line(hidden_own, tail, place, n_mp)
    totals = [even[i].astype(f32) + odd[i].astype(f32) for i in range(n_mp // 2)]
    bit = 2
    while len(totals) > 1:
        sent = jnp.stack(totals[1::2]).astype(bf16)
        other = cross(sent, n_mp, bit)
        totals = [item + other[i].astype(f32) for i, item in enumerate(totals[::2])]
        bit *= 2
    total = totals[0]
    matrices = gather_plane(tie(total[:-FEAT].astype(bf16), first_hop))
    if packed:
        out_weight_grad, up_weight_grad, down_weight_grad = unpack(
            matrices, (width // n_dp, depth // n_dp, hidden_local // n_dp)
        )
    else:
        marks = [0, width, width + hidden_local, width + 2 * hidden_local]
        shapes = [(width, depth), (depth, hidden_local), (hidden_local, depth)]
        out_weight_grad, up_weight_grad, down_weight_grad = (
            matrices[:, marks[i] // n_dp:marks[i + 1] // n_dp].reshape(shapes[i]).astype(f32)
            for i in range(3)
        )
    sums = total[-FEAT:]
    input_sums = input_sums.astype(f32)
    input_grads = []
    for item in input_sums:
        input_grads += [item[:depth], item[depth]]
    return (
        result,
        hidden_grad,
        *input_grads,
        out_weight_grad,
        sums[1],
        sums[2],
        sums[3],
        up_weight_grad,
        sums[0, :hidden_local],
        down_weight_grad,
        sums[4],
        sums[5],
        sums[6],
    )


def solution(mesh):
    in_specs = (
        P("dp", None),
        P("dp", None),
        P(None, "mp"),
        P("mp"),
        P(None, "mp"),
        P("mp"),
        P(None, "mp"),
        P("mp"),
        P("mp", None),
        P(),
        P(),
        P(),
        P(None, "mp"),
        P("mp"),
        P("mp", None),
        P(),
        P(),
        P(),
        P("dp", None),
    )
    out_specs = (
        P("dp", None),
        P("dp", None),
        P(None, "mp"),
        P("mp"),
        P(None, "mp"),
        P("mp"),
        P(None, "mp"),
        P("mp"),
        P("mp", None),
        P(),
        P(),
        P(),
        P(None, "mp"),
        P("mp"),
        P("mp", None),
        P(),
        P(),
        P(),
    )
    body = functools.partial(local, mesh.shape["dp"], mesh.shape["mp"])
    return jax.shard_map(
        body, mesh=mesh, in_specs=in_specs, out_specs=out_specs, check_vma=False
    )
```

time: 1300 us -> 545 us (0.42)
  waiting for transfers between devices: 654 us -> 144 us
  matrix products: 302 us -> 0 us
  Pallas kernels: 0 us -> 260 us
  other arithmetic: 177 us -> 21.1 us
  local copies, waits for them, and re-layouts: 99.3 us -> 10.9 us
  starting transfers between devices: 0.86 us -> 83.7 us
  blocking collectives: 25.7 us -> 0 us
  loops' own time: 16.5 us -> 0 us
    psum x5 -> x1, waiting for transfers between devices: 654 us -> 21.5 us  [local(): input_sums = lax.psum(sums_in, 'dp')]
    dot_general x46 -> x0, matrix products: 302 us -> none  [the longest x8 78.5 us: masked_scores(): jnp.einsum('qhd,khd->hqk', query_part, key_low, preferred_element_type=jn...]
    pallas_call x0 -> x19, Pallas kernels: none -> 260 us  [the longest x4 76 us: attend_back(): pl.pallas_call(functools.partial(attend_back_kernel, chunk), grid_spec=pl...]
    ppermute x0 -> x35, waiting for transfers between devices: none -> 103 us  [the longest x6 54.7 us: hop(): lax.ppermute(behind, 'mp', [(i, i - 1) for i in range(1, count - k + 1)])]
    reduce_sum x14 -> x3, other arithmetic: 71.9 us -> 2.39 us  [local(): jnp.sum(item[3 * c:3 * c + 3].astype(f32), 0)]
    convert_element_type x19 -> x2, other arithmetic: 68.2 us -> 2.68 us  [the longest x1 2.42 us: local(): sent = jnp.stack(totals[1::2]).astype(bf16)]
    ppermute x0 -> x35, starting transfers between devices: none -> 52.2 us  [the longest x11 17.5 us: cross(): return lax.ppermute(value, 'mp', [(i, i ^ bits) for i in range(count)])]
    dynamic_update_slice x8 -> x0, local copies, waits for them, and re-layouts: 46.4 us -> none  [local(): context_blocks, tops, totals = lax.map(forward_block, starts)]
  transfers between devices with their start and end apart: 5 -> 45, of which waited for: 5 -> 17; matrix products, arithmetic and copies ran while one was open for 4% -> 4% of each run, Pallas kernels for 0% -> 47%
where the time goes in v1:
time: 545 us; the launch traced here: 534 us
  Pallas kernels  260 us (48%)
  waiting for transfers between devices  144 us (26%)
  starting transfers between devices  83.7 us (15%)
  other arithmetic  21.1 us (4%)
  between operations  14.9 us (3%)
  local copies, waits for them, and re-layouts  10.9 us (2%)
    pallas_call x4, Pallas kernels, attend_back(): pl.pallas_call(functools.partial(attend_back_kernel, chunk), grid_spec=pl...  76 us
    ppermute x6, waiting for transfers between devices, hop(): lax.ppermute(behind, 'mp', [(i, i - 1) for i in range(1, count - k + 1)])  54.7 us
    pallas_call x3, Pallas kernels, attend(): pl.pallas_call(functools.partial(attend_kernel, heads), grid_spec=pltpu.P...  49.6 us
    pallas_call x1, Pallas kernels, feed(): pl.pallas_call(functools.partial(feed_kernel, n_mp, packed, splits), grid...  34.8 us
    all_to_all x5, starting transfers between devices, trade(): return lax.all_to_all(value, 'mp', 0, 0, tiled=True)  30.8 us
    ppermute x11, waiting for transfers between devices, cross(): return lax.ppermute(value, 'mp', [(i, i ^ bits) for i in range(count)])  29.2 us
    pallas_call x1, Pallas kernels, feed_back(): pl.pallas_call(functools.partial(feed_back_kernel, n_mp, packed, splits),...  23.1 us
    pallas_call x2, Pallas kernels, weigh(): pl.pallas_call(functools.partial(weigh_kernel, shares), grid=(planes, n_d...  21.9 us
  transfers between devices with their start and end apart: 45, of which 17 were waited for; matrix products, arithmetic and copies ran while one was open for 4% of the time, Pallas kernels for 47%

profile of v1, /device:TPU:0, one launch (start us, length us, event | category | flops | bytes accessed | tf_op | source)
XLA Modules:
  0.0 534.4 jit_solution(13446073408034455891)
XLA Ops:
  7.9 2.6 pack.1
  10.5 4.1 collective-permute-start.1
  16.2 11.6 %project.1 = (bf16[4,128,2048]{2,1,0:T(8,128)(2,1)}, bf16[4,64,2048]{2,1,0:T(8,128)(2,1)}, bf16[4,2048,128]{2,1,0:T(8,128)(2,1)}, bf16[4,80,2048]{2,1,0:T(8,128)...) custom-call(s32[1,8]{1,0:T(1,128)} %lengths_ref.1, ...), custom_call_target="tpu_custom_call" | custom-call | flops 3221225472 | bytes 33554432 | tf_op jit(solution)/shard_map/project/pallas_call | solution.py:150
  27.8 13.2 %attend.3 = (bf16[1,256,512]{2,1,0:T(8,128)(2,1)}, f32[1,4,1,512]{3,2,1,0:T(1,128)}) custom-call(s32[2]{0:T(128)} %pad_add_fusion.me_ref, bf16[4,128,2048]{2,1,0:T(8,128)(2,1)} %get-tuple-element.97.qt_ref, bf16[4,2048,128]{2,1,0:T(8,128)(2,1)} %get-tuple-element.98.kn_ref, bf16[4,80,2048]{2,1,0:T(8,128)(2,1)} %get-tuple-element.99.vt_ref), custom_call_target="tpu_custom_call" | custom-call | flops 5368709120 | bytes 8388608 | tf_op jit(solution)/shard_map/attend/pallas_call | solution.py:254
  47.5 1.8 collective-permute-start.5
  49.3 13.2 %attend.4 = (bf16[1,256,512]{2,1,0:T(8,128)(2,1)}, f32[1,4,1,512]{3,2,1,0:T(1,128)}) custom-call(s32[2]{0:T(128)} %pad_add_fusion.me_ref, bf16[4,128,2048]{2,1,0:T(8,128)(2,1)} %get-tuple-element.97.qt_ref, bf16[4,2048,128]{2,1,0:T(8,128)(2,1)} %get-tuple-element.98.kn_ref, bf16[4,80,2048]{2,1,0:T(8,128)(2,1)} %get-tuple-element.99.vt_ref), custom_call_target="tpu_custom_call" | custom-call | flops 5368709120 | bytes 8388608 | tf_op jit(solution)/shard_map/attend/pallas_call | solution.py:254
  62.5 4.4 collective-permute-done.5.refs_0_.refs_3_
  73.5 23.3 %attend.5 = (bf16[2,256,512]{2,1,0:T(8,128)(2,1)}, f32[2,4,1,512]{3,2,1,0:T(1,128)}) custom-call(s32[2]{0:T(128)} %pad_add_fusion.me_ref, bf16[4,128,2048]{2,1,0:T(8,128)(2,1)} %get-tuple-element.97.qt_ref, bf16[4,2048,128]{2,1,0:T(8,128)(2,1)} %get-tuple-element.98.kn_ref, bf16[4,80,2048]{2,1,0:T(8,128)(2,1)} %get-tuple-element.99.vt_ref, ...), custom_call_target="tpu_custom_call" | custom-call | flops 10737418240 | bytes 8388608 | tf_op jit(solution)/shard_map/attend/pallas_call | solution.py:254
  96.8 7.1 %collective-permute-done.9 = bf16[1,1,256,512]{3,2,1,0:T(8,128)(2,1)S(1)} collective-permute-done((bf16[1,1,256,512]{3,2,1,0:T(8,128)(2,1)S(1)}, bf16[1,1,256,512]{3,2,1,0:T(8,128)(2,1)S(1)}, u32[]{:S(2)}, u32[]{:S(2)}) %collective-permute-start.9) | collective-permute-done | bytes 262176 | tf_op jit(solution)/shard_map/ppermute | solution.py:929
  104.0 3.1 pad_maximum_fusion.refs_8_
  111.8 9.7 %collective-permute-done.14 = bf16[2,1,256,512]{3,2,1,0:T(8,128)(2,1)S(1)} collective-permute-done((bf16[2,1,256,512]{3,2,1,0:T(8,128)(2,1)S(1)}, bf16[2,1,256,512]{3,2,1,0:T(8,128)(2,1)S(1)}, u32[]{:S(2)}, u32[]{:S(2)}) %collective-permute-start.14) | collective-permute-done | bytes 524320 | tf_op jit(solution)/shard_map/ppermute | solution.py:929
  122.7 2.1 collective-permute-done.15
  131.3 4.3 collective-permute-start.24
  135.7 34.8 %feed.1 = (bf16[512,1024]{1,0:T(8,128)(2,1)}, bf16[512,1024]{1,0:T(8,128)(2,1)}, bf16[4,512,1024]{2,1,0:T(8,128)(2,1)}, bf16[4,512,1024]{2,1,0:T(8,128)(2,1)}, b...) custom-call(s32[2]{0:T(128)} %pad_add_fusion.me_ref, ...), custom_call_target="tpu_custom_call" | custom-call | flops 17179869184 | bytes 16777216 | tf_op jit(solution)/shard_map/feed/pallas_call | solution.py:645
  173.3 5.5 %collective-permute-start.18 = (bf16[512,1024]{1,0:T(8,128)(2,1)S(1)}, bf16[512,1024]{1,0:T(8,128)(2,1)}, u32[]{:S(2)}, u32[]{:S(2)}) collective-permute-start(bf16[512,1024]{1,0:T(8,128)(2,1)S(1)} %copy-done.13), channel_id=1, source_target_pairs={{0,1},{1,2},{2,3},{4,5},{5,6},{6,7},{8,9},{9,10},{10,11},{12,13},{... | collective-permute-start | bytes 3145736 | tf_op jit(solution)/shard_map/ppermute | solution.py:935
  178.8 23.1 %feed_back.1 = (bf16[4,512,1024]{2,1,0:T(8,128)(2,1)}, bf16[512,1024]{1,0:T(8,128)(2,1)}, f32[512,1024]{1,0:T(8,128)}, bf16[4,272,512]{2,1,0:T(8,128)(2,1)}, bf16[4,16,1024]{2,1,0:T(8,128)(2,1)}) custom-call(s32[2]{0:T(128)} %pad_add_fusion.me_ref, bf16[256,512]{1,0:T(8,128)(2,1)} %get-tuple-element.198.refs_0_, bf16[256,512]{1,0:T(8,128)(2,1)} %copy-done.24, ...), custom_call_target="tpu_custom_call" | custom-call | flops 17179869184 | bytes 16777216 | tf_op jit(solution)/shard_map/feed_back/pallas_call | solution.py:687
  201.9 3.5 all-to-all-start
  205.7 2.2 pad_maximum_fusion.6.ctx_ref
  208.9 11.0 %weigh.3 = bf16[8,2,304,1024]{3,2,1,0:T(8,128)(2,1)} custom-call(bf16[512,1024]{1,0:T(8,128)(2,1)} %get-tuple-element.134.first_ref, bf16[4,512,1024]{2,1,0:T(8,128)(2,1)} %get-tuple-element.135.act_ref, bf16[4,512,1024]{2,1,0:T(8,128)(2,1)} %get-tuple-element.136.ug_ref, bf16[512,1024]{1,0:T(8,128)(2,1)} %get-tuple-element.118.refs_16_.lg_ref, ...), custom_call_target="tpu_custom_call" | custom-call | flops 8589934592 | bytes 8388608 | tf_op jit(solution)/shard_map/weigh/pallas_call | solution.py:735
  219.9 11.9 %all-to-all-done.refs_0_.dot_ref.delta_ref = bf16[4,272,512]{2,1,0:T(8,128)(2,1)S(1)} async-done(((bf16[4,272,512]{2,1,0:T(8,128)(2,1)}), bf16[4,272,512]{2,1,0:T(8,128)(2,1)S(1)}, u32[]{:S(2)}, u32[]{:S(2)}) %all-to-all-start) | async-done | bytes 1114144 | tf_op jit(solution)/shard_map/all_to_all | solution.py:925
  232.8 10.9 %weigh.2.refs_0_ = bf16[8,2,304,1024]{3,2,1,0:T(8,128)(2,1)} custom-call(bf16[512,1024]{1,0:T(8,128)(2,1)} %get-tuple-element.134.first_ref, bf16[4,512,1024]{2,1,0:T(8,128)(2,1)} %get-tuple-element.135.act_ref, bf16[4,512,1024]{2,1,0:T(8,128)(2,1)} %get-tuple-element.136.ug_ref, bf16[512,1024]{1,0:T(8,128)(2,1)} %get-tuple-element.118.refs_16_.lg_ref, ...), custom_call_target="tpu_custom_call" | custom-call | flops 8589934592 | bytes 8388608 | tf_op jit(solution)/shard_map/weigh/pallas_call | solution.py:735
  247.2 19.2 %attend_back.4 = (bf16[64,2048]{1,0:T(8,128)(2,1)}, bf16[64,2048]{1,0:T(8,128)(2,1)}, bf16[64,2048]{1,0:T(8,128)(2,1)}, bf16[4,192,512]{2,1,0:T(8,128)(2,1)}) custom-call(s32[2]{0:T(128)} %pad_add_fusion.me_ref, bf16[4,128,2048]{2,1,0:T(8,128)(2,1)} %get-tuple-element.97.qt_ref, bf16[4,64,2048]{2,1,0:T(8,128)(2,1)} %get-tuple-element.126.kt_ref, ...), custom_call_target="tpu_custom_call" | custom-call | flops 21474836480 | bytes 2097152 | tf_op jit(solution)/shard_map/attend_back/pallas_call | solution.py:378
  266.5 5.8 %all-to-all-start.1 = ((bf16[4,192,512]{2,1,0:T(8,128)(2,1)}), bf16[4,192,512]{2,1,0:T(8,128)(2,1)S(1)}, u32[]{:S(2)}, u32[]{:S(2)}) async-start(bf16[4,192,512]{2,1,0:T(8,128)(2,1)} %get-tuple-element.149), calls=%async_computation.1 | async-start | bytes 1572864 | tf_op jit(solution)/shard_map/all_to_all | solution.py:925
  275.2 19.0 %attend_back.5 = (bf16[64,2048]{1,0:T(8,128)(2,1)}, bf16[64,2048]{1,0:T(8,128)(2,1)}, bf16[64,2048]{1,0:T(8,128)(2,1)}, bf16[4,192,512]{2,1,0:T(8,128)(2,1)}) custom-call(s32[2]{0:T(128)} %pad_add_fusion.me_ref, bf16[4,128,2048]{2,1,0:T(8,128)(2,1)} %get-tuple-element.97.qt_ref, bf16[4,64,2048]{2,1,0:T(8,128)(2,1)} %get-tuple-element.126.kt_ref, ...), custom_call_target="tpu_custom_call" | custom-call | flops 21474836480 | bytes 2097152 | tf_op jit(solution)/shard_map/attend_back/pallas_call | solution.py:378
  294.3 7.2 %all-to-all-start.2 = ((bf16[4,192,512]{2,1,0:T(8,128)(2,1)}), bf16[4,192,512]{2,1,0:T(8,128)(2,1)S(1)}, u32[]{:S(2)}, u32[]{:S(2)}) async-start(bf16[4,192,512]{2,1,0:T(8,128)(2,1)} %get-tuple-element.160), calls=%async_computation.3 | async-start | bytes 1572864 | tf_op jit(solution)/shard_map/all_to_all | solution.py:925
  301.5 14.6 %collective-permute-done.23.refs_5_.refs_1_ = bf16[512,1024]{1,0:T(8,128)(2,1)} collective-permute-done((bf16[512,1024]{1,0:T(8,128)(2,1)}, bf16[512,1024]{1,0:T(8,128)(2,1)}, u32[]{:S(2)}, u32[]{:S(2)}) %collective-permute-start.23) | collective-permute-done | bytes 1048608 | tf_op jit(solution)/shard_map/ppermute | solution.py:936
  316.1 5.9 %reduce-scatter.3.cloned.1.call-done = bf16[1,2,304,1024]{3,2,1,0:T(8,128)(2,1)} async-done(((bf16[8,2,304,1024]{3,2,1,0:T(8,128)(2,1)}), bf16[1,2,304,1024]{3,2,1,0:T(8,128)(2,1)}) %reduce-scatter.3.cloned.1.call-update) | async-done | bytes 1245200 | tf_op jit(solution)/shard_map/reduce_scatter | solution.py:1104
  323.5 18.9 %attend_back.6 = (bf16[64,2048]{1,0:T(8,128)(2,1)}, bf16[64,2048]{1,0:T(8,128)(2,1)}, bf16[64,2048]{1,0:T(8,128)(2,1)}, bf16[4,192,512]{2,1,0:T(8,128)(2,1)}) custom-call(s32[2]{0:T(128)} %pad_add_fusion.me_ref, bf16[4,128,2048]{2,1,0:T(8,128)(2,1)} %get-tuple-element.97.qt_ref, bf16[4,64,2048]{2,1,0:T(8,128)(2,1)} %get-tuple-element.126.kt_ref, ...), custom_call_target="tpu_custom_call" | custom-call | flops 21474836480 | bytes 2097152 | tf_op jit(solution)/shard_map/attend_back/pallas_call | solution.py:378
  342.4 3.7 all-to-all-start.3
  346.0 8.5 %collective-permute-done.27.refs_0_ = bf16[2,304,1024]{2,1,0:T(8,128)(2,1)S(1)} collective-permute-done((bf16[2,304,1024]{2,1,0:T(8,128)(2,1)}, bf16[2,304,1024]{2,1,0:T(8,128)(2,1)S(1)}, u32[]{:S(2)}, u32[]{:S(2)}) %collective-permute-start.27) | collective-permute-done | bytes 1245216 | tf_op jit(solution)/shard_map/ppermute | solution.py:917
  355.5 18.9 %attend_back.7 = (bf16[64,2048]{1,0:T(8,128)(2,1)}, bf16[64,2048]{1,0:T(8,128)(2,1)}, bf16[64,2048]{1,0:T(8,128)(2,1)}, bf16[4,192,512]{2,1,0:T(8,128)(2,1)}) custom-call(s32[2]{0:T(128)} %pad_add_fusion.me_ref, bf16[4,128,2048]{2,1,0:T(8,128)(2,1)} %get-tuple-element.97.qt_ref, bf16[4,64,2048]{2,1,0:T(8,128)(2,1)} %get-tuple-element.126.kt_ref, ...), custom_call_target="tpu_custom_call" | custom-call | flops 21474836480 | bytes 2097152 | tf_op jit(solution)/shard_map/attend_back/pallas_call | solution.py:378
  374.5 10.7 %all-to-all-start.4 = ((bf16[4,192,512]{2,1,0:T(8,128)(2,1)}), bf16[4,192,512]{2,1,0:T(8,128)(2,1)S(1)}, u32[]{:S(2)}, u32[]{:S(2)}) async-start(bf16[4,192,512]{2,1,0:T(8,128)(2,1)} %get-tuple-element.168), calls=%async_computation.5 | async-start | bytes 1572864 | tf_op jit(solution)/shard_map/all_to_all | solution.py:925
  385.4 8.8 %weigh_input.1 = bf16[3,1040,256]{2,1,0:T(8,128)(2,1)} custom-call(bf16[2048,1024]{1,0:T(8,128)(2,1)} %hidden_ref.5, bf16[64,2048]{1,0:T(8,128)(2,1)} %get-tuple-element.138.refs_0_, bf16[64,2048]{1,0:T(8,128)(2,1)} %get-tuple-element.145.refs_1_, bf16[64,2048]{1,0:T(8,128)(2,1)} %get-tuple-element.146.refs_2_, bf16[64,2048]{1,0:T(8,128)(2,1)} %get-tuple-element.141.refs_3_, ...), custom_call_target="tpu_custom_call" | custom-call | flops 3221225472 | bytes 16777216 | tf_op jit(solution)/shard_map/weigh_input/pallas_call | solution.py:874
  394.2 9.9 %input_gradient.2.back_ref = f32[512,1024]{1,0:T(8,128)} custom-call(s32[2]{0:T(128)} %pad_add_fusion.me_ref, f32[512,1024]{1,0:T(8,128)} %get-tuple-element.164.back_ref, bf16[768,1024]{1,0:T(8,128)(2,1)} %get-tuple-element.153.own_ref, bf16[8,3,96,1024]{3,2,1,0:T(8,128)(2,1)} %bitcast.57, bf16[4,192,512]{2,1,0:T(8,128)(2,1)} %copy-done, ...), custom_call_target="tpu_custom_call" | custom-call | flops 3221225472 | bytes 6291456 | tf_op jit(solution)/shard_map/input_gradient/pallas_call | solution.py:795
  404.5 2.4 add_convert_fusion
  406.9 2.7 collective-permute-start.34
  409.6 6.0 %input_gradient.3.own_ref = bf16[512,1024]{1,0:T(8,128)(2,1)} custom-call(s32[2]{0:T(128)} %pad_add_fusion.me_ref, f32[512,1024]{1,0:T(8,128)} %input_gradient.2.back_ref, bf16[768,1024]{1,0:T(8,128)(2,1)} %get-tuple-element.153.own_ref, bf16[8,3,96,1024]{3,2,1,0:T(8,128)(2,1)} %bitcast.58, bf16[4,192,512]{2,1,0:T(8,128)(2,1)} %copy-done.17), custom_call_target="tpu_custom_call" | custom-call | flops 3221225472 | bytes 6291456 | tf_op jit(solution)/shard_map/input_gradient/pallas_call | solution.py:795
  417.0 5.6 %collective-permute-start.28 = (bf16[512,1024]{1,0:T(8,128)(2,1)}, bf16[512,1024]{1,0:T(8,128)(2,1)}, u32[]{:S(2)}, u32[]{:S(2)}) collective-permute-start(bf16[512,1024]{1,0:T(8,128)(2,1)} %input_gradient.3.own_ref), channel_id=1, source_target_pairs={{0,1},{1,2},{2,3},{4,5},{5,6},{6,7},{8,9},{9,10},{10,11},{12,13},{... | collective-permute-start | bytes 3145736 | tf_op jit(solution)/shard_map/ppermute | solution.py:935
  422.7 15.5 %collective-permute-done.34 = bf16[1,304,1024]{2,1,0:T(8,128)(2,1)S(1)} collective-permute-done((bf16[1,304,1024]{2,1,0:T(8,128)(2,1)}, bf16[1,304,1024]{2,1,0:T(8,128)(2,1)S(1)}, u32[]{:S(2)}, u32[]{:S(2)}) %collective-permute-start.34) | collective-permute-done | bytes 622624 | tf_op jit(solution)/shard_map/ppermute | solution.py:917
  440.5 14.1 %collective-permute-done.30.refs_3_ = bf16[512,1024]{1,0:T(8,128)(2,1)} collective-permute-done((bf16[512,1024]{1,0:T(8,128)(2,1)}, bf16[512,1024]{1,0:T(8,128)(2,1)}, u32[]{:S(2)}, u32[]{:S(2)}) %collective-permute-start.30) | collective-permute-done | bytes 1048608 | tf_op jit(solution)/shard_map/ppermute | solution.py:936
  455.9 1.7 collective-permute-start.29
  457.6 21.5 %all-reduce.2.cloned.1.call-done = bf16[3,1040,256]{2,1,0:T(8,128)(2,1)} async-done(((bf16[3,1040,256]{2,1,0:T(8,128)(2,1)}), bf16[3,1040,256]{2,1,0:T(8,128)(2,1)}) %all-reduce.2.cloned.1.call-update) | async-done | bytes 1597456 | tf_op jit(solution)/shard_map/psum | solution.py:1142
  479.1 6.7 %collective-permute-done.31.refs_4_ = bf16[512,1024]{1,0:T(8,128)(2,1)} collective-permute-done((bf16[512,1024]{1,0:T(8,128)(2,1)}, bf16[512,1024]{1,0:T(8,128)(2,1)}, u32[]{:S(2)}, u32[]{:S(2)}) %collective-permute-start.31) | collective-permute-done | bytes 1048608 | tf_op jit(solution)/shard_map/ppermute | solution.py:936
  488.7 4.0 join_line.2
  493.5 1.7 slice_bitcast_fusion
  495.9 19.3 %collective-permute-done.33.refs_5_ = bf16[512,1024]{1,0:T(8,128)(2,1)} collective-permute-done((bf16[512,1024]{1,0:T(8,128)(2,1)}, bf16[512,1024]{1,0:T(8,128)(2,1)}, u32[]{:S(2)}, u32[]{:S(2)}) %collective-permute-start.33) | collective-permute-done | bytes 1048608 | tf_op jit(solution)/shard_map/ppermute | solution.py:936
  515.2 4.0 join_line.3
  519.9 7.5 %unpack.1 = (f32[256,1024]{1,0:T(8,128)}, f32[1024,1024]{1,0:T(8,128)}, f32[1024,1024]{1,0:T(8,128)}) custom-call(bf16[8,288,1024]{2,1,0:T(8,128)(2,1)} %bitcast.59), custom_call_target="tpu_custom_call" | custom-call | tf_op jit(solution)/shard_map/unpack/pallas_call | solution.py:897
  (170 shorter events, 52.3 us)
Async XLA Ops:
  7.2 236.5 %all-gather.5.cloned.1.call-start = ((), (), s32[]{:S(2)}) async-start(), calls=%async_computation.10 | async-start | bytes 5308416 | tf_op jit(solution)/shard_map/all_gather | solution.py:985
  10.5 31.1 %collective-permute-start.1 = (bf16[592,512]{1,0:T(8,128)(2,1)}, bf16[592,512]{1,0:T(8,128)(2,1)S(1)}, u32[]{:S(2)}, u32[]{:S(2)}) collective-permute-start(bf16[592,512]{1,0:T(8,128)(2,1)} %pack.1), channel_id=1, source_target_pairs={{0,2},{1,3},{2,0},{3,1},{4,6},{5,7},{6,4},{7,5},{8,10},{9,11},{10,... | collective-permute-start | bytes 1818632 | tf_op jit(solution)/shard_map/ppermute | solution.py:917
  14.6 27.2 %collective-permute-start = (bf16[592,512]{1,0:T(8,128)(2,1)}, bf16[592,512]{1,0:T(8,128)(2,1)S(1)}, u32[]{:S(2)}, u32[]{:S(2)}) collective-permute-start(bf16[592,512]{1,0:T(8,128)(2,1)} %pack.1), channel_id=1, source_target_pairs={{0,1},{1,0},{2,3},{3,2},{4,5},{5,4},{6,7},{7,6},{8,9},{9,8},{10,11... | collective-permute-start | bytes 1818632 | tf_op jit(solution)/shard_map/ppermute | solution.py:917
  42.8 24.1 %collective-permute-start.3 = (bf16[1,2,320,512]{3,2,1,0:T(8,128)(2,1)S(1)}, bf16[1,2,320,512]{3,2,1,0:T(8,128)(2,1)S(1)}, u32[]{:S(2)}, u32[]{:S(2)}) collective-permute-start(bf16[1,2,320,512]{3,2,1,0:T(8,128)(2,1)S(1)} %slice.187), channel_id=1, source_target_pairs={{0,16},{4,20},{8,24},{12,28},{16,0},{20,4},{24,8},{28,12},{1,17},{... | collective-permute-start | bytes 1966088 | tf_op jit(solution)/shard_map/ppermute | solution.py:929
  44.5 22.4 %collective-permute-start.4 = (bf16[592,512]{1,0:T(8,128)(2,1)S(1)}, bf16[592,512]{1,0:T(8,128)(2,1)S(1)}, u32[]{:S(2)}, u32[]{:S(2)}) collective-permute-start(bf16[592,512]{1,0:T(8,128)(2,1)S(1)} %collective-permute-done.1), channel_id=1, source_target_pairs={{0,1},{1,0},{2,3},{3,2},{4,5},{5,4},{6,7},{7,6},{8,9},{9,8},{10,11... | collective-permute-start | bytes 1818632 | tf_op jit(solution)/shard_map/ppermute | solution.py:917
  45.9 21.0 %collective-permute-start.2 = (bf16[1,2,256,512]{3,2,1,0:T(8,128)(2,1)S(1)}, bf16[1,2,256,512]{3,2,1,0:T(8,128)(2,1)S(1)}, u32[]{:S(2)}, u32[]{:S(2)}) collective-permute-start(bf16[1,2,256,512]{3,2,1,0:T(8,128)(2,1)S(1)} %slice.186), channel_id=1, source_target_pairs={{0,8},{4,12},{8,0},{12,4},{16,24},{20,28},{24,16},{28,20},{1,9},{5... | collective-permute-start | bytes 1572872 | tf_op jit(solution)/shard_map/ppermute | solution.py:929
  47.5 19.4 %collective-permute-start.5 = (bf16[256,512]{1,0:T(8,128)(2,1)}, bf16[256,512]{1,0:T(8,128)(2,1)S(1)}, u32[]{:S(2)}, u32[]{:S(2)}) collective-permute-start(bf16[256,512]{1,0:T(8,128)(2,1)} %bitcast.9), channel_id=1, source_target_pairs={{0,3},{1,2},{2,1},{3,0},{4,7},{5,6},{6,5},{7,4},{8,11},{9,10},{10,... | collective-permute-start | bytes 786440 | tf_op jit(solution)/shard_map/ppermute | solution.py:917
  68.2 35.7 %collective-permute-start.8 = (bf16[2,2,320,512]{3,2,1,0:T(8,128)(2,1)}, bf16[2,2,320,512]{3,2,1,0:T(8,128)(2,1)}, u32[]{:S(2)}, u32[]{:S(2)}) collective-permute-start(bf16[2,2,320,512]{3,2,1,0:T(8,128)(2,1)} %pad_maximum_fusion.2.refs_2_), channel_id=1, source_target_pairs={{0,8},{4,12},{8,0},{12,4},{16,24},{20,28},{24,16},{28,20},{1,9},{5... | collective-permute-start | bytes 3932168 | tf_op jit(solution)/shard_map/ppermute | solution.py:929
  70.8 33.1 %collective-permute-start.7 = (bf16[2,2,256,512]{3,2,1,0:T(8,128)(2,1)}, bf16[2,2,256,512]{3,2,1,0:T(8,128)(2,1)}, u32[]{:S(2)}, u32[]{:S(2)}) collective-permute-start(bf16[2,2,256,512]{3,2,1,0:T(8,128)(2,1)} %pad_maximum_fusion.4.refs_1_), channel_id=1, source_target_pairs={{0,16},{4,20},{8,24},{12,28},{16,0},{20,4},{24,8},{28,12},{1,17},{... | collective-permute-start | bytes 3145736 | tf_op jit(solution)/shard_map/ppermute | solution.py:929
  71.3 25.5 %collective-permute-start.11 = (bf16[256,512]{1,0:T(8,128)(2,1)}, bf16[256,512]{1,0:T(8,128)(2,1)S(1)}, u32[]{:S(2)}, u32[]{:S(2)}) collective-permute-start(bf16[256,512]{1,0:T(8,128)(2,1)} %bitcast.13), channel_id=1, source_target_pairs={{0,2},{1,3},{2,0},{3,1},{4,6},{5,7},{6,4},{7,5},{8,10},{9,11},{10,... | collective-permute-start | bytes 786440 | tf_op jit(solution)/shard_map/ppermute | solution.py:917
  71.4 32.5 %collective-permute-start.9 = (bf16[1,1,256,512]{3,2,1,0:T(8,128)(2,1)S(1)}, bf16[1,1,256,512]{3,2,1,0:T(8,128)(2,1)S(1)}, u32[]{:S(2)}, u32[]{:S(2)}) collective-permute-start(bf16[1,1,256,512]{3,2,1,0:T(8,128)(2,1)S(1)} %slice.188.refs_3_), channel_id=1, source_target_pairs={{0,8},{4,12},{8,0},{12,4},{16,24},{20,28},{24,16},{28,20},{1,9},{5... | collective-permute-start | bytes 786440 | tf_op jit(solution)/shard_map/ppermute | solution.py:929
  72.0 31.9 %collective-permute-start.10 = (bf16[1,1,320,512]{3,2,1,0:T(8,128)(2,1)S(1)}, bf16[1,1,320,512]{3,2,1,0:T(8,128)(2,1)S(1)}, u32[]{:S(2)}, u32[]{:S(2)}) collective-permute-start(bf16[1,1,320,512]{3,2,1,0:T(8,128)(2,1)S(1)} %slice.189.refs_4_), channel_id=1, source_target_pairs={{0,16},{4,20},{8,24},{12,28},{16,0},{20,4},{24,8},{28,12},{1,17},{... | collective-permute-start | bytes 983048 | tf_op jit(solution)/shard_map/ppermute | solution.py:929
  107.1 28.6 %collective-permute-start.13 = (bf16[4,2,320,512]{3,2,1,0:T(8,128)(2,1)}, bf16[4,2,320,512]{3,2,1,0:T(8,128)(2,1)}, u32[]{:S(2)}, u32[]{:S(2)}) collective-permute-start(bf16[4,2,320,512]{3,2,1,0:T(8,128)(2,1)} %pad_maximum_fusion.refs_8_), channel_id=1, source_target_pairs={{0,4},{4,0},{8,12},{12,8},{16,20},{20,16},{24,28},{28,24},{1,5},{5... | collective-permute-start | bytes 7864328 | tf_op jit(solution)/shard_map/ppermute | solution.py:929
  107.2 14.4 %collective-permute-start.14 = (bf16[2,1,256,512]{3,2,1,0:T(8,128)(2,1)S(1)}, bf16[2,1,256,512]{3,2,1,0:T(8,128)(2,1)S(1)}, u32[]{:S(2)}, u32[]{:S(2)}) collective-permute-start(bf16[2,1,256,512]{3,2,1,0:T(8,128)(2,1)S(1)} %pad_maximum_fusion.9), channel_id=1, source_target_pairs={{0,16},{4,20},{8,24},{12,28},{16,0},{20,4},{24,8},{28,12},{1,17},{... | collective-permute-start | bytes 1572872 | tf_op jit(solution)/shard_map/ppermute | solution.py:929
  107.8 16.9 %collective-permute-start.15 = (bf16[2,1,320,512]{3,2,1,0:T(8,128)(2,1)S(1)}, bf16[2,1,320,512]{3,2,1,0:T(8,128)(2,1)S(1)}, u32[]{:S(2)}, u32[]{:S(2)}) collective-permute-start(bf16[2,1,320,512]{3,2,1,0:T(8,128)(2,1)S(1)} %pad_maximum_fusion.7), channel_id=1, source_target_pairs={{0,8},{4,12},{8,0},{12,4},{16,24},{20,28},{24,16},{28,20},{1,9},{5... | collective-permute-start | bytes 1966088 | tf_op jit(solution)/shard_map/ppermute | solution.py:929
  110.8 24.9 %collective-permute-start.12 = (bf16[4,2,256,512]{3,2,1,0:T(8,128)(2,1)S(1)}, bf16[4,2,256,512]{3,2,1,0:T(8,128)(2,1)}, u32[]{:S(2)}, u32[]{:S(2)}) collective-permute-start(bf16[4,2,256,512]{3,2,1,0:T(8,128)(2,1)S(1)} %pad_maximum_fusion.1.refs_7_), channel_id=1, source_target_pairs={{0,4},{4,0},{8,12},{12,8},{16,20},{20,16},{24,28},{28,24},{1,5},{5... | collective-permute-start | bytes 6291464 | tf_op jit(solution)/shard_map/ppermute | solution.py:929
  111.8 14.2 %collective-permute-start.6 = (bf16[256,512]{1,0:T(8,128)(2,1)S(1)}, bf16[256,512]{1,0:T(8,128)(2,1)S(1)}, u32[]{:S(2)}, u32[]{:S(2)}) collective-permute-start(bf16[256,512]{1,0:T(8,128)(2,1)S(1)} %get-tuple-element.199), channel_id=1, source_target_pairs={{0,1},{1,0},{2,3},{3,2},{4,5},{5,4},{6,7},{7,6},{8,9},{9,8},{10,11... | collective-permute-start | bytes 786440 | tf_op jit(solution)/shard_map/ppermute | solution.py:917
  126.0 5.3 collective-permute-start.17
  126.0 5.3 collective-permute-start.16
  127.4 43.1 %collective-permute-start.26 = (bf16[96,1024]{1,0:T(8,128)(2,1)S(1)}, bf16[96,1024]{1,0:T(8,128)(2,1)S(1)}, u32[]{:S(2)}, u32[]{:S(2)}) collective-permute-start(bf16[96,1024]{1,0:T(8,128)(2,1)S(1)} %constant_dynamic-slice_fusion), channel_id=1, source_target_pairs={{0,3},{1,2},{2,1},{3,0},{4,7},{5,6},{6,5},{7,4},{8,11},{9,10},{10,... | collective-permute-start | bytes 589832 | tf_op jit(solution)/shard_map/ppermute | solution.py:917
  131.3 39.2 %collective-permute-start.25 = (bf16[96,1024]{1,0:T(8,128)(2,1)S(1)}, bf16[96,1024]{1,0:T(8,128)(2,1)S(1)}, u32[]{:S(2)}, u32[]{:S(2)}) collective-permute-start(bf16[96,1024]{1,0:T(8,128)(2,1)S(1)} %constant_dynamic-slice_fusion), channel_id=1, source_target_pairs={{0,2},{1,3},{2,0},{3,1},{4,6},{5,7},{6,4},{7,5},{8,10},{9,11},{10,... | collective-permute-start | bytes 589832 | tf_op jit(solution)/shard_map/ppermute | solution.py:917
  131.3 39.2 %collective-permute-start.24 = (bf16[96,1024]{1,0:T(8,128)(2,1)S(1)}, bf16[96,1024]{1,0:T(8,128)(2,1)S(1)}, u32[]{:S(2)}, u32[]{:S(2)}) collective-permute-start(bf16[96,1024]{1,0:T(8,128)(2,1)S(1)} %constant_dynamic-slice_fusion), channel_id=1, source_target_pairs={{0,1},{1,0},{2,3},{3,2},{4,5},{5,4},{6,7},{7,6},{8,9},{9,8},{10,11... | collective-permute-start | bytes 589832 | tf_op jit(solution)/shard_map/ppermute | solution.py:917
  172.0 36.0 %collective-permute-start.19 = (bf16[512,1024]{1,0:T(8,128)(2,1)S(1)}, bf16[512,1024]{1,0:T(8,128)(2,1)S(1)}, u32[]{:S(2)}, u32[]{:S(2)}) collective-permute-start(bf16[512,1024]{1,0:T(8,128)(2,1)S(1)} %copy-done.13), channel_id=1, source_target_pairs={{1,0},{2,1},{3,2},{5,4},{6,5},{7,6},{9,8},{10,9},{11,10},{13,12},{... | collective-permute-start | bytes 3145736 | tf_op jit(solution)/shard_map/ppermute | solution.py:936
  173.3 34.7 %collective-permute-start.18 = (bf16[512,1024]{1,0:T(8,128)(2,1)S(1)}, bf16[512,1024]{1,0:T(8,128)(2,1)}, u32[]{:S(2)}, u32[]{:S(2)}) collective-permute-start(bf16[512,1024]{1,0:T(8,128)(2,1)S(1)} %copy-done.13), channel_id=1, source_target_pairs={{0,1},{1,2},{2,3},{4,5},{5,6},{6,7},{8,9},{9,10},{10,11},{12,13},{... | collective-permute-start | bytes 3145736 | tf_op jit(solution)/shard_map/ppermute | solution.py:935
  201.9 29.9 %all-to-all-start = ((bf16[4,272,512]{2,1,0:T(8,128)(2,1)}), bf16[4,272,512]{2,1,0:T(8,128)(2,1)S(1)}, u32[]{:S(2)}, u32[]{:S(2)}) async-start(bf16[4,272,512]{2,1,0:T(8,128)(2,1)} %get-tuple-element.128), calls=%async_computation | async-start | bytes 2228224 | tf_op jit(solution)/shard_map/all_to_all | solution.py:925
  205.5 116.5 %reduce-scatter.3.cloned.1.call-start = ((), (), s32[]{:S(2)}) async-start(), calls=%async_computation.7 | async-start | bytes 11206656 | tf_op jit(solution)/shard_map/reduce_scatter | solution.py:1104
  243.8 160.7 %reduce-scatter.5.cloned.1.call-start = ((), (), s32[]{:S(2)}) async-start(), calls=%async_computation.9 | async-start | bytes 11206656 | tf_op jit(solution)/shard_map/reduce_scatter | solution.py:1105
  245.2 27.0 %collective-permute-start.20 = (bf16[512,1024]{1,0:T(8,128)(2,1)}, bf16[512,1024]{1,0:T(8,128)(2,1)S(1)}, u32[]{:S(2)}, u32[]{:S(2)}) collective-permute-start(bf16[512,1024]{1,0:T(8,128)(2,1)} %collective-permute-done.18.refs_1_.refs_0_), channel_id=1, source_target_pairs={{1,2},{2,3},{5,6},{6,7},{9,10},{10,11},{13,14},{14,15},{17,18},{18... | collective-permute-start | bytes 3145736 | tf_op jit(solution)/shard_map/ppermute | solution.py:935
  245.9 26.3 %collective-permute-start.21 = (bf16[512,1024]{1,0:T(8,128)(2,1)S(1)}, bf16[512,1024]{1,0:T(8,128)(2,1)}, u32[]{:S(2)}, u32[]{:S(2)}) collective-permute-start(bf16[512,1024]{1,0:T(8,128)(2,1)S(1)} %copy-done.15), channel_id=1, source_target_pairs={{1,0},{2,1},{5,4},{6,5},{9,8},{10,9},{13,12},{14,13},{17,16},{18,1... | collective-permute-start | bytes 3145736 | tf_op jit(solution)/shard_map/ppermute | solution.py:936
  266.5 27.8 %all-to-all-start.1 = ((bf16[4,192,512]{2,1,0:T(8,128)(2,1)}), bf16[4,192,512]{2,1,0:T(8,128)(2,1)S(1)}, u32[]{:S(2)}, u32[]{:S(2)}) async-start(bf16[4,192,512]{2,1,0:T(8,128)(2,1)} %get-tuple-element.149), calls=%async_computation.1 | async-start | bytes 1572864 | tf_op jit(solution)/shard_map/all_to_all | solution.py:925
  272.2 29.2 %collective-permute-start.22 = (bf16[512,1024]{1,0:T(8,128)(2,1)S(1)}, bf16[512,1024]{1,0:T(8,128)(2,1)}, u32[]{:S(2)}, u32[]{:S(2)}) collective-permute-start(bf16[512,1024]{1,0:T(8,128)(2,1)S(1)} %collective-permute-done.20.refs_0_.refs_1_), channel_id=1, source_target_pairs={{2,3},{6,7},{10,11},{14,15},{18,19},{22,23},{26,27},{30,31}} | collective-permute-start | bytes 3145736 | tf_op jit(solution)/shard_map/ppermute | solution.py:935
  273.9 42.1 %collective-permute-start.23 = (bf16[512,1024]{1,0:T(8,128)(2,1)}, bf16[512,1024]{1,0:T(8,128)(2,1)}, u32[]{:S(2)}, u32[]{:S(2)}) collective-permute-start(bf16[512,1024]{1,0:T(8,128)(2,1)} %collective-permute-done.21.refs_1_.refs_4_), channel_id=1, source_target_pairs={{1,0},{5,4},{9,8},{13,12},{17,16},{21,20},{25,24},{29,28}} | collective-permute-start | bytes 3145736 | tf_op jit(solution)/shard_map/ppermute | solution.py:936
  294.3 29.2 %copy-start = (bf16[4,192,512]{2,1,0:T(8,128)(2,1)}, bf16[4,192,512]{2,1,0:T(8,128)(2,1)S(1)}, u32[]{:S(2)}) copy-start(bf16[4,192,512]{2,1,0:T(8,128)(2,1)S(1)} %all-to-all-done.1.refs_2_.refs_0_) | copy-start | bytes 2359300
  294.3 48.0 %all-to-all-start.2 = ((bf16[4,192,512]{2,1,0:T(8,128)(2,1)}), bf16[4,192,512]{2,1,0:T(8,128)(2,1)S(1)}, u32[]{:S(2)}, u32[]{:S(2)}) async-start(bf16[4,192,512]{2,1,0:T(8,128)(2,1)} %get-tuple-element.160), calls=%async_computation.3 | async-start | bytes 1572864 | tf_op jit(solution)/shard_map/all_to_all | solution.py:925
  322.0 32.5 %collective-permute-start.27 = (bf16[2,304,1024]{2,1,0:T(8,128)(2,1)}, bf16[2,304,1024]{2,1,0:T(8,128)(2,1)S(1)}, u32[]{:S(2)}, u32[]{:S(2)}) collective-permute-start(bf16[2,304,1024]{2,1,0:T(8,128)(2,1)} %bitcast.96), channel_id=1, source_target_pairs={{0,1},{1,0},{2,3},{3,2},{4,5},{5,4},{6,7},{7,6},{8,9},{9,8},{10,11... | collective-permute-start | bytes 3735560 | tf_op jit(solution)/shard_map/ppermute | solution.py:917
  342.4 32.1 %all-to-all-start.3 = ((bf16[4,192,512]{2,1,0:T(8,128)(2,1)}), bf16[4,192,512]{2,1,0:T(8,128)(2,1)S(1)}, u32[]{:S(2)}, u32[]{:S(2)}) async-start(bf16[4,192,512]{2,1,0:T(8,128)(2,1)} %get-tuple-element.166), calls=%async_computation.4 | async-start | bytes 1572864 | tf_op jit(solution)/shard_map/all_to_all | solution.py:925
  374.5 19.8 %copy-start.2 = (bf16[4,192,512]{2,1,0:T(8,128)(2,1)}, bf16[4,192,512]{2,1,0:T(8,128)(2,1)S(1)}, u32[]{:S(2)}) copy-start(bf16[4,192,512]{2,1,0:T(8,128)(2,1)S(1)} %all-to-all-done.3.refs_2_) | copy-start | bytes 2359300
  374.5 30.0 %all-to-all-start.4 = ((bf16[4,192,512]{2,1,0:T(8,128)(2,1)}), bf16[4,192,512]{2,1,0:T(8,128)(2,1)S(1)}, u32[]{:S(2)}, u32[]{:S(2)}) async-start(bf16[4,192,512]{2,1,0:T(8,128)(2,1)} %get-tuple-element.168), calls=%async_computation.5 | async-start | bytes 1572864 | tf_op jit(solution)/shard_map/all_to_all | solution.py:925
  385.1 94.0 %all-reduce.2.cloned.1.call-start = ((), (), s32[]{:S(2)}) async-start(), calls=%async_computation.8 | async-start | bytes 3194880 | tf_op jit(solution)/shard_map/psum | solution.py:1142
  406.9 31.3 %collective-permute-start.34 = (bf16[1,304,1024]{2,1,0:T(8,128)(2,1)}, bf16[1,304,1024]{2,1,0:T(8,128)(2,1)S(1)}, u32[]{:S(2)}, u32[]{:S(2)}) collective-permute-start(bf16[1,304,1024]{2,1,0:T(8,128)(2,1)} %add_convert_fusion), channel_id=1, source_target_pairs={{0,2},{1,3},{2,0},{3,1},{4,6},{5,7},{6,4},{7,5},{8,10},{9,11},{10,... | collective-permute-start | bytes 1867784 | tf_op jit(solution)/shard_map/ppermute | solution.py:917
  415.6 22.6 %copy-start.9 = (bf16[1,2,304,1024]{3,2,1,0:T(8,128)(2,1)S(1)}, bf16[1,2,304,1024]{3,2,1,0:T(8,128)(2,1)}, u32[]{:S(2)}) copy-start(bf16[1,2,304,1024]{3,2,1,0:T(8,128)(2,1)} %reduce-scatter.5.cloned.1.call-done) | copy-start | bytes 3735556
  415.6 39.0 %collective-permute-start.30 = (bf16[512,1024]{1,0:T(8,128)(2,1)}, bf16[512,1024]{1,0:T(8,128)(2,1)}, u32[]{:S(2)}, u32[]{:S(2)}) collective-permute-start(bf16[512,1024]{1,0:T(8,128)(2,1)} %input_gradient.3.own_ref), channel_id=1, source_target_pairs={{1,0},{2,1},{3,2},{5,4},{6,5},{7,6},{9,8},{10,9},{11,10},{13,12},{... | collective-permute-start | bytes 3145736 | tf_op jit(solution)/shard_map/ppermute | solution.py:936
  417.0 37.6 %collective-permute-start.28 = (bf16[512,1024]{1,0:T(8,128)(2,1)}, bf16[512,1024]{1,0:T(8,128)(2,1)}, u32[]{:S(2)}, u32[]{:S(2)}) collective-permute-start(bf16[512,1024]{1,0:T(8,128)(2,1)} %input_gradient.3.own_ref), channel_id=1, source_target_pairs={{0,1},{1,2},{2,3},{4,5},{5,6},{6,7},{8,9},{9,10},{10,11},{12,13},{... | collective-permute-start | bytes 3145736 | tf_op jit(solution)/shard_map/ppermute | solution.py:935
  422.6 97.3 %all-gather.7.cloned.1.call-start = ((), (), s32[]{:S(2)}) async-start(), calls=%async_computation.11 | async-start | bytes 5308416 | tf_op jit(solution)/shard_map/all_gather | solution.py:985
  454.6 31.2 %collective-permute-start.31 = (bf16[512,1024]{1,0:T(8,128)(2,1)}, bf16[512,1024]{1,0:T(8,128)(2,1)}, u32[]{:S(2)}, u32[]{:S(2)}) collective-permute-start(bf16[512,1024]{1,0:T(8,128)(2,1)} %collective-permute-done.30.refs_3_), channel_id=1, source_target_pairs={{1,0},{2,1},{5,4},{6,5},{9,8},{10,9},{13,12},{14,13},{17,16},{18,1... | collective-permute-start | bytes 3145736 | tf_op jit(solution)/shard_map/ppermute | solution.py:936
  455.9 29.9 %collective-permute-start.29 = (bf16[512,1024]{1,0:T(8,128)(2,1)}, bf16[512,1024]{1,0:T(8,128)(2,1)}, u32[]{:S(2)}, u32[]{:S(2)}) collective-permute-start(bf16[512,1024]{1,0:T(8,128)(2,1)} %collective-permute-done.28.refs_0_), channel_id=1, source_target_pairs={{1,2},{2,3},{5,6},{6,7},{9,10},{10,11},{13,14},{14,15},{17,18},{18... | collective-permute-start | bytes 3145736 | tf_op jit(solution)/shard_map/ppermute | solution.py:935
  485.8 10.1 %collective-permute-start.32 = (bf16[512,1024]{1,0:T(8,128)(2,1)}, bf16[512,1024]{1,0:T(8,128)(2,1)}, u32[]{:S(2)}, u32[]{:S(2)}) collective-permute-start(bf16[512,1024]{1,0:T(8,128)(2,1)} %collective-permute-done.29.refs_1_), channel_id=1, source_target_pairs={{2,3},{6,7},{10,11},{14,15},{18,19},{22,23},{26,27},{30,31}} | collective-permute-start | bytes 3145736 | tf_op jit(solution)/shard_map/ppermute | solution.py:935
  487.4 27.8 %collective-permute-start.33 = (bf16[512,1024]{1,0:T(8,128)(2,1)}, bf16[512,1024]{1,0:T(8,128)(2,1)}, u32[]{:S(2)}, u32[]{:S(2)}) collective-permute-start(bf16[512,1024]{1,0:T(8,128)(2,1)} %collective-permute-done.31.refs_4_), channel_id=1, source_target_pairs={{1,0},{5,4},{9,8},{13,12},{17,16},{21,20},{25,24},{29,28}} | collective-permute-start | bytes 3145736 | tf_op jit(solution)/shard_map/ppermute | solution.py:936
  (31 other events, 140.7 us)
Sparse Core Ops, SparseCore 0:
  171.6 37.1 all-gather.4
  243.9 78.0 reduce-scatter.2
  325.6 78.8 reduce-scatter.4
  422.8 56.3 all-reduce.1
  481.6 38.3 all-gather.6

commit v2 on v1

--- a/solution.py
+++ b/solution.py
@@ -502,7 +502,7 @@
     bias_ref, vectors_ref = take(2)
     (
         result_ref, first_low_ref, act_ref, slope_ref, lg_ref, normed_ref, inv_ref, back_ref,
-        vec_ref, out_s, up_s, down_s, first_s, sems,
+        vec_ref, out_s, up_s, down_s, first_s, act_s, slope_s, sems, out_sems,
     ) = refs
     depth, local = weights[1].shape
     own = hidden_ref.shape[0]
@@ -530,7 +530,7 @@
     first_s[...] = first
     first_low_ref[...] = first.astype(bf16)
 
-    lowered = None
+    lowered, stored = None, []
     for s in range(n_mp):
         run_all(copies[s][1:], "wait")
         for start in range(0, local, step):
@@ -538,10 +538,17 @@
             upper = nn(first_low_ref[...], up_s[s, :, part]) + bias_ref[s:s + 1, part]
             value, slope = gelu_parts(upper)
             act = value.astype(bf16)
-            act_ref[s, :, part] = act
-            slope_ref[s, :, part] = slope.astype(bf16)
+            act_s[s, :, part] = act
+            slope_s[s, :, part] = slope.astype(bf16)
             piece = nn(act, down_s[s, part, :])
             lowered = piece if lowered is None else lowered + piece
+        stored.append(
+            [
+                pltpu.make_async_copy(act_s.at[s], act_ref.at[s], out_sems.at[0, s]),
+                pltpu.make_async_copy(slope_s.at[s], slope_ref.at[s], out_sems.at[1, s]),
+            ]
+        )
+        run_all(stored[s:], "start")
 
     summed = first_s[...] + (lowered + down_bias)
     centered = summed - row_mean(summed)
@@ -557,6 +564,7 @@
     vec_ref[0:1] = column(low.astype(f32))
     vec_ref[1:2] = column(cotangent * normed)
     vec_ref[2:3] = column(cotangent)
+    run_all(stored, "wait")
 
 
 def feed_back_kernel(n_mp, packed, splits, me_ref, *refs):
@@ -566,7 +574,10 @@
     weights = take(3)
     banks = take(4 * (len(splits) - 1) if packed else 3)
     slope_ref, lg_ref, normed_ref, inv_ref, second_ref, some_ref, gain_ref = take(7)
-    ug_ref, ag_ref, back_ref, dctx_ref, vec_ref, out_s, up_s, down_s, sems = refs[-9:]
+    (
+        ug_ref, ag_ref, back_ref, dctx_ref, vec_ref, out_s, up_s, down_s, slope_s, ug_s,
+        normed_s, sems, more_sems,
+    ) = refs
     depth, local = weights[1].shape
     own = lg_ref.shape[0]
     width = weights[0].shape[0]
@@ -575,8 +586,18 @@
     copies = weight_copies(
         n_mp, packed, splits, me_ref, weights, banks, (out_s, up_s, down_s), sems
     )
+    slopes = [
+        pltpu.make_async_copy(slope_ref.at[s], slope_s.at[s], more_sems.at[0, s])
+        for s in range(n_mp)
+    ]
+    stored = [
+        pltpu.make_async_copy(ug_s.at[s], ug_ref.at[s], more_sems.at[1, s]) for s in range(n_mp)
+    ]
+    normed_copy = pltpu.make_async_copy(normed_ref, normed_s, more_sems.at[2, 0])
     for s in range(n_mp):
+        copies[s][2].append(slopes[s])
         run_all(copies[s][:0:-1], "start")
+    normed_copy.start()
     run_all([copies[s][0] for s in range(n_mp)], "start")
 
     first_grad = second_ref[...]
@@ -586,13 +607,15 @@
         sums = []
         for start in range(0, local, step):
             part = slice(start, start + step)
-            ug = (nt(lg_ref[...], down_s[s, part, :]) * slope_ref[s, :, part]).astype(bf16)
-            ug_ref[s, :, part] = ug
+            ug = (nt(lg_ref[...], down_s[s, part, :]) * slope_s[s, :, part]).astype(bf16)
+            ug_s[s, :, part] = ug
             sums.append(column(ug.astype(f32)))
             first_grad = first_grad + nt(ug, up_s[s, :, part])
         up_bias_grads.append(jnp.concatenate(sums, axis=1))
-
-    normed = normed_ref[...]
+        stored[s].start()
+
+    normed_copy.wait()
+    normed = normed_s[...]
     grad = first_grad * gain_ref[...]
     back = grad - row_mean(grad) - normed * row_mean(grad * normed)
     back = inv_ref[:, :1] * back
@@ -623,6 +646,7 @@
             piece = split_rows(delta, FEAT, own, 3 * h)
             rows = piece if rows is None else rows + piece
         dctx_ref[plane, width:] = rows.astype(bf16)
+    run_all([stored], "wait")
 
 
 def weight_scratch(n_mp, packed, width, depth, local):
@@ -651,8 +675,11 @@
             + [vmem] * n_mp
             + [hbm] * (3 + len(banks))
             + [vmem, vmem],
-            out_specs=[vmem] * 9,
-            scratch_shapes=scratch + [pltpu.VMEM((own, depth), f32), sems],
+            out_specs=[vmem] * 2 + [hbm] * 2 + [vmem] * 5,
+            scratch_shapes=scratch
+            + [pltpu.VMEM((own, depth), f32)]
+            + [pltpu.VMEM((n_mp, own, local), bf16)] * 2
+            + [sems, pltpu.SemaphoreType.DMA((2, n_mp))],
         ),
         out_shape=[
             shape((own, depth), bf16),
@@ -689,9 +716,14 @@
         grid_spec=pltpu.PrefetchScalarGridSpec(
             num_scalar_prefetch=1,
             grid=(1,),
-            in_specs=[vmem] * n_mp + [hbm] * (3 + len(banks)) + [vmem] * 7,
-            out_specs=[vmem] * 5,
-            scratch_shapes=scratch + [sems],
+            in_specs=[vmem] * n_mp
+            + [hbm] * (3 + len(banks))
+            + [hbm, vmem, hbm]
+            + [vmem] * 4,
+            out_specs=[hbm] + [vmem] * 4,
+            scratch_shapes=scratch
+            + [pltpu.VMEM((n_mp, own, local), bf16)] * 2
+            + [pltpu.VMEM((own, depth), f32), sems, pltpu.SemaphoreType.DMA((3, n_mp))],
         ),
         out_shape=[
             shape((n_mp, own, local), bf16),
@@ -1122,15 +1154,14 @@
         if len(hops) < n_mp - 1:
             came = tie(hop(hops[-1], len(hops) + 1, n_mp), part[0])
             hops.append(came)
-        elif h == n_mp - 2:
-            came = odd = tie(cross(odd, n_mp, 1), part[0])
+        else:
+            came = []
         parts.append(part)
         received.append(trade(tie(send, received[-1]) if h else send))
-    if came is not odd:
-        odd = cross(odd, n_mp, 1)
     result = finish_line(result_own, hops, place, n_mp)
     last = heads - 1
     sums_in = weigh_input(hidden, parts)
+    odd = tie(cross(tie(odd, parts[-1][0]), n_mp, 1), sums_in)
     input_grad = input_gradient(
         place, n_mp, packed, 0, tie(first_back, sums_in), turned, input_bank, received[:last], f32
     )
@@ -1138,7 +1169,7 @@
         place, n_mp, packed, last, input_grad, turned, input_bank, received[last:], bf16
     )
     first_hop = hop((hidden_own, hidden_own), 1, n_mp)
-    even = tie(even, received[-1])
+    even = tie(even, hidden_own)
     input_sums = lax.psum(sums_in, "dp")
     tail = [first_hop]
     if n_mp > 2:

time: 545 us -> 547 us (level)
    psum x1, waiting for transfers between devices: 21.5 us -> 0.01 us  [local(): input_sums = lax.psum(sums_in, 'dp')]
    ppermute x6, waiting for transfers between devices: 54.7 us -> 75 us  [hop(): lax.ppermute(behind, 'mp', [(i, i - 1) for i in range(1, count - k + 1)])]
    reduce_scatter x1, waiting for transfers between devices: 0.27 us -> 11 us  [local(): even = lax.psum_scatter(even, 'dp', scatter_dimension=0, tiled=False)]
    reduce_scatter x1, waiting for transfers between devices: 5.91 us -> 0.02 us  [local(): lax.psum_scatter(tie(odd, (even, input_bank)), 'dp', scatter_dimension=0,...]
  transfers between devices with their start and end apart: 45 -> 45, of which waited for: 17 -> 13; matrix products, arithmetic and copies ran while one was open for 4% -> 4% of each run, Pallas kernels for 47% -> 47%
where the time goes in v2:
time: 547 us; the launch traced here: 536 us
  Pallas kernels  264 us (48%)
  waiting for transfers between devices  146 us (27%)
  starting transfers between devices  81.3 us (15%)
  other arithmetic  20.3 us (4%)
  between operations  14.9 us (3%)
  local copies, waits for them, and re-layouts  9.9 us (2%)
    pallas_call x4, Pallas kernels, attend_back(): pl.pallas_call(functools.partial(attend_back_kernel, chunk), grid_spec=pl...  75.6 us
    ppermute x6, waiting for transfers between devices, hop(): lax.ppermute(behind, 'mp', [(i, i - 1) for i in range(1, count - k + 1)])  75 us
    pallas_call x3, Pallas kernels, attend(): pl.pallas_call(functools.partial(attend_kernel, heads), grid_spec=pltpu.P...  49.6 us
    pallas_call x1, Pallas kernels, feed(): pl.pallas_call(functools.partial(feed_kernel, n_mp, packed, splits), grid...  35.7 us
    all_to_all x5, starting transfers between devices, trade(): return lax.all_to_all(value, 'mp', 0, 0, tiled=True)  32.9 us
    ppermute x11, waiting for transfers between devices, cross(): return lax.ppermute(value, 'mp', [(i, i ^ bits) for i in range(count)])  27.3 us
    pallas_call x1, Pallas kernels, feed_back(): pl.pallas_call(functools.partial(feed_back_kernel, n_mp, packed, splits),...  26.8 us
    pallas_call x2, Pallas kernels, weigh(): pl.pallas_call(functools.partial(weigh_kernel, shares), grid=(planes, n_d...  21.9 us
  transfers between devices with their start and end apart: 45, of which 13 were waited for; matrix products, arithmetic and copies ran while one was open for 4% of the time, Pallas kernels for 47%

profile of v2, /device:TPU:0, one launch (start us, length us, event | category | flops | bytes accessed | tf_op | source)
XLA Modules:
  0.0 536.0 jit_solution(12805120221156475120)
XLA Ops:
  7.8 2.6 pack.1
  10.4 3.1 collective-permute-start
  13.5 2.6 collective-permute-start.1
  16.1 11.6 %project.1 = (bf16[4,128,2048]{2,1,0:T(8,128)(2,1)}, bf16[4,64,2048]{2,1,0:T(8,128)(2,1)}, bf16[4,2048,128]{2,1,0:T(8,128)(2,1)}, bf16[4,80,2048]{2,1,0:T(8,128)...) custom-call(s32[1,8]{1,0:T(1,128)} %lengths_ref.1, ...), custom_call_target="tpu_custom_call" | custom-call | flops 3221225472 | bytes 33554432 | tf_op jit(solution)/shard_map/project/pallas_call | solution.py:150
  27.7 13.2 %attend.3 = (bf16[1,256,512]{2,1,0:T(8,128)(2,1)}, f32[1,4,1,512]{3,2,1,0:T(1,128)}) custom-call(s32[2]{0:T(128)} %pad_add_fusion.me_ref, bf16[4,128,2048]{2,1,0:T(8,128)(2,1)} %get-tuple-element.98.qt_ref, bf16[4,2048,128]{2,1,0:T(8,128)(2,1)} %get-tuple-element.99.kn_ref, bf16[4,80,2048]{2,1,0:T(8,128)(2,1)} %get-tuple-element.100.vt_ref), custom_call_target="tpu_custom_call" | custom-call | flops 5368709120 | bytes 8388608 | tf_op jit(solution)/shard_map/attend/pallas_call | solution.py:254
  40.9 1.9 collective-permute-done.1
  46.6 2.0 collective-permute-start.5
  48.7 13.2 %attend.4 = (bf16[1,256,512]{2,1,0:T(8,128)(2,1)}, f32[1,4,1,512]{3,2,1,0:T(1,128)}) custom-call(s32[2]{0:T(128)} %pad_add_fusion.me_ref, bf16[4,128,2048]{2,1,0:T(8,128)(2,1)} %get-tuple-element.98.qt_ref, bf16[4,2048,128]{2,1,0:T(8,128)(2,1)} %get-tuple-element.99.kn_ref, bf16[4,80,2048]{2,1,0:T(8,128)(2,1)} %get-tuple-element.100.vt_ref), custom_call_target="tpu_custom_call" | custom-call | flops 5368709120 | bytes 8388608 | tf_op jit(solution)/shard_map/attend/pallas_call | solution.py:254
  61.8 2.4 collective-permute-done.5.refs_0_.refs_3_
  70.8 23.3 %attend.5 = (bf16[2,256,512]{2,1,0:T(8,128)(2,1)}, f32[2,4,1,512]{3,2,1,0:T(1,128)}) custom-call(s32[2]{0:T(128)} %pad_add_fusion.me_ref, bf16[4,128,2048]{2,1,0:T(8,128)(2,1)} %get-tuple-element.98.qt_ref, bf16[4,2048,128]{2,1,0:T(8,128)(2,1)} %get-tuple-element.99.kn_ref, bf16[4,80,2048]{2,1,0:T(8,128)(2,1)} %get-tuple-element.100.vt_ref, ...), custom_call_target="tpu_custom_call" | custom-call | flops 10737418240 | bytes 8388608 | tf_op jit(solution)/shard_map/attend/pallas_call | solution.py:254
  94.1 4.7 collective-permute-done.9
  98.8 3.1 pad_maximum_fusion.refs_8_
  107.3 10.5 %collective-permute-done.14 = bf16[2,1,256,512]{3,2,1,0:T(8,128)(2,1)S(1)} collective-permute-done((bf16[2,1,256,512]{3,2,1,0:T(8,128)(2,1)S(1)}, bf16[2,1,256,512]{3,2,1,0:T(8,128)(2,1)S(1)}, u32[]{:S(2)}, u32[]{:S(2)}) %collective-permute-start.14) | collective-permute-done | bytes 524320 | tf_op jit(solution)/shard_map/ppermute | solution.py:961
  125.8 4.0 collective-permute-start.25
  130.2 35.7 %feed.1 = (bf16[512,1024]{1,0:T(8,128)(2,1)}, bf16[512,1024]{1,0:T(8,128)(2,1)}, bf16[4,512,1024]{2,1,0:T(8,128)(2,1)}, bf16[4,512,1024]{2,1,0:T(8,128)(2,1)}, b...) custom-call(s32[2]{0:T(128)} %pad_add_fusion.me_ref, ...), custom_call_target="tpu_custom_call" | custom-call | flops 17179869184 | bytes 16777216 | tf_op jit(solution)/shard_map/feed/pallas_call | solution.py:669
  167.3 2.2 collective-permute-start.18
  170.9 26.8 %feed_back.1 = (bf16[4,512,1024]{2,1,0:T(8,128)(2,1)}, bf16[512,1024]{1,0:T(8,128)(2,1)}, f32[512,1024]{1,0:T(8,128)}, bf16[4,272,512]{2,1,0:T(8,128)(2,1)}, bf16[4,16,1024]{2,1,0:T(8,128)(2,1)}) custom-call(s32[2]{0:T(128)} %pad_add_fusion.me_ref, bf16[256,512]{1,0:T(8,128)(2,1)} %get-tuple-element.200.refs_0_, bf16[256,512]{1,0:T(8,128)(2,1)} %copy-done.23, ...), custom_call_target="tpu_custom_call" | custom-call | flops 17179869184 | bytes 16777216 | tf_op jit(solution)/shard_map/feed_back/pallas_call | solution.py:714
  197.6 7.9 %all-to-all-start = ((bf16[4,272,512]{2,1,0:T(8,128)(2,1)}), bf16[4,272,512]{2,1,0:T(8,128)(2,1)S(1)}, u32[]{:S(2)}, u32[]{:S(2)}) async-start(bf16[4,272,512]{2,1,0:T(8,128)(2,1)} %get-tuple-element.129), calls=%async_computation | async-start | bytes 2228224 | tf_op jit(solution)/shard_map/all_to_all | solution.py:957
  205.7 2.2 pad_maximum_fusion.6.ctx_ref
  208.9 10.9 %weigh.3 = bf16[8,2,304,1024]{3,2,1,0:T(8,128)(2,1)} custom-call(bf16[512,1024]{1,0:T(8,128)(2,1)} %get-tuple-element.135.first_ref, bf16[4,512,1024]{2,1,0:T(8,128)(2,1)} %get-tuple-element.136.act_ref, bf16[4,512,1024]{2,1,0:T(8,128)(2,1)} %get-tuple-element.137.ug_ref, bf16[512,1024]{1,0:T(8,128)(2,1)} %get-tuple-element.119.refs_16_.lg_ref, ...), custom_call_target="tpu_custom_call" | custom-call | flops 8589934592 | bytes 8388608 | tf_op jit(solution)/shard_map/weigh/pallas_call | solution.py:767
  219.8 11.8 %all-to-all-done.refs_0_.dot_ref.delta_ref = bf16[4,272,512]{2,1,0:T(8,128)(2,1)S(1)} async-done(((bf16[4,272,512]{2,1,0:T(8,128)(2,1)}), bf16[4,272,512]{2,1,0:T(8,128)(2,1)S(1)}, u32[]{:S(2)}, u32[]{:S(2)}) %all-to-all-start) | async-done | bytes 1114144 | tf_op jit(solution)/shard_map/all_to_all | solution.py:957
  232.6 10.9 %weigh.2.refs_0_ = bf16[8,2,304,1024]{3,2,1,0:T(8,128)(2,1)} custom-call(bf16[512,1024]{1,0:T(8,128)(2,1)} %get-tuple-element.135.first_ref, bf16[4,512,1024]{2,1,0:T(8,128)(2,1)} %get-tuple-element.136.act_ref, bf16[4,512,1024]{2,1,0:T(8,128)(2,1)} %get-tuple-element.137.ug_ref, bf16[512,1024]{1,0:T(8,128)(2,1)} %get-tuple-element.119.refs_16_.lg_ref, ...), custom_call_target="tpu_custom_call" | custom-call | flops 8589934592 | bytes 8388608 | tf_op jit(solution)/shard_map/weigh/pallas_call | solution.py:767
  247.0 18.9 %attend_back.4 = (bf16[64,2048]{1,0:T(8,128)(2,1)}, bf16[64,2048]{1,0:T(8,128)(2,1)}, bf16[64,2048]{1,0:T(8,128)(2,1)}, bf16[4,192,512]{2,1,0:T(8,128)(2,1)}) custom-call(s32[2]{0:T(128)} %pad_add_fusion.me_ref, bf16[4,128,2048]{2,1,0:T(8,128)(2,1)} %get-tuple-element.98.qt_ref, bf16[4,64,2048]{2,1,0:T(8,128)(2,1)} %get-tuple-element.127.kt_ref, ...), custom_call_target="tpu_custom_call" | custom-call | flops 21474836480 | bytes 2097152 | tf_op jit(solution)/shard_map/attend_back/pallas_call | solution.py:378
  265.9 6.3 %all-to-all-start.1 = ((bf16[4,192,512]{2,1,0:T(8,128)(2,1)}), bf16[4,192,512]{2,1,0:T(8,128)(2,1)S(1)}, u32[]{:S(2)}, u32[]{:S(2)}) async-start(bf16[4,192,512]{2,1,0:T(8,128)(2,1)} %get-tuple-element.150), calls=%async_computation.1 | async-start | bytes 1572864 | tf_op jit(solution)/shard_map/all_to_all | solution.py:957
  275.2 18.9 %attend_back.5 = (bf16[64,2048]{1,0:T(8,128)(2,1)}, bf16[64,2048]{1,0:T(8,128)(2,1)}, bf16[64,2048]{1,0:T(8,128)(2,1)}, bf16[4,192,512]{2,1,0:T(8,128)(2,1)}) custom-call(s32[2]{0:T(128)} %pad_add_fusion.me_ref, bf16[4,128,2048]{2,1,0:T(8,128)(2,1)} %get-tuple-element.98.qt_ref, bf16[4,64,2048]{2,1,0:T(8,128)(2,1)} %get-tuple-element.127.kt_ref, ...), custom_call_target="tpu_custom_call" | custom-call | flops 21474836480 | bytes 2097152 | tf_op jit(solution)/shard_map/attend_back/pallas_call | solution.py:378
  294.1 7.3 %all-to-all-start.2 = ((bf16[4,192,512]{2,1,0:T(8,128)(2,1)}), bf16[4,192,512]{2,1,0:T(8,128)(2,1)S(1)}, u32[]{:S(2)}, u32[]{:S(2)}) async-start(bf16[4,192,512]{2,1,0:T(8,128)(2,1)} %get-tuple-element.155), calls=%async_computation.2 | async-start | bytes 1572864 | tf_op jit(solution)/shard_map/all_to_all | solution.py:957
  301.4 14.4 %collective-permute-done.23.refs_5_.refs_1_ = bf16[512,1024]{1,0:T(8,128)(2,1)} collective-permute-done((bf16[512,1024]{1,0:T(8,128)(2,1)}, bf16[512,1024]{1,0:T(8,128)(2,1)}, u32[]{:S(2)}, u32[]{:S(2)}) %collective-permute-start.23) | collective-permute-done | bytes 1048608 | tf_op jit(solution)/shard_map/ppermute | solution.py:968
  315.8 18.9 %attend_back.6 = (bf16[64,2048]{1,0:T(8,128)(2,1)}, bf16[64,2048]{1,0:T(8,128)(2,1)}, bf16[64,2048]{1,0:T(8,128)(2,1)}, bf16[4,192,512]{2,1,0:T(8,128)(2,1)}) custom-call(s32[2]{0:T(128)} %pad_add_fusion.me_ref, bf16[4,128,2048]{2,1,0:T(8,128)(2,1)} %get-tuple-element.98.qt_ref, bf16[4,64,2048]{2,1,0:T(8,128)(2,1)} %get-tuple-element.127.kt_ref, ...), custom_call_target="tpu_custom_call" | custom-call | flops 21474836480 | bytes 2097152 | tf_op jit(solution)/shard_map/attend_back/pallas_call | solution.py:378
  334.7 6.3 %all-to-all-start.3 = ((bf16[4,192,512]{2,1,0:T(8,128)(2,1)}), bf16[4,192,512]{2,1,0:T(8,128)(2,1)S(1)}, u32[]{:S(2)}, u32[]{:S(2)}) async-start(bf16[4,192,512]{2,1,0:T(8,128)(2,1)} %get-tuple-element.165), calls=%async_computation.3 | async-start | bytes 1572864 | tf_op jit(solution)/shard_map/all_to_all | solution.py:957
  341.0 19.0 %attend_back.7 = (bf16[64,2048]{1,0:T(8,128)(2,1)}, bf16[64,2048]{1,0:T(8,128)(2,1)}, bf16[64,2048]{1,0:T(8,128)(2,1)}, bf16[4,192,512]{2,1,0:T(8,128)(2,1)}) custom-call(s32[2]{0:T(128)} %pad_add_fusion.me_ref, bf16[4,128,2048]{2,1,0:T(8,128)(2,1)} %get-tuple-element.98.qt_ref, bf16[4,64,2048]{2,1,0:T(8,128)(2,1)} %get-tuple-element.127.kt_ref, ...), custom_call_target="tpu_custom_call" | custom-call | flops 21474836480 | bytes 2097152 | tf_op jit(solution)/shard_map/attend_back/pallas_call | solution.py:378
  360.0 5.1 all-to-all-start.4
  365.4 2.1 collective-permute-start.33
  367.5 8.3 %weigh_input.1 = bf16[3,1040,256]{2,1,0:T(8,128)(2,1)} custom-call(bf16[2048,1024]{1,0:T(8,128)(2,1)} %hidden_ref.5, bf16[64,2048]{1,0:T(8,128)(2,1)} %get-tuple-element.139.refs_0_, bf16[64,2048]{1,0:T(8,128)(2,1)} %get-tuple-element.146.refs_1_, bf16[64,2048]{1,0:T(8,128)(2,1)} %get-tuple-element.147.refs_2_, bf16[64,2048]{1,0:T(8,128)(2,1)} %get-tuple-element.142.refs_3_, ...), custom_call_target="tpu_custom_call" | custom-call | flops 3221225472 | bytes 16777216 | tf_op jit(solution)/shard_map/weigh_input/pallas_call | solution.py:906
  375.8 9.7 %input_gradient.2.back_ref = f32[512,1024]{1,0:T(8,128)} custom-call(s32[2]{0:T(128)} %pad_add_fusion.me_ref, f32[512,1024]{1,0:T(8,128)} %get-tuple-element.159.back_ref, bf16[768,1024]{1,0:T(8,128)(2,1)} %get-tuple-element.160.own_ref, bf16[8,3,96,1024]{3,2,1,0:T(8,128)(2,1)} %bitcast.57, bf16[4,192,512]{2,1,0:T(8,128)(2,1)} %copy-done, ...), custom_call_target="tpu_custom_call" | custom-call | flops 3221225472 | bytes 6291456 | tf_op jit(solution)/shard_map/input_gradient/pallas_call | solution.py:827
  386.4 6.4 %input_gradient.3.own_ref = bf16[512,1024]{1,0:T(8,128)(2,1)} custom-call(s32[2]{0:T(128)} %pad_add_fusion.me_ref, f32[512,1024]{1,0:T(8,128)} %input_gradient.2.back_ref, bf16[768,1024]{1,0:T(8,128)(2,1)} %get-tuple-element.160.own_ref, bf16[8,3,96,1024]{3,2,1,0:T(8,128)(2,1)} %bitcast.58, bf16[4,192,512]{2,1,0:T(8,128)(2,1)} %copy-done.16), custom_call_target="tpu_custom_call" | custom-call | flops 3221225472 | bytes 6291456 | tf_op jit(solution)/shard_map/input_gradient/pallas_call | solution.py:827
  392.8 11.0 %reduce-scatter.3.cloned.1.call-done = bf16[1,2,304,1024]{3,2,1,0:T(8,128)(2,1)} async-done(((bf16[8,2,304,1024]{3,2,1,0:T(8,128)(2,1)}), bf16[1,2,304,1024]{3,2,1,0:T(8,128)(2,1)}) %reduce-scatter.3.cloned.1.call-update) | async-done | bytes 1245200 | tf_op jit(solution)/shard_map/reduce_scatter | solution.py:1137
  405.4 2.5 collective-permute-start.34
  407.9 4.4 collective-permute-start.27
  413.7 23.0 %collective-permute-done.34 = bf16[1,304,1024]{2,1,0:T(8,128)(2,1)} collective-permute-done((bf16[1,304,1024]{2,1,0:T(8,128)(2,1)S(1)}, bf16[1,304,1024]{2,1,0:T(8,128)(2,1)}, u32[]{:S(2)}, u32[]{:S(2)}) %collective-permute-start.34) | collective-permute-done | bytes 622624 | tf_op jit(solution)/shard_map/ppermute | solution.py:949
  439.2 4.5 collective-permute-done.27.refs_0_
  443.7 7.3 %collective-permute-done.29.refs_3_ = bf16[512,1024]{1,0:T(8,128)(2,1)} collective-permute-done((bf16[512,1024]{1,0:T(8,128)(2,1)S(1)}, bf16[512,1024]{1,0:T(8,128)(2,1)}, u32[]{:S(2)}, u32[]{:S(2)}) %collective-permute-start.29) | collective-permute-done | bytes 1048608 | tf_op jit(solution)/shard_map/ppermute | solution.py:968
  453.9 35.3 %collective-permute-done.30.refs_4_ = bf16[512,1024]{1,0:T(8,128)(2,1)} collective-permute-done((bf16[512,1024]{1,0:T(8,128)(2,1)}, bf16[512,1024]{1,0:T(8,128)(2,1)}, u32[]{:S(2)}, u32[]{:S(2)}) %collective-permute-start.30) | collective-permute-done | bytes 1048608 | tf_op jit(solution)/shard_map/ppermute | solution.py:968
  489.3 1.8 collective-permute-start.31
  492.4 4.0 join_line.2
  497.8 1.7 slice_bitcast_fusion
  499.5 18.0 %collective-permute-done.32.refs_5_ = bf16[512,1024]{1,0:T(8,128)(2,1)} collective-permute-done((bf16[512,1024]{1,0:T(8,128)(2,1)}, bf16[512,1024]{1,0:T(8,128)(2,1)}, u32[]{:S(2)}, u32[]{:S(2)}) %collective-permute-start.32) | collective-permute-done | bytes 1048608 | tf_op jit(solution)/shard_map/ppermute | solution.py:968
  517.5 4.0 join_line.3
  521.5 7.5 %unpack.1 = (f32[256,1024]{1,0:T(8,128)}, f32[1024,1024]{1,0:T(8,128)}, f32[1024,1024]{1,0:T(8,128)}) custom-call(bf16[8,288,1024]{2,1,0:T(8,128)(2,1)} %bitcast.59), custom_call_target="tpu_custom_call" | custom-call | tf_op jit(solution)/shard_map/unpack/pallas_call | solution.py:929
  (168 shorter events, 48.1 us)
Async XLA Ops:
  7.2 236.3 %all-gather.5.cloned.1.call-start = ((), (), s32[]{:S(2)}) async-start(), calls=%async_computation.10 | async-start | bytes 5308416 | tf_op jit(solution)/shard_map/all_gather | solution.py:1017
  10.4 30.4 %collective-permute-start = (bf16[592,512]{1,0:T(8,128)(2,1)}, bf16[592,512]{1,0:T(8,128)(2,1)S(1)}, u32[]{:S(2)}, u32[]{:S(2)}) collective-permute-start(bf16[592,512]{1,0:T(8,128)(2,1)} %pack.1), channel_id=1, source_target_pairs={{0,1},{1,0},{2,3},{3,2},{4,5},{5,4},{6,7},{7,6},{8,9},{9,8},{10,11... | collective-permute-start | bytes 1818632 | tf_op jit(solution)/shard_map/ppermute | solution.py:949
  13.5 29.3 %collective-permute-start.1 = (bf16[592,512]{1,0:T(8,128)(2,1)}, bf16[592,512]{1,0:T(8,128)(2,1)S(1)}, u32[]{:S(2)}, u32[]{:S(2)}) collective-permute-start(bf16[592,512]{1,0:T(8,128)(2,1)} %pack.1), channel_id=1, source_target_pairs={{0,2},{1,3},{2,0},{3,1},{4,6},{5,7},{6,4},{7,5},{8,10},{9,11},{10,... | collective-permute-start | bytes 1818632 | tf_op jit(solution)/shard_map/ppermute | solution.py:949
  43.0 21.2 %collective-permute-start.3 = (bf16[1,2,320,512]{3,2,1,0:T(8,128)(2,1)S(1)}, bf16[1,2,320,512]{3,2,1,0:T(8,128)(2,1)S(1)}, u32[]{:S(2)}, u32[]{:S(2)}) collective-permute-start(bf16[1,2,320,512]{3,2,1,0:T(8,128)(2,1)S(1)} %slice.187), channel_id=1, source_target_pairs={{0,16},{4,20},{8,24},{12,28},{16,0},{20,4},{24,8},{28,12},{1,17},{... | collective-permute-start | bytes 1966088 | tf_op jit(solution)/shard_map/ppermute | solution.py:961
  44.6 19.6 %collective-permute-start.4 = (bf16[592,512]{1,0:T(8,128)(2,1)S(1)}, bf16[592,512]{1,0:T(8,128)(2,1)S(1)}, u32[]{:S(2)}, u32[]{:S(2)}) collective-permute-start(bf16[592,512]{1,0:T(8,128)(2,1)S(1)} %collective-permute-done.1), channel_id=1, source_target_pairs={{0,1},{1,0},{2,3},{3,2},{4,5},{5,4},{6,7},{7,6},{8,9},{9,8},{10,11... | collective-permute-start | bytes 1818632 | tf_op jit(solution)/shard_map/ppermute | solution.py:949
  45.1 19.1 %collective-permute-start.2 = (bf16[1,2,256,512]{3,2,1,0:T(8,128)(2,1)S(1)}, bf16[1,2,256,512]{3,2,1,0:T(8,128)(2,1)S(1)}, u32[]{:S(2)}, u32[]{:S(2)}) collective-permute-start(bf16[1,2,256,512]{3,2,1,0:T(8,128)(2,1)S(1)} %slice.186), channel_id=1, source_target_pairs={{0,8},{4,12},{8,0},{12,4},{16,24},{20,28},{24,16},{28,20},{1,9},{5... | collective-permute-start | bytes 1572872 | tf_op jit(solution)/shard_map/ppermute | solution.py:961
  46.6 17.6 %collective-permute-start.5 = (bf16[256,512]{1,0:T(8,128)(2,1)}, bf16[256,512]{1,0:T(8,128)(2,1)S(1)}, u32[]{:S(2)}, u32[]{:S(2)}) collective-permute-start(bf16[256,512]{1,0:T(8,128)(2,1)} %bitcast.9), channel_id=1, source_target_pairs={{0,3},{1,2},{2,1},{3,0},{4,7},{5,6},{6,5},{7,4},{8,11},{9,10},{10,... | collective-permute-start | bytes 786440 | tf_op jit(solution)/shard_map/ppermute | solution.py:949
  65.5 33.3 %collective-permute-start.8 = (bf16[2,2,320,512]{3,2,1,0:T(8,128)(2,1)}, bf16[2,2,320,512]{3,2,1,0:T(8,128)(2,1)}, u32[]{:S(2)}, u32[]{:S(2)}) collective-permute-start(bf16[2,2,320,512]{3,2,1,0:T(8,128)(2,1)} %pad_maximum_fusion.2.refs_2_), channel_id=1, source_target_pairs={{0,8},{4,12},{8,0},{12,4},{16,24},{20,28},{24,16},{28,20},{1,9},{5... | collective-permute-start | bytes 3932168 | tf_op jit(solution)/shard_map/ppermute | solution.py:961
  68.1 30.7 %collective-permute-start.7 = (bf16[2,2,256,512]{3,2,1,0:T(8,128)(2,1)}, bf16[2,2,256,512]{3,2,1,0:T(8,128)(2,1)}, u32[]{:S(2)}, u32[]{:S(2)}) collective-permute-start(bf16[2,2,256,512]{3,2,1,0:T(8,128)(2,1)} %pad_maximum_fusion.4.refs_1_), channel_id=1, source_target_pairs={{0,16},{4,20},{8,24},{12,28},{16,0},{20,4},{24,8},{28,12},{1,17},{... | collective-permute-start | bytes 3145736 | tf_op jit(solution)/shard_map/ppermute | solution.py:961
  69.0 25.1 %collective-permute-start.11 = (bf16[256,512]{1,0:T(8,128)(2,1)}, bf16[256,512]{1,0:T(8,128)(2,1)S(1)}, u32[]{:S(2)}, u32[]{:S(2)}) collective-permute-start(bf16[256,512]{1,0:T(8,128)(2,1)} %bitcast.13), channel_id=1, source_target_pairs={{0,2},{1,3},{2,0},{3,1},{4,6},{5,7},{6,4},{7,5},{8,10},{9,11},{10,... | collective-permute-start | bytes 786440 | tf_op jit(solution)/shard_map/ppermute | solution.py:949
  69.0 29.7 %collective-permute-start.10 = (bf16[1,1,320,512]{3,2,1,0:T(8,128)(2,1)S(1)}, bf16[1,1,320,512]{3,2,1,0:T(8,128)(2,1)S(1)}, u32[]{:S(2)}, u32[]{:S(2)}) collective-permute-start(bf16[1,1,320,512]{3,2,1,0:T(8,128)(2,1)S(1)} %slice.189.refs_4_), channel_id=1, source_target_pairs={{0,16},{4,20},{8,24},{12,28},{16,0},{20,4},{24,8},{28,12},{1,17},{... | collective-permute-start | bytes 983048 | tf_op jit(solution)/shard_map/ppermute | solution.py:961
  70.3 28.5 %collective-permute-start.9 = (bf16[1,1,256,512]{3,2,1,0:T(8,128)(2,1)S(1)}, bf16[1,1,256,512]{3,2,1,0:T(8,128)(2,1)S(1)}, u32[]{:S(2)}, u32[]{:S(2)}) collective-permute-start(bf16[1,1,256,512]{3,2,1,0:T(8,128)(2,1)S(1)} %slice.188.refs_3_), channel_id=1, source_target_pairs={{0,8},{4,12},{8,0},{12,4},{16,24},{20,28},{24,16},{28,20},{1,9},{5... | collective-permute-start | bytes 786440 | tf_op jit(solution)/shard_map/ppermute | solution.py:961
  101.9 28.2 %collective-permute-start.13 = (bf16[4,2,320,512]{3,2,1,0:T(8,128)(2,1)}, bf16[4,2,320,512]{3,2,1,0:T(8,128)(2,1)}, u32[]{:S(2)}, u32[]{:S(2)}) collective-permute-start(bf16[4,2,320,512]{3,2,1,0:T(8,128)(2,1)} %pad_maximum_fusion.refs_8_), channel_id=1, source_target_pairs={{0,4},{4,0},{8,12},{12,8},{16,20},{20,16},{24,28},{28,24},{1,5},{5... | collective-permute-start | bytes 7864328 | tf_op jit(solution)/shard_map/ppermute | solution.py:961
  102.0 17.2 %collective-permute-start.15 = (bf16[2,1,320,512]{3,2,1,0:T(8,128)(2,1)S(1)}, bf16[2,1,320,512]{3,2,1,0:T(8,128)(2,1)S(1)}, u32[]{:S(2)}, u32[]{:S(2)}) collective-permute-start(bf16[2,1,320,512]{3,2,1,0:T(8,128)(2,1)S(1)} %pad_maximum_fusion.7), channel_id=1, source_target_pairs={{0,8},{4,12},{8,0},{12,4},{16,24},{20,28},{24,16},{28,20},{1,9},{5... | collective-permute-start | bytes 1966088 | tf_op jit(solution)/shard_map/ppermute | solution.py:961
  103.6 14.1 %collective-permute-start.14 = (bf16[2,1,256,512]{3,2,1,0:T(8,128)(2,1)S(1)}, bf16[2,1,256,512]{3,2,1,0:T(8,128)(2,1)S(1)}, u32[]{:S(2)}, u32[]{:S(2)}) collective-permute-start(bf16[2,1,256,512]{3,2,1,0:T(8,128)(2,1)S(1)} %pad_maximum_fusion.9), channel_id=1, source_target_pairs={{0,16},{4,20},{8,24},{12,28},{16,0},{20,4},{24,8},{28,12},{1,17},{... | collective-permute-start | bytes 1572872 | tf_op jit(solution)/shard_map/ppermute | solution.py:961
  106.3 23.9 %collective-permute-start.12 = (bf16[4,2,256,512]{3,2,1,0:T(8,128)(2,1)S(1)}, bf16[4,2,256,512]{3,2,1,0:T(8,128)(2,1)}, u32[]{:S(2)}, u32[]{:S(2)}) collective-permute-start(bf16[4,2,256,512]{3,2,1,0:T(8,128)(2,1)S(1)} %pad_maximum_fusion.1.refs_7_), channel_id=1, source_target_pairs={{0,4},{4,0},{8,12},{12,8},{16,20},{20,16},{24,28},{28,24},{1,5},{5... | collective-permute-start | bytes 6291464 | tf_op jit(solution)/shard_map/ppermute | solution.py:961
  107.3 13.2 %collective-permute-start.6 = (bf16[256,512]{1,0:T(8,128)(2,1)S(1)}, bf16[256,512]{1,0:T(8,128)(2,1)S(1)}, u32[]{:S(2)}, u32[]{:S(2)}) collective-permute-start(bf16[256,512]{1,0:T(8,128)(2,1)S(1)} %get-tuple-element.201), channel_id=1, source_target_pairs={{0,1},{1,0},{2,3},{3,2},{4,5},{5,4},{6,7},{7,6},{8,9},{9,8},{10,11... | collective-permute-start | bytes 786440 | tf_op jit(solution)/shard_map/ppermute | solution.py:949
  120.5 9.3 %collective-permute-start.17 = (bf16[4,1,320,512]{3,2,1,0:T(8,128)(2,1)}, bf16[4,1,320,512]{3,2,1,0:T(8,128)(2,1)}, u32[]{:S(2)}, u32[]{:S(2)}) collective-permute-start(bf16[4,1,320,512]{3,2,1,0:T(8,128)(2,1)} %pad_maximum_fusion.3.refs_12_), channel_id=1, source_target_pairs={{0,4},{4,0},{8,12},{12,8},{16,20},{20,16},{24,28},{28,24},{1,5},{5... | collective-permute-start | bytes 3932168 | tf_op jit(solution)/shard_map/ppermute | solution.py:961
  120.5 5.3 collective-permute-start.16
  121.9 44.0 %collective-permute-start.24 = (bf16[96,1024]{1,0:T(8,128)(2,1)S(1)}, bf16[96,1024]{1,0:T(8,128)(2,1)S(1)}, u32[]{:S(2)}, u32[]{:S(2)}) collective-permute-start(bf16[96,1024]{1,0:T(8,128)(2,1)S(1)} %constant_dynamic-slice_fusion), channel_id=1, source_target_pairs={{0,1},{1,0},{2,3},{3,2},{4,5},{5,4},{6,7},{7,6},{8,9},{9,8},{10,11... | collective-permute-start | bytes 589832 | tf_op jit(solution)/shard_map/ppermute | solution.py:949
  125.8 40.1 %collective-permute-start.25 = (bf16[96,1024]{1,0:T(8,128)(2,1)S(1)}, bf16[96,1024]{1,0:T(8,128)(2,1)S(1)}, u32[]{:S(2)}, u32[]{:S(2)}) collective-permute-start(bf16[96,1024]{1,0:T(8,128)(2,1)S(1)} %constant_dynamic-slice_fusion), channel_id=1, source_target_pairs={{0,2},{1,3},{2,0},{3,1},{4,6},{5,7},{6,4},{7,5},{8,10},{9,11},{10,... | collective-permute-start | bytes 589832 | tf_op jit(solution)/shard_map/ppermute | solution.py:949
  129.8 36.1 %collective-permute-start.26 = (bf16[96,1024]{1,0:T(8,128)(2,1)S(1)}, bf16[96,1024]{1,0:T(8,128)(2,1)S(1)}, u32[]{:S(2)}, u32[]{:S(2)}) collective-permute-start(bf16[96,1024]{1,0:T(8,128)(2,1)S(1)} %constant_dynamic-slice_fusion), channel_id=1, source_target_pairs={{0,3},{1,2},{2,1},{3,0},{4,7},{5,6},{6,5},{7,4},{8,11},{9,10},{10,... | collective-permute-start | bytes 589832 | tf_op jit(solution)/shard_map/ppermute | solution.py:949
  167.3 40.6 %collective-permute-start.18 = (bf16[512,1024]{1,0:T(8,128)(2,1)S(1)}, bf16[512,1024]{1,0:T(8,128)(2,1)S(1)}, u32[]{:S(2)}, u32[]{:S(2)}) collective-permute-start(bf16[512,1024]{1,0:T(8,128)(2,1)S(1)} %copy-done.11), channel_id=1, source_target_pairs={{0,1},{1,2},{2,3},{4,5},{5,6},{6,7},{8,9},{9,10},{10,11},{12,13},{... | collective-permute-start | bytes 3145736 | tf_op jit(solution)/shard_map/ppermute | solution.py:967
  169.6 38.4 %collective-permute-start.19 = (bf16[512,1024]{1,0:T(8,128)(2,1)S(1)}, bf16[512,1024]{1,0:T(8,128)(2,1)}, u32[]{:S(2)}, u32[]{:S(2)}) collective-permute-start(bf16[512,1024]{1,0:T(8,128)(2,1)S(1)} %copy-done.11), channel_id=1, source_target_pairs={{1,0},{2,1},{3,2},{5,4},{6,5},{7,6},{9,8},{10,9},{11,10},{13,12},{... | collective-permute-start | bytes 3145736 | tf_op jit(solution)/shard_map/ppermute | solution.py:968
  197.6 34.0 %all-to-all-start = ((bf16[4,272,512]{2,1,0:T(8,128)(2,1)}), bf16[4,272,512]{2,1,0:T(8,128)(2,1)S(1)}, u32[]{:S(2)}, u32[]{:S(2)}) async-start(bf16[4,272,512]{2,1,0:T(8,128)(2,1)} %get-tuple-element.129), calls=%async_computation | async-start | bytes 2228224 | tf_op jit(solution)/shard_map/all_to_all | solution.py:957
  205.5 159.9 %reduce-scatter.5.cloned.1.call-start = ((), (), s32[]{:S(2)}) async-start(), calls=%async_computation.9 | async-start | bytes 11206656 | tf_op jit(solution)/shard_map/reduce_scatter | solution.py:1136
  243.6 160.2 %reduce-scatter.3.cloned.1.call-start = ((), (), s32[]{:S(2)}) async-start(), calls=%async_computation.8 | async-start | bytes 11206656 | tf_op jit(solution)/shard_map/reduce_scatter | solution.py:1137
  245.0 27.3 %collective-permute-start.20 = (bf16[512,1024]{1,0:T(8,128)(2,1)S(1)}, bf16[512,1024]{1,0:T(8,128)(2,1)S(1)}, u32[]{:S(2)}, u32[]{:S(2)}) collective-permute-start(bf16[512,1024]{1,0:T(8,128)(2,1)S(1)} %copy-done.13), channel_id=1, source_target_pairs={{1,2},{2,3},{5,6},{6,7},{9,10},{10,11},{13,14},{14,15},{17,18},{18... | collective-permute-start | bytes 3145736 | tf_op jit(solution)/shard_map/ppermute | solution.py:967
  245.7 26.5 %collective-permute-start.21 = (bf16[512,1024]{1,0:T(8,128)(2,1)}, bf16[512,1024]{1,0:T(8,128)(2,1)}, u32[]{:S(2)}, u32[]{:S(2)}) collective-permute-start(bf16[512,1024]{1,0:T(8,128)(2,1)} %collective-permute-done.19.refs_2_.refs_3_.refs_1_), channel_id=1, source_target_pairs={{1,0},{2,1},{5,4},{6,5},{9,8},{10,9},{13,12},{14,13},{17,16},{18,1... | collective-permute-start | bytes 3145736 | tf_op jit(solution)/shard_map/ppermute | solution.py:968
  265.9 28.1 %all-to-all-start.1 = ((bf16[4,192,512]{2,1,0:T(8,128)(2,1)}), bf16[4,192,512]{2,1,0:T(8,128)(2,1)S(1)}, u32[]{:S(2)}, u32[]{:S(2)}) async-start(bf16[4,192,512]{2,1,0:T(8,128)(2,1)} %get-tuple-element.150), calls=%async_computation.1 | async-start | bytes 1572864 | tf_op jit(solution)/shard_map/all_to_all | solution.py:957
  272.3 29.1 %collective-permute-start.22 = (bf16[512,1024]{1,0:T(8,128)(2,1)S(1)}, bf16[512,1024]{1,0:T(8,128)(2,1)}, u32[]{:S(2)}, u32[]{:S(2)}) collective-permute-start(bf16[512,1024]{1,0:T(8,128)(2,1)S(1)} %collective-permute-done.20.refs_0_.refs_1_), channel_id=1, source_target_pairs={{2,3},{6,7},{10,11},{14,15},{18,19},{22,23},{26,27},{30,31}} | collective-permute-start | bytes 3145736 | tf_op jit(solution)/shard_map/ppermute | solution.py:967
  273.9 41.9 %collective-permute-start.23 = (bf16[512,1024]{1,0:T(8,128)(2,1)}, bf16[512,1024]{1,0:T(8,128)(2,1)}, u32[]{:S(2)}, u32[]{:S(2)}) collective-permute-start(bf16[512,1024]{1,0:T(8,128)(2,1)} %collective-permute-done.21.refs_1_.refs_4_), channel_id=1, source_target_pairs={{1,0},{5,4},{9,8},{13,12},{17,16},{21,20},{25,24},{29,28}} | collective-permute-start | bytes 3145736 | tf_op jit(solution)/shard_map/ppermute | solution.py:968
  294.1 21.7 %copy-start = (bf16[4,192,512]{2,1,0:T(8,128)(2,1)}, bf16[4,192,512]{2,1,0:T(8,128)(2,1)S(1)}, u32[]{:S(2)}) copy-start(bf16[4,192,512]{2,1,0:T(8,128)(2,1)S(1)} %all-to-all-done.1.refs_2_.refs_0_) | copy-start | bytes 2359300
  294.1 40.6 %all-to-all-start.2 = ((bf16[4,192,512]{2,1,0:T(8,128)(2,1)}), bf16[4,192,512]{2,1,0:T(8,128)(2,1)S(1)}, u32[]{:S(2)}, u32[]{:S(2)}) async-start(bf16[4,192,512]{2,1,0:T(8,128)(2,1)} %get-tuple-element.155), calls=%async_computation.2 | async-start | bytes 1572864 | tf_op jit(solution)/shard_map/all_to_all | solution.py:957
  334.7 25.3 %all-to-all-start.3 = ((bf16[4,192,512]{2,1,0:T(8,128)(2,1)}), bf16[4,192,512]{2,1,0:T(8,128)(2,1)S(1)}, u32[]{:S(2)}, u32[]{:S(2)}) async-start(bf16[4,192,512]{2,1,0:T(8,128)(2,1)} %get-tuple-element.165), calls=%async_computation.3 | async-start | bytes 1572864 | tf_op jit(solution)/shard_map/all_to_all | solution.py:957
  360.0 15.8 %copy-start.2 = (bf16[4,192,512]{2,1,0:T(8,128)(2,1)}, bf16[4,192,512]{2,1,0:T(8,128)(2,1)S(1)}, u32[]{:S(2)}) copy-start(bf16[4,192,512]{2,1,0:T(8,128)(2,1)S(1)} %all-to-all-done.3.refs_2_) | copy-start | bytes 2359300
  360.0 25.5 %all-to-all-start.4 = ((bf16[4,192,512]{2,1,0:T(8,128)(2,1)}), bf16[4,192,512]{2,1,0:T(8,128)(2,1)S(1)}, u32[]{:S(2)}, u32[]{:S(2)}) async-start(bf16[4,192,512]{2,1,0:T(8,128)(2,1)} %get-tuple-element.167), calls=%async_computation.4 | async-start | bytes 1572864 | tf_op jit(solution)/shard_map/all_to_all | solution.py:957
  365.1 124.2 %all-reduce.2.cloned.1.call-start = ((), (), s32[]{:S(2)}) async-start(), calls=%async_computation.7 | async-start | bytes 3194880 | tf_op jit(solution)/shard_map/psum | solution.py:1173
  365.4 38.4 %collective-permute-start.33 = (bf16[2,304,1024]{2,1,0:T(8,128)(2,1)}, bf16[2,304,1024]{2,1,0:T(8,128)(2,1)}, u32[]{:S(2)}, u32[]{:S(2)}) collective-permute-start(bf16[2,304,1024]{2,1,0:T(8,128)(2,1)} %bitcast.96), channel_id=1, source_target_pairs={{0,1},{1,0},{2,3},{3,2},{4,5},{5,4},{6,7},{7,6},{8,9},{9,8},{10,11... | collective-permute-start | bytes 3735560 | tf_op jit(solution)/shard_map/ppermute | solution.py:949
  403.8 32.9 %copy-start.9 = (bf16[1,2,304,1024]{3,2,1,0:T(8,128)(2,1)S(1)}, bf16[1,2,304,1024]{3,2,1,0:T(8,128)(2,1)}, u32[]{:S(2)}) copy-start(bf16[1,2,304,1024]{3,2,1,0:T(8,128)(2,1)} %reduce-scatter.3.cloned.1.call-done) | copy-start | bytes 3735556
  405.4 31.2 %collective-permute-start.34 = (bf16[1,304,1024]{2,1,0:T(8,128)(2,1)S(1)}, bf16[1,304,1024]{2,1,0:T(8,128)(2,1)}, u32[]{:S(2)}, u32[]{:S(2)}) collective-permute-start(bf16[1,304,1024]{2,1,0:T(8,128)(2,1)S(1)} %add_convert_fusion), channel_id=1, source_target_pairs={{0,2},{1,3},{2,0},{3,1},{4,6},{5,7},{6,4},{7,5},{8,10},{9,11},{10,... | collective-permute-start | bytes 1867784 | tf_op jit(solution)/shard_map/ppermute | solution.py:949
  407.9 35.8 %collective-permute-start.27 = (bf16[512,1024]{1,0:T(8,128)(2,1)S(1)}, bf16[512,1024]{1,0:T(8,128)(2,1)}, u32[]{:S(2)}, u32[]{:S(2)}) collective-permute-start(bf16[512,1024]{1,0:T(8,128)(2,1)S(1)} %copy-done.15), channel_id=1, source_target_pairs={{0,1},{1,2},{2,3},{4,5},{5,6},{6,7},{8,9},{9,10},{10,11},{12,13},{... | collective-permute-start | bytes 3145736 | tf_op jit(solution)/shard_map/ppermute | solution.py:967
  412.3 38.7 %collective-permute-start.29 = (bf16[512,1024]{1,0:T(8,128)(2,1)S(1)}, bf16[512,1024]{1,0:T(8,128)(2,1)}, u32[]{:S(2)}, u32[]{:S(2)}) collective-permute-start(bf16[512,1024]{1,0:T(8,128)(2,1)S(1)} %copy-done.15), channel_id=1, source_target_pairs={{1,0},{2,1},{3,2},{5,4},{6,5},{7,6},{9,8},{10,9},{11,10},{13,12},{... | collective-permute-start | bytes 3145736 | tf_op jit(solution)/shard_map/ppermute | solution.py:968
  413.6 107.9 %all-gather.7.cloned.1.call-start = ((), (), s32[]{:S(2)}) async-start(), calls=%async_computation.11 | async-start | bytes 5308416 | tf_op jit(solution)/shard_map/all_gather | solution.py:1017
  451.0 2.9 collective-permute-start.28
  452.6 36.6 %collective-permute-start.30 = (bf16[512,1024]{1,0:T(8,128)(2,1)}, bf16[512,1024]{1,0:T(8,128)(2,1)}, u32[]{:S(2)}, u32[]{:S(2)}) collective-permute-start(bf16[512,1024]{1,0:T(8,128)(2,1)} %collective-permute-done.29.refs_3_), channel_id=1, source_target_pairs={{1,0},{2,1},{5,4},{6,5},{9,8},{10,9},{13,12},{14,13},{17,16},{18,1... | collective-permute-start | bytes 3145736 | tf_op jit(solution)/shard_map/ppermute | solution.py:968
  489.3 10.3 %collective-permute-start.31 = (bf16[512,1024]{1,0:T(8,128)(2,1)}, bf16[512,1024]{1,0:T(8,128)(2,1)}, u32[]{:S(2)}, u32[]{:S(2)}) collective-permute-start(bf16[512,1024]{1,0:T(8,128)(2,1)} %collective-permute-done.28.refs_1_), channel_id=1, source_target_pairs={{2,3},{6,7},{10,11},{14,15},{18,19},{22,23},{26,27},{30,31}} | collective-permute-start | bytes 3145736 | tf_op jit(solution)/shard_map/ppermute | solution.py:967
  491.1 26.4 %collective-permute-start.32 = (bf16[512,1024]{1,0:T(8,128)(2,1)}, bf16[512,1024]{1,0:T(8,128)(2,1)}, u32[]{:S(2)}, u32[]{:S(2)}) collective-permute-start(bf16[512,1024]{1,0:T(8,128)(2,1)} %collective-permute-done.30.refs_4_), channel_id=1, source_target_pairs={{1,0},{5,4},{9,8},{13,12},{17,16},{21,20},{25,24},{29,28}} | collective-permute-start | bytes 3145736 | tf_op jit(solution)/shard_map/ppermute | solution.py:968
  (30 other events, 116.1 us)
Sparse Core Ops, SparseCore 0:
  166.9 39.6 all-gather.4
  243.7 77.4 reduce-scatter.4
  324.8 78.9 reduce-scatter.2
  413.7 58.4 all-reduce.1
  474.7 38.3 all-gather.6

commit v3 on v1

--- a/solution.py
+++ b/solution.py
@@ -724,29 +724,30 @@
         out_ref[d, 0, at:] = vec_ref[0]
 
 
-def weigh(n_dp, width, start, step, first_low, act, ug, lg, ctx, ag, vec, after):
+def weigh(n_dp, width, start, planes, first_low, act, ug, lg, ctx, ag, vec, base, after):
     own, depth = first_low.shape
     n_mp, _, local = act.shape
     shares = (width // n_dp, depth // n_dp, local // n_dp)
     total = sum(shares) + FEAT
     count = min(4, n_dp)
-    planes = n_mp // step
+    extra = ([] if base is None else [base]) + after
     whole = lambda *shape: pl.BlockSpec(shape, lambda s, d: (0, 0))
     return pl.pallas_call(
         functools.partial(weigh_kernel, shares),
         grid=(planes, n_dp // count),
         in_specs=[
             pl.BlockSpec((own, count * shares[1]), lambda s, d: (0, d)),
-            pl.BlockSpec((1, own, count * shares[2]), lambda s, d: (start + step * s, 0, d)),
-            pl.BlockSpec((1, own, local), lambda s, d: (start + step * s, 0, 0)),
+            pl.BlockSpec((1, own, count * shares[2]), lambda s, d: (start + s, 0, d)),
+            pl.BlockSpec((1, own, local), lambda s, d: (start + s, 0, 0)),
             whole(own, depth),
-            pl.BlockSpec((1, count * shares[0], own), lambda s, d: (start + step * s, d, 0)),
+            pl.BlockSpec((1, count * shares[0], own), lambda s, d: (start + s, d, 0)),
             whole(own, depth),
-            pl.BlockSpec((1, FEAT, depth), lambda s, d: (start + step * s, 0, 0)),
+            pl.BlockSpec((1, FEAT, depth), lambda s, d: (start + s, 0, 0)),
         ]
-        + [pl.BlockSpec(memory_space=pl.ANY)] * len(after),
-        out_specs=pl.BlockSpec((count, 1, total, depth), lambda s, d: (d, s, 0, 0)),
-        out_shape=jax.ShapeDtypeStruct((n_dp, planes, total, depth), bf16),
+        + [pl.BlockSpec(memory_space=pl.ANY)] * len(extra),
+        out_specs=pl.BlockSpec((count, 1, total, depth), lambda s, d: (d, start + s, 0, 0)),
+        out_shape=jax.ShapeDtypeStruct((n_dp, n_mp, total, depth), bf16),
+        input_output_aliases={} if base is None else {7: 0},
         compiler_params=params("arbitrary", "arbitrary"),
         cost_estimate=pl.CostEstimate(
             flops=8 * own * depth * local * planes,
@@ -754,7 +755,7 @@
             transcendentals=0,
         ),
         name="weigh",
-    )(first_low, act, ug, lg, ctx, ag, vec, *after)
+    )(first_low, act, ug, lg, ctx, ag, vec, *extra)
 
 
 def input_kernel(n_mp, packed, first, me_ref, back_ref, own_ref, bank_ref, *refs):
@@ -1098,11 +1099,14 @@
     if packed:
         stacked = jnp.stack([item[:width] for item in contexts])
         operands = (first_low, act, ug, lg, stacked, ag, vec)
-        odd = weigh(n_dp, width, 1, 2, *operands, list(came))
-        even = weigh(n_dp, width, 0, 2, *operands, [grads])
-        ready = [even]
-        odd = lax.psum_scatter(tie(odd, (even, input_bank)), "dp", scatter_dimension=0, tiled=False)
-        even = lax.psum_scatter(even, "dp", scatter_dimension=0, tiled=False)
+        half = n_mp // 2
+        pieces = weigh(n_dp, width, 0, half, *operands, None, list(came))
+        pieces = weigh(n_dp, width, half, n_mp - half, *operands, pieces, [grads])
+        ready = [pieces]
+        pieces = lax.psum_scatter(
+            tie(pieces, input_bank), "dp", scatter_dimension=0, tiled=False
+        )
+        odd, even = pieces[1::2], pieces[::2]
     else:
         parts, ready = [], []
         for s in steps:
@@ -1122,23 +1126,22 @@
         if len(hops) < n_mp - 1:
             came = tie(hop(hops[-1], len(hops) + 1, n_mp), part[0])
             hops.append(came)
-        elif h == n_mp - 2:
-            came = odd = tie(cross(odd, n_mp, 1), part[0])
+        else:
+            came = []
         parts.append(part)
         received.append(trade(tie(send, received[-1]) if h else send))
-    if came is not odd:
-        odd = cross(odd, n_mp, 1)
     result = finish_line(result_own, hops, place, n_mp)
     last = heads - 1
-    sums_in = weigh_input(hidden, parts)
+    sums_in = weigh_input(hidden, tie(parts, received[max(last - 1, 0)]))
     input_grad = input_gradient(
         place, n_mp, packed, 0, tie(first_back, sums_in), turned, input_bank, received[:last], f32
     )
+    odd = tie(cross(tie(odd, sums_in), n_mp, 1), input_grad)
     hidden_own = input_gradient(
         place, n_mp, packed, last, input_grad, turned, input_bank, received[last:], bf16
     )
     first_hop = hop((hidden_own, hidden_own), 1, n_mp)
-    even = tie(even, received[-1])
+    odd = tie(odd, hidden_own)
     input_sums = lax.psum(sums_in, "dp")
     tail = [first_hop]
     if n_mp > 2:

time: 545 us -> 541 us (level)
    psum x1, waiting for transfers between devices: 21.5 us -> 0.01 us  [local(): input_sums = lax.psum(sums_in, 'dp')]
    ppermute x6, waiting for transfers between devices: 54.7 us -> 75.6 us  [hop(): lax.ppermute(behind, 'mp', [(i, i - 1) for i in range(1, count - k + 1)])]
    reduce_scatter x2 -> x1, waiting for transfers between devices: 6.19 us -> 0.01 us  [local(): lax.psum_scatter(tie(pieces, input_bank), 'dp', scatter_dimension=0, tile...]
    ppermute x11, waiting for transfers between devices: 29.2 us -> 34.7 us  [cross(): return lax.ppermute(value, 'mp', [(i, i ^ bits) for i in range(count)])]
  transfers between devices with their start and end apart: 45 -> 44, of which waited for: 17 -> 13; matrix products, arithmetic and copies ran while one was open for 4% -> 4% of each run, Pallas kernels for 47% -> 47%
where the time goes in v3:
time: 541 us; the launch traced here: 531 us
  Pallas kernels  259 us (48%)
  waiting for transfers between devices  143 us (26%)
  starting transfers between devices  80.8 us (15%)
  other arithmetic  19.9 us (4%)
  between operations  14.9 us (3%)
  local copies, waits for them, and re-layouts  13.4 us (2%)
    pallas_call x4, Pallas kernels, attend_back(): pl.pallas_call(functools.partial(attend_back_kernel, chunk), grid_spec=pl...  75.8 us
    ppermute x6, waiting for transfers between devices, hop(): lax.ppermute(behind, 'mp', [(i, i - 1) for i in range(1, count - k + 1)])  75.6 us
    pallas_call x3, Pallas kernels, attend(): pl.pallas_call(functools.partial(attend_kernel, heads), grid_spec=pltpu.P...  49.6 us
    pallas_call x1, Pallas kernels, feed(): pl.pallas_call(functools.partial(feed_kernel, n_mp, packed, splits), grid...  34.8 us
    ppermute x11, waiting for transfers between devices, cross(): return lax.ppermute(value, 'mp', [(i, i ^ bits) for i in range(count)])  34.7 us
    all_to_all x5, starting transfers between devices, trade(): return lax.all_to_all(value, 'mp', 0, 0, tiled=True)  32 us
    pallas_call x1, Pallas kernels, feed_back(): pl.pallas_call(functools.partial(feed_back_kernel, n_mp, packed, splits),...  23.7 us
    pallas_call x2, Pallas kernels, weigh(): pl.pallas_call(functools.partial(weigh_kernel, shares), grid=(planes, n_d...  22 us
  transfers between devices with their start and end apart: 44, of which 13 were waited for; matrix products, arithmetic and copies ran while one was open for 4% of the time, Pallas kernels for 47%

profile of v3, /device:TPU:0, one launch (start us, length us, event | category | flops | bytes accessed | tf_op | source)
XLA Modules:
  0.0 531.1 jit_solution(11716471781083993036)
XLA Ops:
  7.8 2.6 pack.1
  10.4 3.1 collective-permute-start
  13.5 2.6 collective-permute-start.1
  16.1 11.6 %project.1 = (bf16[4,128,2048]{2,1,0:T(8,128)(2,1)}, bf16[4,64,2048]{2,1,0:T(8,128)(2,1)}, bf16[4,2048,128]{2,1,0:T(8,128)(2,1)}, bf16[4,80,2048]{2,1,0:T(8,128)...) custom-call(s32[1,8]{1,0:T(1,128)} %lengths_ref.1, ...), custom_call_target="tpu_custom_call" | custom-call | flops 3221225472 | bytes 33554432 | tf_op jit(solution)/shard_map/project/pallas_call | solution.py:150
  27.7 13.2 %attend.3 = (bf16[1,256,512]{2,1,0:T(8,128)(2,1)}, f32[1,4,1,512]{3,2,1,0:T(1,128)}) custom-call(s32[2]{0:T(128)} %pad_add_fusion.me_ref, bf16[4,128,2048]{2,1,0:T(8,128)(2,1)} %get-tuple-element.110.qt_ref, bf16[4,2048,128]{2,1,0:T(8,128)(2,1)} %get-tuple-element.111.kn_ref, bf16[4,80,2048]{2,1,0:T(8,128)(2,1)} %get-tuple-element.112.vt_ref), custom_call_target="tpu_custom_call" | custom-call | flops 5368709120 | bytes 8388608 | tf_op jit(solution)/shard_map/attend/pallas_call | solution.py:254
  40.9 1.9 collective-permute-done.1
  46.6 2.0 collective-permute-start.5
  48.7 13.2 %attend.4 = (bf16[1,256,512]{2,1,0:T(8,128)(2,1)}, f32[1,4,1,512]{3,2,1,0:T(1,128)}) custom-call(s32[2]{0:T(128)} %pad_add_fusion.me_ref, bf16[4,128,2048]{2,1,0:T(8,128)(2,1)} %get-tuple-element.110.qt_ref, bf16[4,2048,128]{2,1,0:T(8,128)(2,1)} %get-tuple-element.111.kn_ref, bf16[4,80,2048]{2,1,0:T(8,128)(2,1)} %get-tuple-element.112.vt_ref), custom_call_target="tpu_custom_call" | custom-call | flops 5368709120 | bytes 8388608 | tf_op jit(solution)/shard_map/attend/pallas_call | solution.py:254
  61.8 2.4 collective-permute-done.5.refs_0_.refs_3_
  70.8 23.3 %attend.5 = (bf16[2,256,512]{2,1,0:T(8,128)(2,1)}, f32[2,4,1,512]{3,2,1,0:T(1,128)}) custom-call(s32[2]{0:T(128)} %pad_add_fusion.me_ref, bf16[4,128,2048]{2,1,0:T(8,128)(2,1)} %get-tuple-element.110.qt_ref, bf16[4,2048,128]{2,1,0:T(8,128)(2,1)} %get-tuple-element.111.kn_ref, bf16[4,80,2048]{2,1,0:T(8,128)(2,1)} %get-tuple-element.112.vt_ref, ...), custom_call_target="tpu_custom_call" | custom-call | flops 10737418240 | bytes 8388608 | tf_op jit(solution)/shard_map/attend/pallas_call | solution.py:254
  94.0 4.7 collective-permute-done.9
  98.8 3.1 pad_maximum_fusion.refs_8_
  107.2 9.2 %collective-permute-done.14 = bf16[2,1,256,512]{3,2,1,0:T(8,128)(2,1)S(1)} collective-permute-done((bf16[2,1,256,512]{3,2,1,0:T(8,128)(2,1)S(1)}, bf16[2,1,256,512]{3,2,1,0:T(8,128)(2,1)S(1)}, u32[]{:S(2)}, u32[]{:S(2)}) %collective-permute-start.14) | collective-permute-done | bytes 524320 | tf_op jit(solution)/shard_map/ppermute | solution.py:930
  117.5 2.7 collective-permute-done.15
  126.8 4.0 collective-permute-start.25
  131.1 34.8 %feed.1 = (bf16[512,1024]{1,0:T(8,128)(2,1)}, bf16[512,1024]{1,0:T(8,128)(2,1)}, bf16[4,512,1024]{2,1,0:T(8,128)(2,1)}, bf16[4,512,1024]{2,1,0:T(8,128)(2,1)}, b...) custom-call(s32[2]{0:T(128)} %pad_add_fusion.me_ref, ...), custom_call_target="tpu_custom_call" | custom-call | flops 17179869184 | bytes 16777216 | tf_op jit(solution)/shard_map/feed/pallas_call | solution.py:645
  166.9 2.2 collective-permute-start.18
  170.4 23.7 %feed_back.1 = (bf16[4,512,1024]{2,1,0:T(8,128)(2,1)}, bf16[512,1024]{1,0:T(8,128)(2,1)}, f32[512,1024]{1,0:T(8,128)}, bf16[4,272,512]{2,1,0:T(8,128)(2,1)}, bf16[4,16,1024]{2,1,0:T(8,128)(2,1)}) custom-call(s32[2]{0:T(128)} %pad_add_fusion.me_ref, bf16[256,512]{1,0:T(8,128)(2,1)} %get-tuple-element.226.refs_0_, bf16[256,512]{1,0:T(8,128)(2,1)} %copy-done.23, ...), custom_call_target="tpu_custom_call" | custom-call | flops 17179869184 | bytes 16777216 | tf_op jit(solution)/shard_map/feed_back/pallas_call | solution.py:687
  194.2 7.0 %all-to-all-start = ((bf16[4,272,512]{2,1,0:T(8,128)(2,1)}), bf16[4,272,512]{2,1,0:T(8,128)(2,1)S(1)}, u32[]{:S(2)}, u32[]{:S(2)}) async-start(bf16[4,272,512]{2,1,0:T(8,128)(2,1)} %get-tuple-element.141), calls=%async_computation | async-start | bytes 2228224 | tf_op jit(solution)/shard_map/all_to_all | solution.py:926
  201.4 2.2 pad_maximum_fusion.6.ctx_ref
  205.0 11.0 %weigh.2.refs_0_ = bf16[8,4,304,1024]{3,2,1,0:T(8,128)(2,1)} custom-call(bf16[512,1024]{1,0:T(8,128)(2,1)} %get-tuple-element.147.first_ref, bf16[4,512,1024]{2,1,0:T(8,128)(2,1)} %get-tuple-element.148.act_ref, bf16[4,512,1024]{2,1,0:T(8,128)(2,1)} %get-tuple-element.149.ug_ref, bf16[512,1024]{1,0:T(8,128)(2,1)} %get-tuple-element.131.refs_16_.lg_ref, ...), custom_call_target="tpu_custom_call" | custom-call | flops 8589934592 | bytes 8388608 | tf_op jit(solution)/shard_map/weigh/pallas_call | solution.py:735
  216.0 11.1 %all-to-all-done.refs_1_.dot_ref.delta_ref = bf16[4,272,512]{2,1,0:T(8,128)(2,1)S(1)} async-done(((bf16[4,272,512]{2,1,0:T(8,128)(2,1)}), bf16[4,272,512]{2,1,0:T(8,128)(2,1)S(1)}, u32[]{:S(2)}, u32[]{:S(2)}) %all-to-all-start) | async-done | bytes 1114144 | tf_op jit(solution)/shard_map/all_to_all | solution.py:926
  228.1 11.0 %weigh.3.refs_0_ = bf16[8,4,304,1024]{3,2,1,0:T(8,128)(2,1)} custom-call(bf16[512,1024]{1,0:T(8,128)(2,1)} %get-tuple-element.147.first_ref, bf16[4,512,1024]{2,1,0:T(8,128)(2,1)} %get-tuple-element.148.act_ref, bf16[4,512,1024]{2,1,0:T(8,128)(2,1)} %get-tuple-element.149.ug_ref, ...), custom_call_target="tpu_custom_call", output_to_operand_aliasing={{}: (7, {})} | custom-call | flops 8589934592 | bytes 8388608 | tf_op jit(solution)/shard_map/weigh/pallas_call | solution.py:735
  243.4 18.8 %attend_back.4 = (bf16[64,2048]{1,0:T(8,128)(2,1)}, bf16[64,2048]{1,0:T(8,128)(2,1)}, bf16[64,2048]{1,0:T(8,128)(2,1)}, bf16[4,192,512]{2,1,0:T(8,128)(2,1)}) custom-call(s32[2]{0:T(128)} %pad_add_fusion.me_ref, bf16[4,128,2048]{2,1,0:T(8,128)(2,1)} %get-tuple-element.110.qt_ref, bf16[4,64,2048]{2,1,0:T(8,128)(2,1)} %get-tuple-element.139.kt_ref, ...), custom_call_target="tpu_custom_call" | custom-call | flops 21474836480 | bytes 2097152 | tf_op jit(solution)/shard_map/attend_back/pallas_call | solution.py:378
  262.3 6.4 %all-to-all-start.1 = ((bf16[4,192,512]{2,1,0:T(8,128)(2,1)}), bf16[4,192,512]{2,1,0:T(8,128)(2,1)S(1)}, u32[]{:S(2)}, u32[]{:S(2)}) async-start(bf16[4,192,512]{2,1,0:T(8,128)(2,1)} %get-tuple-element.162), calls=%async_computation.1 | async-start | bytes 1572864 | tf_op jit(solution)/shard_map/all_to_all | solution.py:926
  271.6 18.9 %attend_back.5 = (bf16[64,2048]{1,0:T(8,128)(2,1)}, bf16[64,2048]{1,0:T(8,128)(2,1)}, bf16[64,2048]{1,0:T(8,128)(2,1)}, bf16[4,192,512]{2,1,0:T(8,128)(2,1)}) custom-call(s32[2]{0:T(128)} %pad_add_fusion.me_ref, bf16[4,128,2048]{2,1,0:T(8,128)(2,1)} %get-tuple-element.110.qt_ref, bf16[4,64,2048]{2,1,0:T(8,128)(2,1)} %get-tuple-element.139.kt_ref, ...), custom_call_target="tpu_custom_call" | custom-call | flops 21474836480 | bytes 2097152 | tf_op jit(solution)/shard_map/attend_back/pallas_call | solution.py:378
  290.5 7.7 %all-to-all-start.2 = ((bf16[4,192,512]{2,1,0:T(8,128)(2,1)}), bf16[4,192,512]{2,1,0:T(8,128)(2,1)S(1)}, u32[]{:S(2)}, u32[]{:S(2)}) async-start(bf16[4,192,512]{2,1,0:T(8,128)(2,1)} %get-tuple-element.167), calls=%async_computation.2 | async-start | bytes 1572864 | tf_op jit(solution)/shard_map/all_to_all | solution.py:926
  298.2 14.4 %collective-permute-done.23.refs_5_.refs_1_ = bf16[512,1024]{1,0:T(8,128)(2,1)} collective-permute-done((bf16[512,1024]{1,0:T(8,128)(2,1)}, bf16[512,1024]{1,0:T(8,128)(2,1)}, u32[]{:S(2)}, u32[]{:S(2)}) %collective-permute-start.23) | collective-permute-done | bytes 1048608 | tf_op jit(solution)/shard_map/ppermute | solution.py:937
  312.7 18.9 %attend_back.6 = (bf16[64,2048]{1,0:T(8,128)(2,1)}, bf16[64,2048]{1,0:T(8,128)(2,1)}, bf16[64,2048]{1,0:T(8,128)(2,1)}, bf16[4,192,512]{2,1,0:T(8,128)(2,1)}) custom-call(s32[2]{0:T(128)} %pad_add_fusion.me_ref, bf16[4,128,2048]{2,1,0:T(8,128)(2,1)} %get-tuple-element.110.qt_ref, bf16[4,64,2048]{2,1,0:T(8,128)(2,1)} %get-tuple-element.139.kt_ref, ...), custom_call_target="tpu_custom_call" | custom-call | flops 21474836480 | bytes 2097152 | tf_op jit(solution)/shard_map/attend_back/pallas_call | solution.py:378
  331.5 5.8 %all-to-all-start.3 = ((bf16[4,192,512]{2,1,0:T(8,128)(2,1)}), bf16[4,192,512]{2,1,0:T(8,128)(2,1)S(1)}, u32[]{:S(2)}, u32[]{:S(2)}) async-start(bf16[4,192,512]{2,1,0:T(8,128)(2,1)} %get-tuple-element.172), calls=%async_computation.3 | async-start | bytes 1572864 | tf_op jit(solution)/shard_map/all_to_all | solution.py:926
  337.4 19.2 %attend_back.7 = (bf16[64,2048]{1,0:T(8,128)(2,1)}, bf16[64,2048]{1,0:T(8,128)(2,1)}, bf16[64,2048]{1,0:T(8,128)(2,1)}, bf16[4,192,512]{2,1,0:T(8,128)(2,1)}) custom-call(s32[2]{0:T(128)} %pad_add_fusion.me_ref, bf16[4,128,2048]{2,1,0:T(8,128)(2,1)} %get-tuple-element.110.qt_ref, bf16[4,64,2048]{2,1,0:T(8,128)(2,1)} %get-tuple-element.139.kt_ref, ...), custom_call_target="tpu_custom_call" | custom-call | flops 21474836480 | bytes 2097152 | tf_op jit(solution)/shard_map/attend_back/pallas_call | solution.py:378
  356.6 5.0 all-to-all-start.4
  361.9 8.0 %weigh_input.1 = bf16[3,1040,256]{2,1,0:T(8,128)(2,1)} custom-call(bf16[2048,1024]{1,0:T(8,128)(2,1)} %hidden_ref.5, bf16[64,2048]{1,0:T(8,128)(2,1)} %get-tuple-element.173.refs_0_, bf16[64,2048]{1,0:T(8,128)(2,1)} %get-tuple-element.174.refs_1_, bf16[64,2048]{1,0:T(8,128)(2,1)} %get-tuple-element.175.refs_2_, bf16[64,2048]{1,0:T(8,128)(2,1)} %get-tuple-element.176.refs_3_, ...), custom_call_target="tpu_custom_call" | custom-call | flops 3221225472 | bytes 16777216 | tf_op jit(solution)/shard_map/weigh_input/pallas_call | solution.py:875
  369.9 3.0 fusion.1
  373.0 2.0 collective-permute-start.33
  375.0 9.7 %input_gradient.2.back_ref = f32[512,1024]{1,0:T(8,128)} custom-call(s32[2]{0:T(128)} %pad_add_fusion.me_ref, f32[512,1024]{1,0:T(8,128)} %get-tuple-element.185.back_ref, bf16[768,1024]{1,0:T(8,128)(2,1)} %get-tuple-element.186.own_ref, bf16[8,3,96,1024]{3,2,1,0:T(8,128)(2,1)} %bitcast.56, bf16[4,192,512]{2,1,0:T(8,128)(2,1)} %copy-done.5, ...), custom_call_target="tpu_custom_call" | custom-call | flops 3221225472 | bytes 6291456 | tf_op jit(solution)/shard_map/input_gradient/pallas_call | solution.py:796
  385.6 6.0 %input_gradient.3.own_ref = bf16[512,1024]{1,0:T(8,128)(2,1)} custom-call(s32[2]{0:T(128)} %pad_add_fusion.me_ref, f32[512,1024]{1,0:T(8,128)} %input_gradient.2.back_ref, bf16[768,1024]{1,0:T(8,128)(2,1)} %get-tuple-element.186.own_ref, bf16[8,3,96,1024]{3,2,1,0:T(8,128)(2,1)} %bitcast.57, bf16[4,192,512]{2,1,0:T(8,128)(2,1)} %copy-done.16), custom_call_target="tpu_custom_call" | custom-call | flops 3221225472 | bytes 6291456 | tf_op jit(solution)/shard_map/input_gradient/pallas_call | solution.py:796
  391.6 9.8 %collective-permute-done.33 = bf16[2,304,1024]{2,1,0:T(8,128)(2,1)S(1)} collective-permute-done((bf16[2,304,1024]{2,1,0:T(8,128)(2,1)}, bf16[2,304,1024]{2,1,0:T(8,128)(2,1)S(1)}, u32[]{:S(2)}, u32[]{:S(2)}) %collective-permute-start.33) | collective-permute-done | bytes 1245216 | tf_op jit(solution)/shard_map/ppermute | solution.py:918
  402.7 2.1 collective-permute-start.34
  404.8 4.4 collective-permute-start.27
  410.5 20.6 %collective-permute-done.34 = bf16[1,304,1024]{2,1,0:T(8,128)(2,1)} collective-permute-done((bf16[1,304,1024]{2,1,0:T(8,128)(2,1)}, bf16[1,304,1024]{2,1,0:T(8,128)(2,1)}, u32[]{:S(2)}, u32[]{:S(2)}) %collective-permute-start.34) | collective-permute-done | bytes 622624 | tf_op jit(solution)/shard_map/ppermute | solution.py:918
  433.6 4.6 collective-permute-done.27.refs_0_
  438.2 7.9 %collective-permute-done.29.refs_3_ = bf16[512,1024]{1,0:T(8,128)(2,1)} collective-permute-done((bf16[512,1024]{1,0:T(8,128)(2,1)S(1)}, bf16[512,1024]{1,0:T(8,128)(2,1)}, u32[]{:S(2)}, u32[]{:S(2)}) %collective-permute-start.29) | collective-permute-done | bytes 1048608 | tf_op jit(solution)/shard_map/ppermute | solution.py:937
  449.1 34.7 %collective-permute-done.30.refs_4_ = bf16[512,1024]{1,0:T(8,128)(2,1)} collective-permute-done((bf16[512,1024]{1,0:T(8,128)(2,1)}, bf16[512,1024]{1,0:T(8,128)(2,1)}, u32[]{:S(2)}, u32[]{:S(2)}) %collective-permute-start.30) | collective-permute-done | bytes 1048608 | tf_op jit(solution)/shard_map/ppermute | solution.py:937
  486.8 4.0 join_line.2
  493.4 18.6 %collective-permute-done.32.refs_5_ = bf16[512,1024]{1,0:T(8,128)(2,1)} collective-permute-done((bf16[512,1024]{1,0:T(8,128)(2,1)}, bf16[512,1024]{1,0:T(8,128)(2,1)}, u32[]{:S(2)}, u32[]{:S(2)}) %collective-permute-start.32) | collective-permute-done | bytes 1048608 | tf_op jit(solution)/shard_map/ppermute | solution.py:937
  512.0 4.0 join_line.3
  516.5 7.5 %unpack.1 = (f32[256,1024]{1,0:T(8,128)}, f32[1024,1024]{1,0:T(8,128)}, f32[1024,1024]{1,0:T(8,128)}) custom-call(bf16[8,288,1024]{2,1,0:T(8,128)(2,1)} %bitcast.58), custom_call_target="tpu_custom_call" | custom-call | tf_op jit(solution)/shard_map/unpack/pallas_call | solution.py:898
  (166 shorter events, 51.5 us)
Async XLA Ops:
  7.2 231.9 %all-gather.5.cloned.1.call-start = ((), (), s32[]{:S(2)}) async-start(), calls=%async_computation.8 | async-start | bytes 5308416 | tf_op jit(solution)/shard_map/all_gather | solution.py:986
  10.4 30.4 %collective-permute-start = (bf16[592,512]{1,0:T(8,128)(2,1)}, bf16[592,512]{1,0:T(8,128)(2,1)S(1)}, u32[]{:S(2)}, u32[]{:S(2)}) collective-permute-start(bf16[592,512]{1,0:T(8,128)(2,1)} %pack.1), channel_id=1, source_target_pairs={{0,1},{1,0},{2,3},{3,2},{4,5},{5,4},{6,7},{7,6},{8,9},{9,8},{10,11... | collective-permute-start | bytes 1818632 | tf_op jit(solution)/shard_map/ppermute | solution.py:918
  13.5 29.3 %collective-permute-start.1 = (bf16[592,512]{1,0:T(8,128)(2,1)}, bf16[592,512]{1,0:T(8,128)(2,1)S(1)}, u32[]{:S(2)}, u32[]{:S(2)}) collective-permute-start(bf16[592,512]{1,0:T(8,128)(2,1)} %pack.1), channel_id=1, source_target_pairs={{0,2},{1,3},{2,0},{3,1},{4,6},{5,7},{6,4},{7,5},{8,10},{9,11},{10,... | collective-permute-start | bytes 1818632 | tf_op jit(solution)/shard_map/ppermute | solution.py:918
  43.0 21.2 %collective-permute-start.3 = (bf16[1,2,320,512]{3,2,1,0:T(8,128)(2,1)S(1)}, bf16[1,2,320,512]{3,2,1,0:T(8,128)(2,1)S(1)}, u32[]{:S(2)}, u32[]{:S(2)}) collective-permute-start(bf16[1,2,320,512]{3,2,1,0:T(8,128)(2,1)S(1)} %slice.195), channel_id=1, source_target_pairs={{0,16},{4,20},{8,24},{12,28},{16,0},{20,4},{24,8},{28,12},{1,17},{... | collective-permute-start | bytes 1966088 | tf_op jit(solution)/shard_map/ppermute | solution.py:930
  44.6 19.6 %collective-permute-start.4 = (bf16[592,512]{1,0:T(8,128)(2,1)S(1)}, bf16[592,512]{1,0:T(8,128)(2,1)S(1)}, u32[]{:S(2)}, u32[]{:S(2)}) collective-permute-start(bf16[592,512]{1,0:T(8,128)(2,1)S(1)} %collective-permute-done.1), channel_id=1, source_target_pairs={{0,1},{1,0},{2,3},{3,2},{4,5},{5,4},{6,7},{7,6},{8,9},{9,8},{10,11... | collective-permute-start | bytes 1818632 | tf_op jit(solution)/shard_map/ppermute | solution.py:918
  45.1 19.1 %collective-permute-start.2 = (bf16[1,2,256,512]{3,2,1,0:T(8,128)(2,1)S(1)}, bf16[1,2,256,512]{3,2,1,0:T(8,128)(2,1)S(1)}, u32[]{:S(2)}, u32[]{:S(2)}) collective-permute-start(bf16[1,2,256,512]{3,2,1,0:T(8,128)(2,1)S(1)} %slice.194), channel_id=1, source_target_pairs={{0,8},{4,12},{8,0},{12,4},{16,24},{20,28},{24,16},{28,20},{1,9},{5... | collective-permute-start | bytes 1572872 | tf_op jit(solution)/shard_map/ppermute | solution.py:930
  46.6 17.6 %collective-permute-start.5 = (bf16[256,512]{1,0:T(8,128)(2,1)}, bf16[256,512]{1,0:T(8,128)(2,1)S(1)}, u32[]{:S(2)}, u32[]{:S(2)}) collective-permute-start(bf16[256,512]{1,0:T(8,128)(2,1)} %bitcast.9), channel_id=1, source_target_pairs={{0,3},{1,2},{2,1},{3,0},{4,7},{5,6},{6,5},{7,4},{8,11},{9,10},{10,... | collective-permute-start | bytes 786440 | tf_op jit(solution)/shard_map/ppermute | solution.py:918
  65.5 33.3 %collective-permute-start.8 = (bf16[2,2,320,512]{3,2,1,0:T(8,128)(2,1)}, bf16[2,2,320,512]{3,2,1,0:T(8,128)(2,1)}, u32[]{:S(2)}, u32[]{:S(2)}) collective-permute-start(bf16[2,2,320,512]{3,2,1,0:T(8,128)(2,1)} %pad_maximum_fusion.2.refs_2_), channel_id=1, source_target_pairs={{0,8},{4,12},{8,0},{12,4},{16,24},{20,28},{24,16},{28,20},{1,9},{5... | collective-permute-start | bytes 3932168 | tf_op jit(solution)/shard_map/ppermute | solution.py:930
  68.1 30.7 %collective-permute-start.7 = (bf16[2,2,256,512]{3,2,1,0:T(8,128)(2,1)}, bf16[2,2,256,512]{3,2,1,0:T(8,128)(2,1)}, u32[]{:S(2)}, u32[]{:S(2)}) collective-permute-start(bf16[2,2,256,512]{3,2,1,0:T(8,128)(2,1)} %pad_maximum_fusion.4.refs_1_), channel_id=1, source_target_pairs={{0,16},{4,20},{8,24},{12,28},{16,0},{20,4},{24,8},{28,12},{1,17},{... | collective-permute-start | bytes 3145736 | tf_op jit(solution)/shard_map/ppermute | solution.py:930
  68.9 25.1 %collective-permute-start.11 = (bf16[256,512]{1,0:T(8,128)(2,1)}, bf16[256,512]{1,0:T(8,128)(2,1)S(1)}, u32[]{:S(2)}, u32[]{:S(2)}) collective-permute-start(bf16[256,512]{1,0:T(8,128)(2,1)} %bitcast.13), channel_id=1, source_target_pairs={{0,2},{1,3},{2,0},{3,1},{4,6},{5,7},{6,4},{7,5},{8,10},{9,11},{10,... | collective-permute-start | bytes 786440 | tf_op jit(solution)/shard_map/ppermute | solution.py:918
  69.0 29.7 %collective-permute-start.9 = (bf16[1,1,256,512]{3,2,1,0:T(8,128)(2,1)S(1)}, bf16[1,1,256,512]{3,2,1,0:T(8,128)(2,1)S(1)}, u32[]{:S(2)}, u32[]{:S(2)}) collective-permute-start(bf16[1,1,256,512]{3,2,1,0:T(8,128)(2,1)S(1)} %slice.196.refs_3_), channel_id=1, source_target_pairs={{0,8},{4,12},{8,0},{12,4},{16,24},{20,28},{24,16},{28,20},{1,9},{5... | collective-permute-start | bytes 786440 | tf_op jit(solution)/shard_map/ppermute | solution.py:930
  69.6 29.1 %collective-permute-start.10 = (bf16[1,1,320,512]{3,2,1,0:T(8,128)(2,1)S(1)}, bf16[1,1,320,512]{3,2,1,0:T(8,128)(2,1)S(1)}, u32[]{:S(2)}, u32[]{:S(2)}) collective-permute-start(bf16[1,1,320,512]{3,2,1,0:T(8,128)(2,1)S(1)} %slice.197.refs_4_), channel_id=1, source_target_pairs={{0,16},{4,20},{8,24},{12,28},{16,0},{20,4},{24,8},{28,12},{1,17},{... | collective-permute-start | bytes 983048 | tf_op jit(solution)/shard_map/ppermute | solution.py:930
  101.9 29.2 %collective-permute-start.13 = (bf16[4,2,320,512]{3,2,1,0:T(8,128)(2,1)}, bf16[4,2,320,512]{3,2,1,0:T(8,128)(2,1)}, u32[]{:S(2)}, u32[]{:S(2)}) collective-permute-start(bf16[4,2,320,512]{3,2,1,0:T(8,128)(2,1)} %pad_maximum_fusion.refs_8_), channel_id=1, source_target_pairs={{0,4},{4,0},{8,12},{12,8},{16,20},{20,16},{24,28},{28,24},{1,5},{5... | collective-permute-start | bytes 7864328 | tf_op jit(solution)/shard_map/ppermute | solution.py:930
  102.0 14.4 %collective-permute-start.14 = (bf16[2,1,256,512]{3,2,1,0:T(8,128)(2,1)S(1)}, bf16[2,1,256,512]{3,2,1,0:T(8,128)(2,1)S(1)}, u32[]{:S(2)}, u32[]{:S(2)}) collective-permute-start(bf16[2,1,256,512]{3,2,1,0:T(8,128)(2,1)S(1)} %pad_maximum_fusion.9), channel_id=1, source_target_pairs={{0,16},{4,20},{8,24},{12,28},{16,0},{20,4},{24,8},{28,12},{1,17},{... | collective-permute-start | bytes 1572872 | tf_op jit(solution)/shard_map/ppermute | solution.py:930
  103.2 16.9 %collective-permute-start.15 = (bf16[2,1,320,512]{3,2,1,0:T(8,128)(2,1)S(1)}, bf16[2,1,320,512]{3,2,1,0:T(8,128)(2,1)S(1)}, u32[]{:S(2)}, u32[]{:S(2)}) collective-permute-start(bf16[2,1,320,512]{3,2,1,0:T(8,128)(2,1)S(1)} %pad_maximum_fusion.7), channel_id=1, source_target_pairs={{0,8},{4,12},{8,0},{12,4},{16,24},{20,28},{24,16},{28,20},{1,9},{5... | collective-permute-start | bytes 1966088 | tf_op jit(solution)/shard_map/ppermute | solution.py:930
  106.2 11.2 %copy-start.12 = (bf16[4,2,256,512]{3,2,1,0:T(8,128)(2,1)}, bf16[4,2,256,512]{3,2,1,0:T(8,128)(2,1)S(1)}, u32[]{:S(2)}) copy-start(bf16[4,2,256,512]{3,2,1,0:T(8,128)(2,1)S(1)} %pad_maximum_fusion.1.refs_7_) | copy-start | bytes 6291460
  106.2 24.9 %collective-permute-start.12 = (bf16[4,2,256,512]{3,2,1,0:T(8,128)(2,1)S(1)}, bf16[4,2,256,512]{3,2,1,0:T(8,128)(2,1)}, u32[]{:S(2)}, u32[]{:S(2)}) collective-permute-start(bf16[4,2,256,512]{3,2,1,0:T(8,128)(2,1)S(1)} %pad_maximum_fusion.1.refs_7_), channel_id=1, source_target_pairs={{0,4},{4,0},{8,12},{12,8},{16,20},{20,16},{24,28},{28,24},{1,5},{5... | collective-permute-start | bytes 6291464 | tf_op jit(solution)/shard_map/ppermute | solution.py:930
  107.2 14.3 %collective-permute-start.6 = (bf16[256,512]{1,0:T(8,128)(2,1)S(1)}, bf16[256,512]{1,0:T(8,128)(2,1)S(1)}, u32[]{:S(2)}, u32[]{:S(2)}) collective-permute-start(bf16[256,512]{1,0:T(8,128)(2,1)S(1)} %get-tuple-element.227), channel_id=1, source_target_pairs={{0,1},{1,0},{2,3},{3,2},{4,5},{5,4},{6,7},{7,6},{8,9},{9,8},{10,11... | collective-permute-start | bytes 786440 | tf_op jit(solution)/shard_map/ppermute | solution.py:918
  121.5 9.3 %collective-permute-start.17 = (bf16[4,1,320,512]{3,2,1,0:T(8,128)(2,1)}, bf16[4,1,320,512]{3,2,1,0:T(8,128)(2,1)}, u32[]{:S(2)}, u32[]{:S(2)}) collective-permute-start(bf16[4,1,320,512]{3,2,1,0:T(8,128)(2,1)} %pad_maximum_fusion.3.refs_12_), channel_id=1, source_target_pairs={{0,4},{4,0},{8,12},{12,8},{16,20},{20,16},{24,28},{28,24},{1,5},{5... | collective-permute-start | bytes 3932168 | tf_op jit(solution)/shard_map/ppermute | solution.py:930
  121.5 5.3 %collective-permute-start.16 = (bf16[4,1,256,512]{3,2,1,0:T(8,128)(2,1)}, bf16[4,1,256,512]{3,2,1,0:T(8,128)(2,1)}, u32[]{:S(2)}, u32[]{:S(2)}) collective-permute-start(bf16[4,1,256,512]{3,2,1,0:T(8,128)(2,1)} %pad_maximum_fusion.5.refs_11_), channel_id=1, source_target_pairs={{0,4},{4,0},{8,12},{12,8},{16,20},{20,16},{24,28},{28,24},{1,5},{5... | collective-permute-start | bytes 3145736 | tf_op jit(solution)/shard_map/ppermute | solution.py:930
  122.9 43.1 %collective-permute-start.24 = (bf16[96,1024]{1,0:T(8,128)(2,1)S(1)}, bf16[96,1024]{1,0:T(8,128)(2,1)S(1)}, u32[]{:S(2)}, u32[]{:S(2)}) collective-permute-start(bf16[96,1024]{1,0:T(8,128)(2,1)S(1)} %constant_dynamic-slice_fusion), channel_id=1, source_target_pairs={{0,1},{1,0},{2,3},{3,2},{4,5},{5,4},{6,7},{7,6},{8,9},{9,8},{10,11... | collective-permute-start | bytes 589832 | tf_op jit(solution)/shard_map/ppermute | solution.py:918
  126.8 39.2 %collective-permute-start.25 = (bf16[96,1024]{1,0:T(8,128)(2,1)S(1)}, bf16[96,1024]{1,0:T(8,128)(2,1)S(1)}, u32[]{:S(2)}, u32[]{:S(2)}) collective-permute-start(bf16[96,1024]{1,0:T(8,128)(2,1)S(1)} %constant_dynamic-slice_fusion), channel_id=1, source_target_pairs={{0,2},{1,3},{2,0},{3,1},{4,6},{5,7},{6,4},{7,5},{8,10},{9,11},{10,... | collective-permute-start | bytes 589832 | tf_op jit(solution)/shard_map/ppermute | solution.py:918
  130.8 35.2 %collective-permute-start.26 = (bf16[96,1024]{1,0:T(8,128)(2,1)S(1)}, bf16[96,1024]{1,0:T(8,128)(2,1)S(1)}, u32[]{:S(2)}, u32[]{:S(2)}) collective-permute-start(bf16[96,1024]{1,0:T(8,128)(2,1)S(1)} %constant_dynamic-slice_fusion), channel_id=1, source_target_pairs={{0,3},{1,2},{2,1},{3,0},{4,7},{5,6},{6,5},{7,4},{8,11},{9,10},{10,... | collective-permute-start | bytes 589832 | tf_op jit(solution)/shard_map/ppermute | solution.py:918
  166.9 36.7 %collective-permute-start.18 = (bf16[512,1024]{1,0:T(8,128)(2,1)}, bf16[512,1024]{1,0:T(8,128)(2,1)S(1)}, u32[]{:S(2)}, u32[]{:S(2)}) collective-permute-start(bf16[512,1024]{1,0:T(8,128)(2,1)} %get-tuple-element.129.own_ref), channel_id=1, source_target_pairs={{0,1},{1,2},{2,3},{4,5},{5,6},{6,7},{8,9},{9,10},{10,11},{12,13},{... | collective-permute-start | bytes 3145736 | tf_op jit(solution)/shard_map/ppermute | solution.py:936
  169.1 34.5 %collective-permute-start.19 = (bf16[512,1024]{1,0:T(8,128)(2,1)}, bf16[512,1024]{1,0:T(8,128)(2,1)S(1)}, u32[]{:S(2)}, u32[]{:S(2)}) collective-permute-start(bf16[512,1024]{1,0:T(8,128)(2,1)} %get-tuple-element.129.own_ref), channel_id=1, source_target_pairs={{1,0},{2,1},{3,2},{5,4},{6,5},{7,6},{9,8},{10,9},{11,10},{13,12},{... | collective-permute-start | bytes 3145736 | tf_op jit(solution)/shard_map/ppermute | solution.py:937
  194.2 32.9 %all-to-all-start = ((bf16[4,272,512]{2,1,0:T(8,128)(2,1)}), bf16[4,272,512]{2,1,0:T(8,128)(2,1)S(1)}, u32[]{:S(2)}, u32[]{:S(2)}) async-start(bf16[4,272,512]{2,1,0:T(8,128)(2,1)} %get-tuple-element.141), calls=%async_computation | async-start | bytes 2228224 | tf_op jit(solution)/shard_map/all_to_all | solution.py:926
  201.2 168.7 %reduce-scatter.2.cloned.1.call-start = ((), (), s32[]{:S(2)}) async-start(), calls=%async_computation.7 | async-start | bytes 22413312 | tf_op jit(solution)/shard_map/reduce_scatter | solution.py:1106
  240.5 28.2 %collective-permute-start.20 = (bf16[512,1024]{1,0:T(8,128)(2,1)S(1)}, bf16[512,1024]{1,0:T(8,128)(2,1)}, u32[]{:S(2)}, u32[]{:S(2)}) collective-permute-start(bf16[512,1024]{1,0:T(8,128)(2,1)S(1)} %copy-done.2), channel_id=1, source_target_pairs={{1,2},{2,3},{5,6},{6,7},{9,10},{10,11},{13,14},{14,15},{17,18},{18... | collective-permute-start | bytes 3145736 | tf_op jit(solution)/shard_map/ppermute | solution.py:936
  242.1 26.5 %collective-permute-start.21 = (bf16[512,1024]{1,0:T(8,128)(2,1)S(1)}, bf16[512,1024]{1,0:T(8,128)(2,1)}, u32[]{:S(2)}, u32[]{:S(2)}) collective-permute-start(bf16[512,1024]{1,0:T(8,128)(2,1)S(1)} %copy-done.4), channel_id=1, source_target_pairs={{1,0},{2,1},{5,4},{6,5},{9,8},{10,9},{13,12},{14,13},{17,16},{18,1... | collective-permute-start | bytes 3145736 | tf_op jit(solution)/shard_map/ppermute | solution.py:937
  262.3 28.2 %all-to-all-start.1 = ((bf16[4,192,512]{2,1,0:T(8,128)(2,1)}), bf16[4,192,512]{2,1,0:T(8,128)(2,1)S(1)}, u32[]{:S(2)}, u32[]{:S(2)}) async-start(bf16[4,192,512]{2,1,0:T(8,128)(2,1)} %get-tuple-element.162), calls=%async_computation.1 | async-start | bytes 1572864 | tf_op jit(solution)/shard_map/all_to_all | solution.py:926
  268.7 29.6 %collective-permute-start.22 = (bf16[512,1024]{1,0:T(8,128)(2,1)}, bf16[512,1024]{1,0:T(8,128)(2,1)}, u32[]{:S(2)}, u32[]{:S(2)}) collective-permute-start(bf16[512,1024]{1,0:T(8,128)(2,1)} %collective-permute-done.20.refs_0_.refs_1_), channel_id=1, source_target_pairs={{2,3},{6,7},{10,11},{14,15},{18,19},{22,23},{26,27},{30,31}} | collective-permute-start | bytes 3145736 | tf_op jit(solution)/shard_map/ppermute | solution.py:936
  270.3 42.3 %collective-permute-start.23 = (bf16[512,1024]{1,0:T(8,128)(2,1)}, bf16[512,1024]{1,0:T(8,128)(2,1)}, u32[]{:S(2)}, u32[]{:S(2)}) collective-permute-start(bf16[512,1024]{1,0:T(8,128)(2,1)} %collective-permute-done.21.refs_1_.refs_4_), channel_id=1, source_target_pairs={{1,0},{5,4},{9,8},{13,12},{17,16},{21,20},{25,24},{29,28}} | collective-permute-start | bytes 3145736 | tf_op jit(solution)/shard_map/ppermute | solution.py:937
  290.5 22.2 %copy-start.5 = (bf16[4,192,512]{2,1,0:T(8,128)(2,1)}, bf16[4,192,512]{2,1,0:T(8,128)(2,1)S(1)}, u32[]{:S(2)}) copy-start(bf16[4,192,512]{2,1,0:T(8,128)(2,1)S(1)} %all-to-all-done.1.refs_2_.refs_0_) | copy-start | bytes 2359300
  290.5 41.0 %all-to-all-start.2 = ((bf16[4,192,512]{2,1,0:T(8,128)(2,1)}), bf16[4,192,512]{2,1,0:T(8,128)(2,1)S(1)}, u32[]{:S(2)}, u32[]{:S(2)}) async-start(bf16[4,192,512]{2,1,0:T(8,128)(2,1)} %get-tuple-element.167), calls=%async_computation.2 | async-start | bytes 1572864 | tf_op jit(solution)/shard_map/all_to_all | solution.py:926
  331.5 25.1 %all-to-all-start.3 = ((bf16[4,192,512]{2,1,0:T(8,128)(2,1)}), bf16[4,192,512]{2,1,0:T(8,128)(2,1)S(1)}, u32[]{:S(2)}, u32[]{:S(2)}) async-start(bf16[4,192,512]{2,1,0:T(8,128)(2,1)} %get-tuple-element.172), calls=%async_computation.3 | async-start | bytes 1572864 | tf_op jit(solution)/shard_map/all_to_all | solution.py:926
  356.6 13.3 %copy-start.7 = (bf16[4,192,512]{2,1,0:T(8,128)(2,1)}, bf16[4,192,512]{2,1,0:T(8,128)(2,1)S(1)}, u32[]{:S(2)}) copy-start(bf16[4,192,512]{2,1,0:T(8,128)(2,1)S(1)} %all-to-all-done.3.refs_2_) | copy-start | bytes 2359300
  356.6 28.1 %all-to-all-start.4 = ((bf16[4,192,512]{2,1,0:T(8,128)(2,1)}), bf16[4,192,512]{2,1,0:T(8,128)(2,1)S(1)}, u32[]{:S(2)}, u32[]{:S(2)}) async-start(bf16[4,192,512]{2,1,0:T(8,128)(2,1)} %get-tuple-element.191), calls=%async_computation.4 | async-start | bytes 1572864 | tf_op jit(solution)/shard_map/all_to_all | solution.py:926
  361.6 122.1 %all-reduce.2.cloned.1.call-start = ((), (), s32[]{:S(2)}) async-start(), calls=%async_computation.6 | async-start | bytes 3194880 | tf_op jit(solution)/shard_map/psum | solution.py:1145
  373.0 28.4 %collective-permute-start.33 = (bf16[2,304,1024]{2,1,0:T(8,128)(2,1)}, bf16[2,304,1024]{2,1,0:T(8,128)(2,1)S(1)}, u32[]{:S(2)}, u32[]{:S(2)}) collective-permute-start(bf16[2,304,1024]{2,1,0:T(8,128)(2,1)} %get-tuple-element.195), channel_id=1, source_target_pairs={{0,1},{1,0},{2,3},{3,2},{4,5},{5,4},{6,7},{7,6},{8,9},{9,8},{10,11... | collective-permute-start | bytes 3735560 | tf_op jit(solution)/shard_map/ppermute | solution.py:918
  391.6 13.1 %copy-start.15 = (bf16[512,1024]{1,0:T(8,128)(2,1)S(1)}, bf16[512,1024]{1,0:T(8,128)(2,1)}, u32[]{:S(2)}) copy-start(bf16[512,1024]{1,0:T(8,128)(2,1)} %input_gradient.3.own_ref) | copy-start | bytes 3145732
  402.7 28.5 %collective-permute-start.34 = (bf16[1,304,1024]{2,1,0:T(8,128)(2,1)}, bf16[1,304,1024]{2,1,0:T(8,128)(2,1)}, u32[]{:S(2)}, u32[]{:S(2)}) collective-permute-start(bf16[1,304,1024]{2,1,0:T(8,128)(2,1)} %add_convert_fusion), channel_id=1, source_target_pairs={{0,2},{1,3},{2,0},{3,1},{4,6},{5,7},{6,4},{7,5},{8,10},{9,11},{10,... | collective-permute-start | bytes 1867784 | tf_op jit(solution)/shard_map/ppermute | solution.py:918
  404.8 33.4 %collective-permute-start.27 = (bf16[512,1024]{1,0:T(8,128)(2,1)S(1)}, bf16[512,1024]{1,0:T(8,128)(2,1)}, u32[]{:S(2)}, u32[]{:S(2)}) collective-permute-start(bf16[512,1024]{1,0:T(8,128)(2,1)S(1)} %copy-done.15), channel_id=1, source_target_pairs={{0,1},{1,2},{2,3},{4,5},{5,6},{6,7},{8,9},{9,10},{10,11},{12,13},{... | collective-permute-start | bytes 3145736 | tf_op jit(solution)/shard_map/ppermute | solution.py:936
  409.1 37.0 %collective-permute-start.29 = (bf16[512,1024]{1,0:T(8,128)(2,1)S(1)}, bf16[512,1024]{1,0:T(8,128)(2,1)}, u32[]{:S(2)}, u32[]{:S(2)}) collective-permute-start(bf16[512,1024]{1,0:T(8,128)(2,1)S(1)} %copy-done.15), channel_id=1, source_target_pairs={{1,0},{2,1},{3,2},{5,4},{6,5},{7,6},{9,8},{10,9},{11,10},{13,12},{... | collective-permute-start | bytes 3145736 | tf_op jit(solution)/shard_map/ppermute | solution.py:937
  410.4 106.1 %all-gather.7.cloned.1.call-start = ((), (), s32[]{:S(2)}) async-start(), calls=%async_computation.9 | async-start | bytes 5308416 | tf_op jit(solution)/shard_map/all_gather | solution.py:986
  446.1 2.9 collective-permute-start.28
  447.8 36.0 %collective-permute-start.30 = (bf16[512,1024]{1,0:T(8,128)(2,1)}, bf16[512,1024]{1,0:T(8,128)(2,1)}, u32[]{:S(2)}, u32[]{:S(2)}) collective-permute-start(bf16[512,1024]{1,0:T(8,128)(2,1)} %collective-permute-done.29.refs_3_), channel_id=1, source_target_pairs={{1,0},{2,1},{5,4},{6,5},{9,8},{10,9},{13,12},{14,13},{17,16},{18,1... | collective-permute-start | bytes 3145736 | tf_op jit(solution)/shard_map/ppermute | solution.py:937
  483.7 9.6 %collective-permute-start.31 = (bf16[512,1024]{1,0:T(8,128)(2,1)}, bf16[512,1024]{1,0:T(8,128)(2,1)}, u32[]{:S(2)}, u32[]{:S(2)}) collective-permute-start(bf16[512,1024]{1,0:T(8,128)(2,1)} %collective-permute-done.28.refs_1_), channel_id=1, source_target_pairs={{2,3},{6,7},{10,11},{14,15},{18,19},{22,23},{26,27},{30,31}} | collective-permute-start | bytes 3145736 | tf_op jit(solution)/shard_map/ppermute | solution.py:936
  485.5 26.4 %collective-permute-start.32 = (bf16[512,1024]{1,0:T(8,128)(2,1)}, bf16[512,1024]{1,0:T(8,128)(2,1)}, u32[]{:S(2)}, u32[]{:S(2)}) collective-permute-start(bf16[512,1024]{1,0:T(8,128)(2,1)} %collective-permute-done.30.refs_4_), channel_id=1, source_target_pairs={{1,0},{5,4},{9,8},{13,12},{17,16},{21,20},{25,24},{29,28}} | collective-permute-start | bytes 3145736 | tf_op jit(solution)/shard_map/ppermute | solution.py:937
  (29 other events, 110.1 us)
Sparse Core Ops, SparseCore 0:
  167.0 39.3 all-gather.4
  239.3 129.4 reduce-scatter.1
  410.5 58.4 all-reduce.1
  471.5 38.3 all-gather.6
